TPU v7x, 256 devices: a whole 4x4x8 slice. The times are simulated.
256 devices in a mesh: group: 4 (over y), psg: 64 (over x, z, core).
Axes of the slice: x: 4, y: 4, z: 8, core: 2. Of those that a mesh axis runs over, the one named last changes fastest.
Arguments:
- queries: bfloat16 [4096, 2048], P(('group', 'psg')), parts along dimension 0, as said below
- keys: bfloat16 [256, 512, 2048], P(('group', 'psg')), parts along dimension 0
- values: bfloat16 [256, 512, 2048], P(('group', 'psg')), parts along dimension 0, may hold values from -6 to 6
- grad_out: bfloat16 [4096, 2048], P(('group', 'psg')), parts along dimension 0, may hold values from -6 to 6
- lengths: int32 [256], P(('group', 'psg')), parts along dimension 0, may hold values from 1 to 8, 256 in all
- slot_query: int32 [256], P(('group', 'psg')), parts along dimension 0, may hold values from 0 to 1, as said below
Outputs:
- grad_queries: bfloat16 [4096, 2048], P(('group', 'psg')), parts along dimension 0
- grad_keys: bfloat16 [256, 512, 2048], P(('group', 'psg')), parts along dimension 0
- grad_values: bfloat16 [256, 512, 2048], P(('group', 'psg')), parts along dimension 0
There are 4 independent parts, one for each index of `group`. A program takes and returns all parts, laid end to end along the dimension named above; each array names one. Nothing has to cross between parts.
Inputs may be any that keep to these rules, and one draw needn't show every extreme that they name: `slot_query`: every query 0 to 1 owns exactly 32 passages. `queries`: some query rows may align with keys, so that scores can reach a few hundred.
All inputs are finite; a program needn't handle non-finite values. No bound on the sum of `lengths` on one device may be relied on, other than what follows from the above.
Results may differ from a plain program's by a relative error of at most 0.0051.
Values may be sent and summed in bfloat16 or wider, within the bound.
No kernel may reach another device: no remote copies, remote signals or barrier semaphores. Data moves between devices by JAX's collectives and lax.ppermute only.
A program may use at most 256 MiB of HBM per device.

v0:
```python
import jax
import jax.numpy as jnp
from jax import lax
from jax.sharding import PartitionSpec as P

HEADS = 32
HDIM = 64
BKT = 64
QRY = 2


def per_device(queries, keys, values, grad_out, lengths, slot_query):
    whole_q, whole_g = (
        lax.all_gather(queries, "psg", axis=0, tiled=True),
        lax.all_gather(grad_out, "psg", axis=0, tiled=True),
    )
    owner_query = slot_query[0]
    dec_rows = whole_q.shape[0] // QRY
    width = HEADS * HDIM
    q_heads = lax.dynamic_slice_in_dim(whole_q, owner_query * dec_rows, dec_rows, 0).reshape(
        dec_rows, HEADS, HDIM
    )
    g_heads = lax.dynamic_slice_in_dim(whole_g, owner_query * dec_rows, dec_rows, 0).reshape(
        dec_rows, HEADS, HDIM
    )
    slot_count = keys.shape[1]
    k_heads = keys[0].reshape(slot_count, HEADS, HDIM)
    v_heads = values[0].reshape(slot_count, HEADS, HDIM)
    is_valid = jnp.arange(slot_count) < lengths[0] * BKT
    scores = jnp.einsum("rhd,khd->hrk", q_heads, k_heads, preferred_element_type=jnp.float32)
    scores = jnp.where(is_valid[None, None, :], scores, -jnp.inf)
    upstream = jnp.einsum("rhd,khd->hrk", g_heads, v_heads, preferred_element_type=jnp.float32)
    local_max = jnp.max(scores, axis=-1)
    weights = jnp.exp(scores - local_max[..., None])
    local_sum = jnp.sum(weights, axis=-1)
    local_dot = jnp.sum(weights * upstream, axis=-1)
    is_owner = (jnp.arange(QRY) == owner_query)[:, None, None]

    def place_rows(stat, filler):
        return jnp.where(is_owner, stat[None], jnp.float32(filler))

    row_top = lax.pmax(place_rows(local_max, -1e30).astype(jnp.bfloat16), "psg").astype(jnp.float32)
    top_own = row_top[owner_query]
    factor = jnp.exp(local_max - top_own)
    row_total, dotted = lax.psum(
        (place_rows(local_sum * factor, 0.0), place_rows(local_dot * factor, 0.0)), "psg"
    )
    total_own = row_total[owner_query]
    row_delta = dotted[owner_query] / total_own
    attn_probs = jnp.exp(scores - top_own[..., None]) / total_own[..., None]
    probs_low = attn_probs.astype(jnp.bfloat16)
    dscore = (attn_probs * (upstream - row_delta[..., None])).astype(jnp.bfloat16)
    grad_val = jnp.einsum("hrk,rhd->khd", probs_low, g_heads, preferred_element_type=jnp.float32)
    grad_key = jnp.einsum("hrk,rhd->khd", dscore, q_heads, preferred_element_type=jnp.float32)
    all_rows = whole_q.shape[0]
    owner_start = owner_query * dec_rows
    own_term = jnp.einsum(
        "hrk,khd->rhd", dscore, k_heads, preferred_element_type=jnp.float32
    ).reshape(dec_rows, width)
    dense_term = lax.dynamic_update_slice_in_dim(
        jnp.zeros((all_rows, width), jnp.float32), own_term, owner_start, 0
    )
    grad_rows = lax.psum_scatter(dense_term, "psg", scatter_dimension=0, tiled=True)
    grad_queries = grad_rows.astype(jnp.bfloat16)
    grad_keys = grad_key.reshape(1, slot_count, width).astype(jnp.bfloat16)
    grad_values = grad_val.reshape(1, slot_count, width).astype(jnp.bfloat16)
    return (grad_queries, grad_keys, grad_values)


def solution(mesh):
    placed = (
        P(("group", "psg"), None),
        P(("group", "psg"), None, None),
        P(("group", "psg"), None, None),
        P(("group", "psg"), None),
        P(("group", "psg")),
        P(("group", "psg")),
    )
    return jax.shard_map(
        per_device,
        mesh=mesh,
        in_specs=placed,
        out_specs=(
            P(("group", "psg"), None),
            P(("group", "psg"), None, None),
            P(("group", "psg"), None, None),
        ),
        check_vma=False,
    )
```

profile of v0, /device:TPU:25, one launch (start us, length us, event | category | flops | bytes accessed | tf_op | source)
XLA Modules:
  0.0 748.1 jit_solution(17402392121266230271)
XLA Ops:
  7.2 0.0 all-gather.3.cloned.1.call-start
  7.2 0.7 all-gather.3.cloned.1.call-update
  7.9 0.0 all-gather.5.cloned.1.call-start
  7.9 0.7 all-gather.5.cloned.1.call-update
  8.6 0.0 all-reduce.4.cloned.1.call-start
  10.0 2.9 copy.21
  12.9 3.9 copy.23
  16.8 76.1 %all-gather.3.cloned.1.call-done = bf16[1024,2048]{1,0:T(8,128)(2,1)} async-done(((bf16[16,2048]{1,0:T(8,128)(2,1)}), bf16[1024,2048]{1,0:T(8,128)(2,1)}) %all-gather.3.cloned.1.call-update) | async-done | bytes 4194320 | tf_op jit(solution)/shard_map/all_gather | solution.py:14
  92.9 79.1 %all-gather.5.cloned.1.call-done = bf16[1024,2048]{1,0:T(8,128)(2,1)} async-done(((bf16[16,2048]{1,0:T(8,128)(2,1)}), bf16[1024,2048]{1,0:T(8,128)(2,1)}) %all-gather.5.cloned.1.call-update) | async-done | bytes 4194320 | tf_op jit(solution)/shard_map/all_gather | solution.py:15
  172.0 4.8 constant_dynamic-slice_fusion
  176.8 3.9 copy.20
  180.8 3.9 copy.22
  184.7 15.4 %select_reduce_fusion = (f32[32,512]{1,0:T(8,128)S(1)}, f32[32,512,512]{1,2,0:T(8,128)}) fusion(pred[512]{0:T(512)(128)(4,1)S(1)} %iota_compare_fusion, bf16[512,32,64]{0,2,1:T(8,128)(2,1)} %bitcast.58, bf16[512,32,64]{0,2,1:T(8,128)(2,1)S(1)} %bitcast.55), kind=kOutput, calls=%fused_computation.5 | convolution fusion | flops 1090502656 | bytes 37814784 | tf_op jit(solution)/shard_map/rhd,khd->hrk/dot_general | solution.py:30
  200.1 0.7 select_convert_fusion
  200.8 0.0 all-reduce.4.cloned.1.call-update
  200.8 0.0 all-reduce.6.cloned.1.call-start
  200.9 27.0 %fusion = (f32[32,512]{1,0:T(8,128)S(1)}, f32[32,512]{1,0:T(8,128)S(1)}, f32[32,512,512]{1,2,0:T(8,128)}) fusion(f32[32,512,512]{1,2,0:T(8,128)} %get-tuple-element.18, f32[32,512]{1,0:T(8,128)S(1)} %get-tuple-element.17, pred[512]{0:T(512)(128)(4,1)S(1)} %iota_compare_fusion, bf16[512,32,64]{0,2,1:T(8,128)(2,1)} %bitcast.60, bf16[512,32,64]{0,2,1:T(8,128)(2,1)} %bitcast.62), kind=kOutput, calls=%fused_computation.4 | convolution fusion | flops 1115652096 | bytes 71500288 | tf_op jit(solution)/shard_map/rhd,khd->hrk/dot_general | solution.py:32
  227.9 138.4 %all-reduce.4.cloned.1.call-done = bf16[2,32,512]{2,1,0:T(8,128)(2,1)} async-done(((bf16[2,32,512]{2,1,0:T(8,128)(2,1)}), bf16[2,32,512]{2,1,0:T(8,128)(2,1)}) %all-reduce.4.cloned.1.call-update) | async-done | bytes 65552 | tf_op jit(solution)/shard_map/pmax | solution.py:42
  366.2 0.8 fusion.8
  367.0 0.8 broadcast_select_fusion.1
  367.8 0.0 all-reduce.6.cloned.1.call-update
  367.9 0.2 reduce-scatter.2.cloned.1.call-start
  368.1 0.8 convert_bitcast_fusion
  368.9 174.3 %all-reduce.6.cloned.1.call-done = (f32[2,32,512]{2,1,0:T(8,128)}, f32[2,32,512]{2,1,0:T(8,128)}) async-done(((f32[2,32,512]{2,1,0:T(8,128)}, f32[2,32,512]{2,1,0:T(8,128)}), (f32[2,32,512]{2,1,0:T(8,128)}, f32[2,32,512]{2,1,0:T(8,128)})) %all-reduce.6.cloned.1.call-update) | async-done | bytes 262160 | tf_op jit(solution)/shard_map/psum | solution.py:45
  543.2 0.8 dynamic-slice_bitcast_fusion
  544.0 0.9 bitcast_divide_fusion
  544.9 27.7 %multiply_convert_fusion = bf16[32,512,512]{1,2,0:T(8,128)(2,1)} fusion(f32[32,512,512]{1,2,0:T(8,128)} %get-tuple-element.19, f32[32,512]{1,0:T(8,128)S(1)} %bitcast_divide_fusion, f32[32,512]{1,0:T(8,128)S(1)} %dynamic-slice_bitcast_fusion, f32[32,512]{1,0:T(8,128)S(1)} %convert_bitcast_fusion, f32[32,512,512]{1,2,0:T(8,128)} %get-tuple-element.18, ...), kind=kLoop, calls=%fused_computation | loop fusion | flops 50331648 | bytes 84083200 | tf_op jit(solution)/shard_map/convert_element_type | solution.py:52
  572.6 10.8 %fusion.9 = f32[32,512,64]{1,2,0:T(8,128)} fusion(bf16[512,32,64]{0,2,1:T(8,128)(2,1)S(1)} %bitcast.56, bf16[32,512,512]{1,2,0:T(8,128)(2,1)} %multiply_convert_fusion), kind=kOutput, calls=%fused_computation.27 | convolution fusion | flops 1073741824 | bytes 23068672 | tf_op jit(solution)/shard_map/hrk,khd->rhd/dot_general | solution.py:57
  583.4 5.4 copy.25
  588.8 0.0 copy-start.1
  588.8 4.3 broadcast_in_dim.66
  593.1 0.0 copy-done.1
  593.1 2.3 constant_dynamic-update-slice_fusion
  595.4 0.0 reduce-scatter.2.cloned.1.call-update
  595.5 0.0 copy-start
  595.5 16.6 %fusion.3 = bf16[32,64,512]{2,1,0:T(8,128)(2,1)} fusion(bf16[512,32,64]{0,2,1:T(8,128)(2,1)} %bitcast.61, f32[32,512,512]{1,2,0:T(8,128)} %get-tuple-element.18, f32[32,512]{1,0:T(8,128)S(1)} %dynamic-slice_bitcast_fusion, f32[32,512]{1,0:T(8,128)S(1)} %convert_bitcast_fusion, pred[512]{0:T(512)(128)(4,1)S(1)} %iota_compare_fusion), kind=kOutput, calls=%fused_computation.9 | convolution fusion | flops 1108344832 | bytes 37880320 | tf_op jit(solution)/shard_map/hrk,rhd->khd/dot_general | solution.py:53
  612.0 3.9 copy.29
  616.0 0.0 copy-done
  616.0 12.7 %convolution_convert_fusion = bf16[32,64,512]{2,1,0:T(8,128)(2,1)} fusion(bf16[512,32,64]{0,2,1:T(8,128)(2,1)S(1)} %bitcast.59, bf16[32,512,512]{1,2,0:T(8,128)(2,1)} %multiply_convert_fusion), kind=kOutput, calls=%fused_computation.8 | convolution fusion | flops 1074790400 | bytes 20971520 | tf_op jit(solution)/shard_map/hrk,rhd->khd/dot_general | solution.py:54
  628.7 4.0 copy.28
  632.7 107.4 %reduce-scatter.2.cloned.1.call-done = f32[16,2048]{1,0:T(8,128)} async-done(((f32[1024,2048]{1,0:T(8,128)}), f32[16,2048]{1,0:T(8,128)}) %reduce-scatter.2.cloned.1.call-update) | async-done | bytes 131088 | tf_op jit(solution)/shard_map/reduce_scatter | solution.py:63
  740.0 1.5 convert_element_type.52
  (2 shorter events, 0.0 us)
Async XLA Ops:
  7.2 85.7 %all-gather.3.cloned.1.call-start = ((), (), s32[]{:S(2)}) async-start(), calls=%async_computation.1 | async-start | bytes 4259840 | tf_op jit(solution)/shard_map/all_gather | solution.py:14
  7.9 164.1 %all-gather.5.cloned.1.call-start = ((), (), s32[]{:S(2)}) async-start(), calls=%async_computation.3 | async-start | bytes 4259840 | tf_op jit(solution)/shard_map/all_gather | solution.py:15
  8.6 357.6 %all-reduce.4.cloned.1.call-start = ((), (), s32[]{:S(2)}) async-start(), calls=%async_computation.2 | async-start | bytes 131072 | tf_op jit(solution)/shard_map/pmax | solution.py:42
  200.8 342.4 %all-reduce.6.cloned.1.call-start = ((), (), s32[]{:S(2)}) async-start(), calls=%async_computation.5 | async-start | bytes 524288 | tf_op jit(solution)/shard_map/psum | solution.py:45
  367.9 372.2 %reduce-scatter.2.cloned.1.call-start = ((), (), s32[]{:S(2)}) async-start(), calls=%async_computation.4 | async-start | bytes 8519680 | tf_op jit(solution)/shard_map/reduce_scatter | solution.py:63
  588.8 4.3 copy-start.1
  595.5 20.5 %copy-start = (bf16[512,2048]{0,1:T(8,128)(2,1)S(1)}, bf16[512,2048]{0,1:T(8,128)(2,1)}, u32[]{:S(2)}) copy-start(bf16[512,2048]{0,1:T(8,128)(2,1)} %copy.20) | copy-start | bytes 6291460
Sparse Core Ops, SparseCore 0:
  10.8 82.0 all-gather.2
  95.7 76.2 all-gather.4
  200.9 165.2 all-reduce.3
  370.6 172.4 all-reduce.5
  595.6 144.3 reduce-scatter.1
where the time goes:
time: 754 us; the launch traced here: 748 us
  waiting for transfers between devices  577 us (77%)
  matrix products  82.5 us (11%)
  local copies, waits for them, and re-layouts  40.2 us (5%)
  other arithmetic  33.2 us (4%)
  between operations  15.1 us (2%)
    psum x1, waiting for transfers between devices, per_device(): lax.psum((place_rows(local_sum * factor, 0.0), place_rows(local_dot * fac...  174 us
    pmax x1, waiting for transfers between devices, per_device(): lax.pmax(place_rows(local_max, -1e+30).astype(jnp.bfloat16), 'psg')  138 us
    reduce_scatter x1, waiting for transfers between devices, per_device(): lax.psum_scatter(dense_term, 'psg', scatter_dimension=0, tiled=True)  107 us
    all_gather x1, waiting for transfers between devices, per_device(): lax.all_gather(grad_out, 'psg', axis=0, tiled=True)  79.1 us
    all_gather x1, waiting for transfers between devices, per_device(): lax.all_gather(queries, 'psg', axis=0, tiled=True)  76.1 us
    convert_element_type x1, other arithmetic, per_device(): (attn_probs * (upstream - row_delta[..., None])).astype(jnp.bfloat16)  27.7 us
    dot_general x1, matrix products, per_device(): jnp.einsum('rhd,khd->hrk', g_heads, v_heads, preferred_element_type=jnp.f...  27 us
    dot_general x1, matrix products, per_device(): jnp.einsum('hrk,rhd->khd', probs_low, g_heads, preferred_element_type=jnp...  16.6 us
  transfers between devices with their start and end apart: 5, of which 5 were waited for; matrix products, arithmetic and copies ran while one was open for 10% of the time, Pallas kernels for 0%

commit v1 on v0

v1 whole, which is shorter than its diff:
```python
import jax
import jax.numpy as jnp
from jax import lax
from jax.experimental import pallas as pl
from jax.experimental.pallas import tpu as pltpu
from jax.sharding import Mesh
from jax.sharding import PartitionSpec as P

HDIM = 64
BKT = 64
QRY = 2
LANES = 128
F32 = jnp.float32
BF16 = jnp.bfloat16
CHIP = ("x", "z")


def shifted(value, axis, size, step):
    return lax.ppermute(value, axis, [(i, (i + step) % size) for i in range(size)])


def swap_cores(value):
    return lax.ppermute(value, "core", [(0, 1), (1, 0)])


def placed(pieces, index, count):
    whole = jnp.zeros((count,) + pieces[0][1].shape, pieces[0][1].dtype)
    for offset, piece in pieces:
        whole = lax.dynamic_update_slice_in_dim(whole, piece[None], (index + offset) % count, 0)
    return whole


def direct_gather(value, axis, size):
    pieces = [(0, value)]
    for step in range(1, size):
        pieces.append((-step, shifted(value, axis, size, step)))
    return placed(pieces, lax.axis_index(axis), size)


def ring_gather(value, axis, size):
    pieces, up, down = [(0, value)], value, value
    for step in range(1, size // 2):
        up, down = shifted(up, axis, size, 1), shifted(down, axis, size, -1)
        pieces += [(-step, up), (step, down)]
    half = value.shape[0] // 2
    last = jnp.concatenate(
        [shifted(up[:half], axis, size, 1), shifted(down[half:], axis, size, -1)], 0
    )
    pieces.append((size // 2, last))
    return placed(pieces, lax.axis_index(axis), size)


def gather_rows(value, x_size, z_size, x_first):
    rows, width = value.shape
    if x_first:
        part = direct_gather(value, "x", x_size).reshape(x_size * rows, width)
        whole = ring_gather(part, "z", z_size).reshape(z_size, x_size, rows, width)
        return whole.transpose(1, 0, 2, 3).reshape(-1, width)
    part = direct_gather(value, "z", z_size).reshape(z_size * rows, width)
    return ring_gather(part, "x", x_size).reshape(-1, width)


def dot_nt(a, b):
    return lax.dot_general(a, b, (((1,), (1,)), ((), ())), preferred_element_type=F32)


def dot_nn(a, b):
    return lax.dot_general(a, b, (((1,), (0,)), ((), ())), preferred_element_type=F32)


def over_chunks(buckets, step):
    fours = buckets // 4

    def body(i, carry):
        step(pl.multiple_of(i * (4 * BKT), 4 * BKT), 4 * BKT)
        return carry

    lax.fori_loop(0, fours, body, 0)
    start = fours * (4 * BKT)

    @pl.when((buckets & 2) != 0)
    def _():
        step(pl.multiple_of(start, 4 * BKT), 2 * BKT)

    @pl.when((buckets & 1) != 0)
    def _():
        step(pl.multiple_of(start + (buckets & 2) * BKT, BKT), BKT)


def load_keys(own_k, sib_k, own_v, sib_v, keys, vals):
    keys[0], keys[1] = own_k[...], sib_k[...]
    vals[0], vals[1] = own_v[...], sib_v[...]


def load_rows(owner, rows, q_ref, g_ref, q_head, g_head):
    at = pl.ds(pl.multiple_of(owner * rows, rows), rows)
    q_rows, g_rows = q_ref[at, :], g_ref[at, :]
    lane = lax.broadcasted_iota(jnp.int32, (rows, LANES), 1)
    for h in range(2):
        mine = (lane < HDIM) if h == 0 else (lane >= HDIM)
        q_head[h] = jnp.where(mine, q_rows, jnp.zeros_like(q_rows))
        g_head[h] = jnp.where(mine, g_rows, jnp.zeros_like(g_rows))


def stats_kernel(info, own_k, sib_k, own_v, sib_v, q_ref, g_ref, out_ref,
                 keys, vals, q_head, g_head, top, total, dotted):
    rows = q_head.shape[1]
    load_keys(own_k, sib_k, own_v, sib_v, keys, vals)

    def passage(p, carry):
        load_rows(info[1 + p], rows, q_ref, g_ref, q_head, g_head)
        top[...] = jnp.full(top.shape, -jnp.inf, F32)
        total[...] = jnp.zeros(total.shape, F32)
        dotted[...] = jnp.zeros(dotted.shape, F32)

        def step(start, count):
            k_part = keys[p, pl.ds(start, count), :]
            v_part = vals[p, pl.ds(start, count), :]
            for h in range(2):
                scores = dot_nt(k_part, q_head[h]).reshape(count // 8, 8, rows)
                upstream = dot_nt(v_part, g_head[h]).reshape(count // 8, 8, rows)
                old = top[h]
                new = jnp.maximum(old, jnp.max(scores, axis=0))
                weights = jnp.exp(scores - new[None])
                factor = jnp.exp(old - new)
                top[h] = new
                total[h] = total[h] * factor + jnp.sum(weights, axis=0)
                dotted[h] = dotted[h] * factor + jnp.sum(weights * upstream, axis=0)

        over_chunks(info[3 + p], step)
        half = rows // 2
        for h in range(2):
            peak = jnp.max(top[h], axis=0, keepdims=True)
            factor = jnp.exp(top[h] - peak)
            stats = (
                peak,
                jnp.sum(total[h] * factor, axis=0, keepdims=True),
                jnp.sum(dotted[h] * factor, axis=0, keepdims=True),
                jnp.full((1, rows), info[1 + p].astype(F32)),
            )
            for s in range(2):
                for t, stat in enumerate(stats):
                    out_ref[2 * h + s, pl.ds(2 * t + p, 1), :] = stat[:, s * half:(s + 1) * half]
        return carry

    lax.fori_loop(0, 2, passage, 0)


def merge_kernel(in_ref, out_ref):
    chips = in_ref.shape[0]
    merged = []
    tops = [in_ref[:, t, :] for t in range(2)]
    sums = [in_ref[:, 2 + t, :] for t in range(2)]
    dots = [in_ref[:, 4 + t, :] for t in range(2)]
    owners = [in_ref[:, 6 + t, :] for t in range(2)]
    for query in range(QRY):
        held = [jnp.where(owners[t] == query, tops[t], -jnp.inf) for t in range(2)]
        peak = jnp.max(jnp.maximum(held[0], held[1]), axis=0, keepdims=True)
        factors = [jnp.exp(held[t] - peak) for t in range(2)]
        total = jnp.sum(sums[0] * factors[0] + sums[1] * factors[1], axis=0, keepdims=True)
        dotted = jnp.sum(dots[0] * factors[0] + dots[1] * factors[1], axis=0, keepdims=True)
        merged.append((peak + jnp.log(total), dotted / total))
    table = jnp.concatenate(
        [merged[0][0], merged[1][0], merged[0][1], merged[1][1]]
        + [jnp.zeros_like(merged[0][0])] * 4, axis=0
    )
    out_ref[...] = jnp.broadcast_to(table[None], out_ref.shape)


def grads_kernel(info, own_k, sib_k, own_v, sib_v, q_ref, g_ref, st_ref,
                 own_dk, sib_dk, own_dv, sib_dv, dq_ref,
                 keys, vals, q_head, g_head, dkeys, dvals, turned, dq_sum):
    rows = q_head.shape[1]
    load_keys(own_k, sib_k, own_v, sib_v, keys, vals)
    dkeys[...] = jnp.zeros(dkeys.shape, BF16)
    dvals[...] = jnp.zeros(dvals.shape, BF16)
    dq_sum[...] = jnp.zeros(dq_sum.shape, F32)

    def passage(p, carry):
        owner = info[1 + p]
        load_rows(owner, rows, q_ref, g_ref, q_head, g_head)
        turned[...] = jnp.zeros(turned.shape, F32)

        def row_stat(h, t):
            return jnp.concatenate(
                [st_ref[2 * h + s, pl.ds(2 * t + owner, 1), :] for s in range(2)], axis=1
            )

        def step(start, count):
            at = pl.ds(start, count)
            k_part, v_part = keys[p, at, :], vals[p, at, :]
            k_turned = k_part.T
            dk_part = dv_part = None
            for h in range(2):
                probs = jnp.exp(dot_nt(k_part, q_head[h]) - row_stat(h, 0))
                dscore = (probs * (dot_nt(v_part, g_head[h]) - row_stat(h, 1))).astype(BF16)
                dv_term = dot_nn(probs.astype(BF16), g_head[h])
                dk_term = dot_nn(dscore, q_head[h])
                dv_part = dv_term if h == 0 else dv_part + dv_term
                dk_part = dk_term if h == 0 else dk_part + dk_term
                own = slice(h * HDIM, (h + 1) * HDIM)
                turned[own, :] += dot_nn(k_turned[own, :], dscore)
            dkeys[p, at, :] = dk_part.astype(BF16)
            dvals[p, at, :] = dv_part.astype(BF16)

        over_chunks(info[3 + p], step)
        at = pl.ds(pl.multiple_of(owner * rows, rows), rows)
        dq_sum[at, :] += turned[...].T
        return carry

    lax.fori_loop(0, 2, passage, 0)
    own_dk[...], sib_dk[...] = dkeys[0], dkeys[1]
    own_dv[...], sib_dv[...] = dvals[0], dvals[1]
    dq_ref[...] = dq_sum[...].astype(BF16)


def per_device(x_size, z_size, queries, keys, values, grad_out, lengths, slot_query):
    chips = x_size * z_size
    core = lax.axis_index("core")
    slots, width = keys.shape[1], keys.shape[2]
    half = width // 2
    pairs = half // LANES
    keys, values = keys[0], values[0]

    mine = jnp.concatenate([slot_query, lengths])
    theirs = swap_cores(mine)
    info = jnp.stack([core, mine[0], theirs[0], mine[1], theirs[1]]).astype(jnp.int32)

    def features(value, of_core):
        return lax.dynamic_slice_in_dim(value, of_core * half, half, value.ndim - 1)

    def chip_rows(value):
        return features(lax.all_gather(value, "core", axis=0, tiled=True), core)

    whole_q = gather_rows(chip_rows(queries), x_size, z_size, True)
    whole_g = gather_rows(chip_rows(grad_out), x_size, z_size, False)
    sib_k = swap_cores(features(keys, 1 - core))
    sib_v = swap_cores(features(values, 1 - core))
    all_rows = whole_q.shape[0]
    rows = all_rows // QRY
    limit = pltpu.CompilerParams(
        dimension_semantics=("arbitrary",), vmem_limit_bytes=48 * 1024 * 1024
    )

    own_block = pl.BlockSpec((slots, LANES), lambda i, info: (0, info[0] * pairs + i))
    sib_block = pl.BlockSpec((slots, LANES), lambda i, info: (0, i))
    row_block = pl.BlockSpec((all_rows, LANES), lambda i, info: (0, i))
    stat_block = pl.BlockSpec((4, 8, rows // 2), lambda i, info: (i, 0, 0))
    stat_shape = jax.ShapeDtypeStruct((4 * pairs, 8, rows // 2), F32)
    key_scratch = [pltpu.VMEM((2, slots, LANES), BF16)] * 2
    row_scratch = [pltpu.VMEM((2, rows, LANES), BF16)] * 2
    operands = (info, keys, sib_k, values, sib_v, whole_q, whole_g)
    in_blocks = [own_block, sib_block, own_block, sib_block, row_block, row_block]

    stats = pl.pallas_call(
        stats_kernel,
        grid_spec=pltpu.PrefetchScalarGridSpec(
            num_scalar_prefetch=1,
            grid=(pairs,),
            in_specs=in_blocks,
            out_specs=stat_block,
            scratch_shapes=key_scratch + row_scratch + [pltpu.VMEM((2, 8, rows), F32)] * 3,
        ),
        out_shape=stat_shape,
        compiler_params=limit,
        name="row_stats",
    )(*operands)

    stats = lax.all_to_all(stats, CHIP, 0, 0, tiled=True)
    stats = pl.pallas_call(
        merge_kernel,
        out_shape=stat_shape,
        in_specs=[pl.BlockSpec(memory_space=pltpu.VMEM)],
        out_specs=pl.BlockSpec(memory_space=pltpu.VMEM),
        name="merge_stats",
    )(stats)
    stats = lax.all_to_all(stats, CHIP, 0, 0, tiled=True)

    own_dk, sib_dk, own_dv, sib_dv, dq = pl.pallas_call(
        grads_kernel,
        grid_spec=pltpu.PrefetchScalarGridSpec(
            num_scalar_prefetch=1,
            grid=(pairs,),
            in_specs=in_blocks + [stat_block],
            out_specs=[own_block, sib_block, own_block, sib_block, row_block],
            scratch_shapes=key_scratch + row_scratch + key_scratch
            + [pltpu.VMEM((LANES, rows), F32), pltpu.VMEM((all_rows, LANES), F32)],
        ),
        out_shape=[
            jax.ShapeDtypeStruct((slots, width), BF16),
            jax.ShapeDtypeStruct((slots, half), BF16),
            jax.ShapeDtypeStruct((slots, width), BF16),
            jax.ShapeDtypeStruct((slots, half), BF16),
            jax.ShapeDtypeStruct((all_rows, half), BF16),
        ],
        compiler_params=limit,
        name="gradients",
    )(*operands, stats)

    chip_rows_count = all_rows // chips
    terms = lax.all_to_all(dq.reshape(chips, chip_rows_count, half), CHIP, 0, 0, tiled=True)
    summed = jnp.sum(terms.astype(F32), axis=0).astype(BF16)
    own_rows = chip_rows_count // 2
    kept = lax.dynamic_slice_in_dim(summed, core * own_rows, own_rows, 0)
    given = swap_cores(lax.dynamic_slice_in_dim(summed, (1 - core) * own_rows, own_rows, 0))
    grad_queries = jnp.where(
        core == 0, jnp.concatenate([kept, given], 1), jnp.concatenate([given, kept], 1)
    )

    def completed(own, sib):
        return lax.dynamic_update_slice_in_dim(own, swap_cores(sib), (1 - core) * half, 1)[None]

    return grad_queries, completed(own_dk, sib_dk), completed(own_dv, sib_dv)


def solution(mesh):
    groups = mesh.devices.shape[0]
    x_size, z_size = 4, 8
    fine = Mesh(
        mesh.devices.reshape(groups, x_size, z_size, 2), ("group", "x", "z", "core")
    )
    at = ("group", "x", "z", "core")

    def step(*args):
        return per_device(x_size, z_size, *args)

    return jax.shard_map(
        step,
        mesh=fine,
        in_specs=(P(at, None), P(at, None, None), P(at, None, None), P(at, None), P(at), P(at)),
        out_specs=(P(at, None), P(at, None, None), P(at, None, None)),
        check_vma=False,
    )
```

time: 754 us -> 243 us (0.32)
  the two profiles are of different devices: /device:TPU:25 before, /device:TPU:17 now
where the time goes in v1:
time: 243 us
  starting transfers between devices  66.5 us (27%)
  waiting for transfers between devices  58.1 us (24%)
  Pallas kernels  57.7 us (24%)
  blocking collectives  35.4 us (15%)
  local copies, waits for them, and re-layouts  20.1 us (8%)
  other arithmetic  2.74 us (1%)
    ppermute x22, starting transfers between devices, shifted(): lax.ppermute(value, axis, [(i, (i + step) % size) for i in range(size)])  39.4 us
    all_to_all x1, waiting for transfers between devices, per_device(): lax.all_to_all(dq.reshape(chips, chip_rows_count, half), CHIP, 0, 0, tile...  36.4 us
    pallas_call x1, Pallas kernels, per_device(): pl.pallas_call(grads_kernel, grid_spec=pltpu.PrefetchScalarGridSpec(num_s...  36.3 us
    all_to_all x2, blocking collectives, per_device(): stats = lax.all_to_all(stats, CHIP, 0, 0, tiled=True)  30.7 us
    pallas_call x1, Pallas kernels, per_device(): pl.pallas_call(stats_kernel, grid_spec=pltpu.PrefetchScalarGridSpec(num_s...  19.5 us
    ppermute x22, waiting for transfers between devices, shifted(): lax.ppermute(value, axis, [(i, (i + step) % size) for i in range(size)])  18.9 us
    ppermute x6, starting transfers between devices, swap_cores(): return lax.ppermute(value, 'core', [(0, 1), (1, 0)])  17.4 us
    all_to_all x1, starting transfers between devices, per_device(): lax.all_to_all(dq.reshape(chips, chip_rows_count, half), CHIP, 0, 0, tile...  9.69 us
  transfers between devices with their start and end apart: 29, of which 11 were waited for; matrix products, arithmetic and copies ran while one was open for 8% of the time, Pallas kernels for 0%

profile of v1, /device:TPU:17, one launch (start us, length us, event | category | flops | bytes accessed | tf_op | source)
XLA Modules:
  0.0 242.8 jit_solution(5251352672117520883)
XLA Ops:
  0.7 2.6 %all_gather.7 = bf16[32,2048]{1,0:T(8,128)(2,1)S(1)} all-gather(bf16[16,2048]{1,0:T(8,128)(2,1)} %param.9), channel_id=1, replica_groups=mesh['group'=4,'x'=4,'z'=8,'core'=2] {'core'}, dimensions={0}, use_global_device_ids=true | all-gather | bytes 196608 | tf_op jit(solution)/shard_map/all_gather | solution.py:233
  3.2 0.9 broadcast_in_dim.102
  4.7 1.6 collective-permute-start.14
  6.4 3.0 %collective-permute-start.15 = (bf16[32,1024]{1,0:T(8,128)(2,1)S(1)}, bf16[32,1024]{1,0:T(8,128)(2,1)S(1)}, u32[]{:S(2)}, u32[]{:S(2)}) collective-permute-start(bf16[32,1024]{1,0:T(8,128)(2,1)S(1)} %get-tuple-element.14), channel_id=1, source_target_pairs={{0,4},{2,6},{4,8},{6,10},{8,12},{10,14},{12,0},{14,2},{1,5},{3,7},... | collective-permute-start | bytes 196616 | tf_op jit(solution)/shard_map/ppermute | solution.py:19
  9.4 3.7 %collective-permute-start.16 = (bf16[32,1024]{1,0:T(8,128)(2,1)S(1)}, bf16[32,1024]{1,0:T(8,128)(2,1)S(1)}, u32[]{:S(2)}, u32[]{:S(2)}) collective-permute-start(bf16[32,1024]{1,0:T(8,128)(2,1)S(1)} %get-tuple-element.14), channel_id=1, source_target_pairs={{0,6},{2,8},{4,10},{6,12},{8,14},{10,0},{12,2},{14,4},{1,7},{3,9},... | collective-permute-start | bytes 196616 | tf_op jit(solution)/shard_map/ppermute | solution.py:19
  14.9 1.3 collective-permute-start
  16.2 2.1 all_gather.6
  18.3 2.3 dynamic-slice_bitcast_fusion.1
  20.6 1.1 dynamic-slice_bitcast_fusion
  21.7 4.7 %collective-permute-start.18 = (bf16[32,1024]{1,0:T(8,128)(2,1)S(1)}, bf16[32,1024]{1,0:T(8,128)(2,1)S(1)}, u32[]{:S(2)}, u32[]{:S(2)}) collective-permute-start(bf16[32,1024]{1,0:T(8,128)(2,1)S(1)} %get-tuple-element.14), channel_id=1, source_target_pairs={{0,10},{2,12},{4,14},{6,0},{8,2},{10,4},{12,6},{14,8},{1,11},{3,13... | collective-permute-start | bytes 196616 | tf_op jit(solution)/shard_map/ppermute | solution.py:19
  27.1 1.3 stack.7.info
  28.4 2.4 collective-permute-start.19
  32.8 1.2 collective-permute-start.3
  34.7 2.5 %collective-permute-done.3 = bf16[32,1024]{1,0:T(8,128)(2,1)S(1)} collective-permute-done((bf16[32,1024]{1,0:T(8,128)(2,1)S(1)}, bf16[32,1024]{1,0:T(8,128)(2,1)S(1)}, u32[]{:S(2)}, u32[]{:S(2)}) %collective-permute-start.3) | collective-permute-done | bytes 65568 | tf_op jit(solution)/shard_map/ppermute | solution.py:19
  37.1 1.8 collective-permute-start.4
  39.0 2.8 %collective-permute-done.4 = bf16[32,1024]{1,0:T(8,128)(2,1)S(1)} collective-permute-done((bf16[32,1024]{1,0:T(8,128)(2,1)S(1)}, bf16[32,1024]{1,0:T(8,128)(2,1)S(1)}, u32[]{:S(2)}, u32[]{:S(2)}) %collective-permute-start.4) | collective-permute-done | bytes 65568 | tf_op jit(solution)/shard_map/ppermute | solution.py:19
  41.8 1.5 collective-permute-start.5
  43.3 1.6 collective-permute-done.5
  44.9 4.6 %collective-permute-start.1 = (bf16[512,1024]{1,0:T(8,128)(2,1)}, bf16[512,1024]{1,0:T(8,128)(2,1)S(1)}, u32[]{:S(2)}, u32[]{:S(2)}) collective-permute-start(bf16[512,1024]{1,0:T(8,128)(2,1)} %dynamic-slice_bitcast_fusion.1), channel_id=1, source_target_pairs={{0,1},{1,0},{2,3},{3,2},{4,5},{5,4},{6,7},{7,6},{8,9},{9,8},{10,11... | collective-permute-start | bytes 3145736 | tf_op jit(solution)/shard_map/ppermute | solution.py:23
  49.5 0.8 collective-permute-start.6
  52.9 2.6 %collective-permute-start.22 = (bf16[256,1024]{1,0:T(8,128)(2,1)}, bf16[256,1024]{1,0:T(8,128)(2,1)S(1)}, u32[]{:S(2)}, u32[]{:S(2)}) collective-permute-start(bf16[256,1024]{1,0:T(8,128)(2,1)} %bitcast.30), channel_id=1, source_target_pairs={{0,48},{16,0},{32,16},{48,32},{1,49},{17,1},{33,17},{49,33},{2,50}... | collective-permute-start | bytes 1572872 | tf_op jit(solution)/shard_map/ppermute | solution.py:19
  55.5 1.9 collective-permute-start.7
  57.7 1.1 bitcast_dynamic-update-slice_fusion.4
  59.2 3.3 %collective-permute-done.7 = bf16[128,1024]{1,0:T(8,128)(2,1)S(1)} collective-permute-done((bf16[128,1024]{1,0:T(8,128)(2,1)S(1)}, bf16[128,1024]{1,0:T(8,128)(2,1)S(1)}, u32[]{:S(2)}, u32[]{:S(2)}) %collective-permute-start.7) | collective-permute-done | bytes 262176 | tf_op jit(solution)/shard_map/ppermute | solution.py:19
  62.5 3.1 %collective-permute-start.9 = (bf16[128,1024]{1,0:T(8,128)(2,1)S(1)}, bf16[128,1024]{1,0:T(8,128)(2,1)S(1)}, u32[]{:S(2)}, u32[]{:S(2)}) collective-permute-start(bf16[128,1024]{1,0:T(8,128)(2,1)S(1)} %collective-permute-done.7), channel_id=1, source_target_pairs={{0,14},{2,0},{4,2},{6,4},{8,6},{10,8},{12,10},{14,12},{1,15},{3,1}... | collective-permute-start | bytes 786440 | tf_op jit(solution)/shard_map/ppermute | solution.py:19
  65.7 1.8 collective-permute-done.21
  67.5 1.1 collective-permute-start.2
  69.5 3.4 %collective-permute-start.11 = (bf16[128,1024]{1,0:T(8,128)(2,1)S(1)}, bf16[128,1024]{1,0:T(8,128)(2,1)S(1)}, u32[]{:S(2)}, u32[]{:S(2)}) collective-permute-start(bf16[128,1024]{1,0:T(8,128)(2,1)S(1)} %collective-permute-done.9), channel_id=1, source_target_pairs={{0,14},{2,0},{4,2},{6,4},{8,6},{10,8},{12,10},{14,12},{1,15},{3,1}... | collective-permute-start | bytes 786440 | tf_op jit(solution)/shard_map/ppermute | solution.py:19
  73.1 4.1 %collective-permute-done.10 = bf16[128,1024]{1,0:T(8,128)(2,1)S(1)} collective-permute-done((bf16[128,1024]{1,0:T(8,128)(2,1)S(1)}, bf16[128,1024]{1,0:T(8,128)(2,1)S(1)}, u32[]{:S(2)}, u32[]{:S(2)}) %collective-permute-start.10) | collective-permute-done | bytes 262176 | tf_op jit(solution)/shard_map/ppermute | solution.py:19
  77.2 3.1 %collective-permute-start.24 = (bf16[128,1024]{1,0:T(8,128)(2,1)S(1)}, bf16[128,1024]{1,0:T(8,128)(2,1)S(1)}, u32[]{:S(2)}, u32[]{:S(2)}) collective-permute-start(bf16[128,1024]{1,0:T(8,128)(2,1)S(1)} %slice.27), channel_id=1, source_target_pairs={{0,48},{16,0},{32,16},{48,32},{1,49},{17,1},{33,17},{49,33},{2,50}... | collective-permute-start | bytes 786440 | tf_op jit(solution)/shard_map/ppermute | solution.py:19
  80.4 2.7 %collective-permute-start.13 = (bf16[64,1024]{1,0:T(8,128)(2,1)S(1)}, bf16[64,1024]{1,0:T(8,128)(2,1)S(1)}, u32[]{:S(2)}, u32[]{:S(2)}) collective-permute-start(bf16[64,1024]{1,0:T(8,128)(2,1)S(1)} %slice.25), channel_id=1, source_target_pairs={{0,14},{2,0},{4,2},{6,4},{8,6},{10,8},{12,10},{14,12},{1,15},{3,1}... | collective-permute-start | bytes 393224 | tf_op jit(solution)/shard_map/ppermute | solution.py:19
  83.2 1.6 collective-permute-done.24
  85.5 1.6 copy.9
  87.1 0.8 copy-done
  87.9 19.5 %row_stats.1 = f32[32,8,256]{2,1,0:T(8,128)S(1)} custom-call(s32[5]{0:T(128)S(1)} %stack.7.info, bf16[512,2048]{1,0:T(8,128)(2,1)S(1)} %bitcast.76, bf16[512,1024]{1,0:T(8,128)(2,1)S(1)} %collective-permute-done.1.sib_k, bf16[512,2048]{1,0:T(8,128)(2,1)} %bitcast.81, bf16[512,1024]{1,0:T(8,128)(2,1)S(1)} %collective-permute-done.2.sib_v, ...), custom_call_target="tpu_custom_call" | custom-call | tf_op jit(solution)/shard_map/row_stats/pallas_call | solution.py:255
  107.4 16.4 %all_to_all.15.in_ref = f32[32,8,256]{2,1,0:T(8,128)} all-to-all(f32[32,8,256]{2,1,0:T(8,128)S(1)} %row_stats.1), channel_id=1, replica_groups=mesh['group'=4,'x'=4,'z'=8,'core'=2] {'x','z'}, dimensions={0} | all-to-all | bytes 524288 | tf_op jit(solution)/shard_map/all_to_all | solution.py:269
  123.8 2.0 merge_stats.1
  125.7 14.4 %all_to_all.16.st_ref = f32[32,8,256]{2,1,0:T(8,128)S(1)} all-to-all(f32[32,8,256]{2,1,0:T(8,128)} %merge_stats.1), channel_id=1, replica_groups=mesh['group'=4,'x'=4,'z'=8,'core'=2] {'x','z'}, dimensions={0} | all-to-all | bytes 524288 | tf_op jit(solution)/shard_map/all_to_all | solution.py:277
  140.1 1.2 copy-done.2
  141.3 36.3 %gradients.1 = (bf16[512,2048]{1,0:T(8,128)(2,1)}, bf16[512,1024]{1,0:T(8,128)(2,1)S(1)}, bf16[512,2048]{1,0:T(8,128)(2,1)}, bf16[512,1024]{1,0:T(8,128)(2,1)S(1)}, bf16[1024,1024]{1,0:T(8,128)(2,1)}) custom-call(s32[5]{0:T(128)S(1)} %stack.7.info, bf16[512,2048]{1,0:T(8,128)(2,1)} %bitcast.75, bf16[512,1024]{1,0:T(8,128)(2,1)S(1)} %collective-permute-done.1.sib_k, ...), custom_call_target="tpu_custom_call" | custom-call | tf_op jit(solution)/shard_map/gradients/pallas_call | solution.py:279
  177.6 9.7 %all-to-all-start.2 = ((bf16[32,32,1024]{2,1,0:T(8,128)(2,1)}), bf16[32,32,1024]{2,1,0:T(8,128)(2,1)}, u32[]{:S(2)}, u32[]{:S(2)}) async-start(bf16[32,32,1024]{2,1,0:T(8,128)(2,1)} %bitcast.84), calls=%async_computation.2 | async-start | bytes 4194304 | tf_op jit(solution)/shard_map/all_to_all | solution.py:301
  187.3 4.6 %collective-permute-start.27 = (bf16[512,1024]{1,0:T(8,128)(2,1)S(1)}, bf16[512,1024]{1,0:T(8,128)(2,1)}, u32[]{:S(2)}, u32[]{:S(2)}) collective-permute-start(bf16[512,1024]{1,0:T(8,128)(2,1)S(1)} %get-tuple-element.12), channel_id=1, source_target_pairs={{0,1},{1,0},{2,3},{3,2},{4,5},{5,4},{6,7},{7,6},{8,9},{9,8},{10,11... | collective-permute-start | bytes 3145736 | tf_op jit(solution)/shard_map/ppermute | solution.py:23
  192.0 2.8 %collective-permute-done.27 = bf16[512,1024]{1,0:T(8,128)(2,1)} collective-permute-done((bf16[512,1024]{1,0:T(8,128)(2,1)S(1)}, bf16[512,1024]{1,0:T(8,128)(2,1)}, u32[]{:S(2)}, u32[]{:S(2)}) %collective-permute-start.27) | collective-permute-done | bytes 1048608 | tf_op jit(solution)/shard_map/ppermute | solution.py:23
  194.8 2.3 bitcast_dynamic-update-slice_fusion
  197.1 36.4 %all-to-all-done.2 = bf16[32,32,1024]{2,1,0:T(8,128)(2,1)} async-done(((bf16[32,32,1024]{2,1,0:T(8,128)(2,1)}), bf16[32,32,1024]{2,1,0:T(8,128)(2,1)}, u32[]{:S(2)}, u32[]{:S(2)}) %all-to-all-start.2) | async-done | bytes 2097184 | tf_op jit(solution)/shard_map/all_to_all | solution.py:301
  233.5 2.0 reduce_sum.12
  235.5 5.7 %collective-permute-start.25 = (bf16[16,1024]{1,0:T(8,128)(2,1)S(1)}, bf16[16,1024]{1,0:T(8,128)(2,1)S(1)}, u32[]{:S(2)}, u32[]{:S(2)}) collective-permute-start(bf16[16,1024]{1,0:T(8,128)(2,1)S(1)} %get-tuple-element.18), channel_id=1, source_target_pairs={{0,1},{1,0},{2,3},{3,2},{4,5},{5,4},{6,7},{7,6},{8,9},{9,8},{10,11... | collective-permute-start | bytes 98312 | tf_op jit(solution)/shard_map/ppermute | solution.py:23
  241.1 1.0 bitcast_dynamic-update-slice_fusion.1
  (72 shorter events, 10.3 us)
Async XLA Ops:
  0.6 20.0 %copy-start.4 = (bf16[1,512,2048]{2,1,0:T(8,128)(2,1)S(1)}, bf16[1,512,2048]{2,1,0:T(8,128)(2,1)}, u32[]{:S(2)}) copy-start(bf16[1,512,2048]{2,1,0:T(8,128)(2,1)} %param.8) | copy-start | bytes 6291460
  4.7 23.7 %collective-permute-start.14 = (bf16[32,1024]{1,0:T(8,128)(2,1)S(1)}, bf16[32,1024]{1,0:T(8,128)(2,1)S(1)}, u32[]{:S(2)}, u32[]{:S(2)}) collective-permute-start(bf16[32,1024]{1,0:T(8,128)(2,1)S(1)} %get-tuple-element.14), channel_id=1, source_target_pairs={{0,2},{2,4},{4,6},{6,8},{8,10},{10,12},{12,14},{14,0},{1,3},{3,5},... | collective-permute-start | bytes 196616 | tf_op jit(solution)/shard_map/ppermute | solution.py:19
  6.4 25.1 %collective-permute-start.15 = (bf16[32,1024]{1,0:T(8,128)(2,1)S(1)}, bf16[32,1024]{1,0:T(8,128)(2,1)S(1)}, u32[]{:S(2)}, u32[]{:S(2)}) collective-permute-start(bf16[32,1024]{1,0:T(8,128)(2,1)S(1)} %get-tuple-element.14), channel_id=1, source_target_pairs={{0,4},{2,6},{4,8},{6,10},{8,12},{10,14},{12,0},{14,2},{1,5},{3,7},... | collective-permute-start | bytes 196616 | tf_op jit(solution)/shard_map/ppermute | solution.py:19
  9.4 23.5 %collective-permute-start.16 = (bf16[32,1024]{1,0:T(8,128)(2,1)S(1)}, bf16[32,1024]{1,0:T(8,128)(2,1)S(1)}, u32[]{:S(2)}, u32[]{:S(2)}) collective-permute-start(bf16[32,1024]{1,0:T(8,128)(2,1)S(1)} %get-tuple-element.14), channel_id=1, source_target_pairs={{0,6},{2,8},{4,10},{6,12},{8,14},{10,0},{12,2},{14,4},{1,7},{3,9},... | collective-permute-start | bytes 196616 | tf_op jit(solution)/shard_map/ppermute | solution.py:19
  13.1 36.4 %collective-permute-start.17 = (bf16[32,1024]{1,0:T(8,128)(2,1)S(1)}, bf16[32,1024]{1,0:T(8,128)(2,1)S(1)}, u32[]{:S(2)}, u32[]{:S(2)}) collective-permute-start(bf16[32,1024]{1,0:T(8,128)(2,1)S(1)} %get-tuple-element.14), channel_id=1, source_target_pairs={{0,8},{2,10},{4,12},{6,14},{8,0},{10,2},{12,4},{14,6},{1,9},{3,11}... | collective-permute-start | bytes 196616 | tf_op jit(solution)/shard_map/ppermute | solution.py:19
  14.9 6.8 %collective-permute-start = (s32[2]{0:T(128)S(1)}, s32[2]{0:T(128)S(1)}, u32[]{:S(2)}, u32[]{:S(2)}) collective-permute-start(s32[2]{0:T(128)S(1)} %pad_add_fusion), channel_id=1, source_target_pairs={{0,1},{1,0},{2,3},{3,2},{4,5},{5,4},{6,7},{7,6},{8,9},{9,8},{10,11... | collective-permute-start | bytes 32 | tf_op jit(solution)/shard_map/ppermute | solution.py:23
  21.7 29.2 %collective-permute-start.18 = (bf16[32,1024]{1,0:T(8,128)(2,1)S(1)}, bf16[32,1024]{1,0:T(8,128)(2,1)S(1)}, u32[]{:S(2)}, u32[]{:S(2)}) collective-permute-start(bf16[32,1024]{1,0:T(8,128)(2,1)S(1)} %get-tuple-element.14), channel_id=1, source_target_pairs={{0,10},{2,12},{4,14},{6,0},{8,2},{10,4},{12,6},{14,8},{1,11},{3,13... | collective-permute-start | bytes 196616 | tf_op jit(solution)/shard_map/ppermute | solution.py:19
  28.4 23.2 %collective-permute-start.19 = (bf16[32,1024]{1,0:T(8,128)(2,1)S(1)}, bf16[32,1024]{1,0:T(8,128)(2,1)S(1)}, u32[]{:S(2)}, u32[]{:S(2)}) collective-permute-start(bf16[32,1024]{1,0:T(8,128)(2,1)S(1)} %get-tuple-element.14), channel_id=1, source_target_pairs={{0,12},{2,14},{4,0},{6,2},{8,4},{10,6},{12,8},{14,10},{1,13},{3,15... | collective-permute-start | bytes 196616 | tf_op jit(solution)/shard_map/ppermute | solution.py:19
  31.5 20.7 %collective-permute-start.20 = (bf16[32,1024]{1,0:T(8,128)(2,1)S(1)}, bf16[32,1024]{1,0:T(8,128)(2,1)S(1)}, u32[]{:S(2)}, u32[]{:S(2)}) collective-permute-start(bf16[32,1024]{1,0:T(8,128)(2,1)S(1)} %get-tuple-element.14), channel_id=1, source_target_pairs={{0,14},{2,0},{4,2},{6,4},{8,6},{10,8},{12,10},{14,12},{1,15},{3,1}... | collective-permute-start | bytes 196616 | tf_op jit(solution)/shard_map/ppermute | solution.py:19
  32.8 4.3 %collective-permute-start.3 = (bf16[32,1024]{1,0:T(8,128)(2,1)S(1)}, bf16[32,1024]{1,0:T(8,128)(2,1)S(1)}, u32[]{:S(2)}, u32[]{:S(2)}) collective-permute-start(bf16[32,1024]{1,0:T(8,128)(2,1)S(1)} %get-tuple-element.16), channel_id=1, source_target_pairs={{0,16},{16,32},{32,48},{48,0},{1,17},{17,33},{33,49},{49,1},{2,18}... | collective-permute-start | bytes 196616 | tf_op jit(solution)/shard_map/ppermute | solution.py:19
  37.1 4.6 %collective-permute-start.4 = (bf16[32,1024]{1,0:T(8,128)(2,1)S(1)}, bf16[32,1024]{1,0:T(8,128)(2,1)S(1)}, u32[]{:S(2)}, u32[]{:S(2)}) collective-permute-start(bf16[32,1024]{1,0:T(8,128)(2,1)S(1)} %get-tuple-element.16), channel_id=1, source_target_pairs={{0,32},{16,48},{32,0},{48,16},{1,33},{17,49},{33,1},{49,17},{2,34}... | collective-permute-start | bytes 196616 | tf_op jit(solution)/shard_map/ppermute | solution.py:19
  41.8 3.1 %collective-permute-start.5 = (bf16[32,1024]{1,0:T(8,128)(2,1)S(1)}, bf16[32,1024]{1,0:T(8,128)(2,1)S(1)}, u32[]{:S(2)}, u32[]{:S(2)}) collective-permute-start(bf16[32,1024]{1,0:T(8,128)(2,1)S(1)} %get-tuple-element.16), channel_id=1, source_target_pairs={{0,48},{16,0},{32,16},{48,32},{1,49},{17,1},{33,17},{49,33},{2,50}... | collective-permute-start | bytes 196616 | tf_op jit(solution)/shard_map/ppermute | solution.py:19
  44.9 42.2 %collective-permute-start.1 = (bf16[512,1024]{1,0:T(8,128)(2,1)}, bf16[512,1024]{1,0:T(8,128)(2,1)S(1)}, u32[]{:S(2)}, u32[]{:S(2)}) collective-permute-start(bf16[512,1024]{1,0:T(8,128)(2,1)} %dynamic-slice_bitcast_fusion.1), channel_id=1, source_target_pairs={{0,1},{1,0},{2,3},{3,2},{4,5},{5,4},{6,7},{7,6},{8,9},{9,8},{10,11... | collective-permute-start | bytes 3145736 | tf_op jit(solution)/shard_map/ppermute | solution.py:23
  49.5 9.6 %collective-permute-start.6 = (bf16[128,1024]{1,0:T(8,128)(2,1)S(1)}, bf16[128,1024]{1,0:T(8,128)(2,1)S(1)}, u32[]{:S(2)}, u32[]{:S(2)}) collective-permute-start(bf16[128,1024]{1,0:T(8,128)(2,1)S(1)} %bitcast.85), channel_id=1, source_target_pairs={{0,2},{2,4},{4,6},{6,8},{8,10},{10,12},{12,14},{14,0},{1,3},{3,5},... | collective-permute-start | bytes 786440 | tf_op jit(solution)/shard_map/ppermute | solution.py:19
  52.8 14.7 %collective-permute-start.21 = (bf16[256,1024]{1,0:T(8,128)(2,1)}, bf16[256,1024]{1,0:T(8,128)(2,1)S(1)}, u32[]{:S(2)}, u32[]{:S(2)}) collective-permute-start(bf16[256,1024]{1,0:T(8,128)(2,1)} %bitcast.30), channel_id=1, source_target_pairs={{0,16},{16,32},{32,48},{48,0},{1,17},{17,33},{33,49},{49,1},{2,18}... | collective-permute-start | bytes 1572872 | tf_op jit(solution)/shard_map/ppermute | solution.py:19
  52.9 15.8 %collective-permute-start.22 = (bf16[256,1024]{1,0:T(8,128)(2,1)}, bf16[256,1024]{1,0:T(8,128)(2,1)S(1)}, u32[]{:S(2)}, u32[]{:S(2)}) collective-permute-start(bf16[256,1024]{1,0:T(8,128)(2,1)} %bitcast.30), channel_id=1, source_target_pairs={{0,48},{16,0},{32,16},{48,32},{1,49},{17,1},{33,17},{49,33},{2,50}... | collective-permute-start | bytes 1572872 | tf_op jit(solution)/shard_map/ppermute | solution.py:19
  55.5 7.0 %collective-permute-start.7 = (bf16[128,1024]{1,0:T(8,128)(2,1)S(1)}, bf16[128,1024]{1,0:T(8,128)(2,1)S(1)}, u32[]{:S(2)}, u32[]{:S(2)}) collective-permute-start(bf16[128,1024]{1,0:T(8,128)(2,1)S(1)} %bitcast.86), channel_id=1, source_target_pairs={{0,14},{2,0},{4,2},{6,4},{8,6},{10,8},{12,10},{14,12},{1,15},{3,1}... | collective-permute-start | bytes 786440 | tf_op jit(solution)/shard_map/ppermute | solution.py:19
  58.8 8.7 %copy-start.5 = (bf16[512,1024]{1,0:T(8,128)(2,1)S(1)}, bf16[512,1024]{1,0:T(8,128)(2,1)}, u32[]{:S(2)}) copy-start(bf16[512,1024]{1,0:T(8,128)(2,1)} %dynamic-slice_bitcast_fusion) | copy-start | bytes 3145732
  59.1 9.7 %collective-permute-start.8 = (bf16[128,1024]{1,0:T(8,128)(2,1)S(1)}, bf16[128,1024]{1,0:T(8,128)(2,1)S(1)}, u32[]{:S(2)}, u32[]{:S(2)}) collective-permute-start(bf16[128,1024]{1,0:T(8,128)(2,1)S(1)} %collective-permute-done.6), channel_id=1, source_target_pairs={{0,2},{2,4},{4,6},{6,8},{8,10},{10,12},{12,14},{14,0},{1,3},{3,5},... | collective-permute-start | bytes 786440 | tf_op jit(solution)/shard_map/ppermute | solution.py:19
  62.5 7.0 %collective-permute-start.9 = (bf16[128,1024]{1,0:T(8,128)(2,1)S(1)}, bf16[128,1024]{1,0:T(8,128)(2,1)S(1)}, u32[]{:S(2)}, u32[]{:S(2)}) collective-permute-start(bf16[128,1024]{1,0:T(8,128)(2,1)S(1)} %collective-permute-done.7), channel_id=1, source_target_pairs={{0,14},{2,0},{4,2},{6,4},{8,6},{10,8},{12,10},{14,12},{1,15},{3,1}... | collective-permute-start | bytes 786440 | tf_op jit(solution)/shard_map/ppermute | solution.py:19
  67.5 19.6 %collective-permute-start.2 = (bf16[512,1024]{1,0:T(8,128)(2,1)S(1)}, bf16[512,1024]{1,0:T(8,128)(2,1)S(1)}, u32[]{:S(2)}, u32[]{:S(2)}) collective-permute-start(bf16[512,1024]{1,0:T(8,128)(2,1)S(1)} %copy-done.5), channel_id=1, source_target_pairs={{0,1},{1,0},{2,3},{3,2},{4,5},{5,4},{6,7},{7,6},{8,9},{9,8},{10,11... | collective-permute-start | bytes 3145736 | tf_op jit(solution)/shard_map/ppermute | solution.py:23
  68.7 11.8 %collective-permute-start.23 = (bf16[128,1024]{1,0:T(8,128)(2,1)S(1)}, bf16[128,1024]{1,0:T(8,128)(2,1)S(1)}, u32[]{:S(2)}, u32[]{:S(2)}) collective-permute-start(bf16[128,1024]{1,0:T(8,128)(2,1)S(1)} %slice.26), channel_id=1, source_target_pairs={{0,16},{16,32},{32,48},{48,0},{1,17},{17,33},{33,49},{49,1},{2,18}... | collective-permute-start | bytes 786440 | tf_op jit(solution)/shard_map/ppermute | solution.py:19
  68.8 8.4 %collective-permute-start.10 = (bf16[128,1024]{1,0:T(8,128)(2,1)S(1)}, bf16[128,1024]{1,0:T(8,128)(2,1)S(1)}, u32[]{:S(2)}, u32[]{:S(2)}) collective-permute-start(bf16[128,1024]{1,0:T(8,128)(2,1)S(1)} %collective-permute-done.8), channel_id=1, source_target_pairs={{0,2},{2,4},{4,6},{6,8},{8,10},{10,12},{12,14},{14,0},{1,3},{3,5},... | collective-permute-start | bytes 786440 | tf_op jit(solution)/shard_map/ppermute | solution.py:19
  69.5 10.8 %collective-permute-start.11 = (bf16[128,1024]{1,0:T(8,128)(2,1)S(1)}, bf16[128,1024]{1,0:T(8,128)(2,1)S(1)}, u32[]{:S(2)}, u32[]{:S(2)}) collective-permute-start(bf16[128,1024]{1,0:T(8,128)(2,1)S(1)} %collective-permute-done.9), channel_id=1, source_target_pairs={{0,14},{2,0},{4,2},{6,4},{8,6},{10,8},{12,10},{14,12},{1,15},{3,1}... | collective-permute-start | bytes 786440 | tf_op jit(solution)/shard_map/ppermute | solution.py:19
  77.2 7.6 %collective-permute-start.24 = (bf16[128,1024]{1,0:T(8,128)(2,1)S(1)}, bf16[128,1024]{1,0:T(8,128)(2,1)S(1)}, u32[]{:S(2)}, u32[]{:S(2)}) collective-permute-start(bf16[128,1024]{1,0:T(8,128)(2,1)S(1)} %slice.27), channel_id=1, source_target_pairs={{0,48},{16,0},{32,16},{48,32},{1,49},{17,1},{33,17},{49,33},{2,50}... | collective-permute-start | bytes 786440 | tf_op jit(solution)/shard_map/ppermute | solution.py:19
  80.3 5.1 %collective-permute-start.12 = (bf16[64,1024]{1,0:T(8,128)(2,1)S(1)}, bf16[64,1024]{1,0:T(8,128)(2,1)S(1)}, u32[]{:S(2)}, u32[]{:S(2)}) collective-permute-start(bf16[64,1024]{1,0:T(8,128)(2,1)S(1)} %slice.24), channel_id=1, source_target_pairs={{0,2},{2,4},{4,6},{6,8},{8,10},{10,12},{12,14},{14,0},{1,3},{3,5},... | collective-permute-start | bytes 393224 | tf_op jit(solution)/shard_map/ppermute | solution.py:19
  80.4 5.0 %collective-permute-start.13 = (bf16[64,1024]{1,0:T(8,128)(2,1)S(1)}, bf16[64,1024]{1,0:T(8,128)(2,1)S(1)}, u32[]{:S(2)}, u32[]{:S(2)}) collective-permute-start(bf16[64,1024]{1,0:T(8,128)(2,1)S(1)} %slice.25), channel_id=1, source_target_pairs={{0,14},{2,0},{4,2},{6,4},{8,6},{10,8},{12,10},{14,12},{1,15},{3,1}... | collective-permute-start | bytes 393224 | tf_op jit(solution)/shard_map/ppermute | solution.py:19
  84.8 2.2 copy-start.3
  85.5 2.4 copy-start
  87.1 20.3 %copy-start.1 = (bf16[512,1024]{1,0:T(8,128)(2,1)}, bf16[512,1024]{1,0:T(8,128)(2,1)S(1)}, u32[]{:S(2)}) copy-start(bf16[512,1024]{1,0:T(8,128)(2,1)S(1)} %collective-permute-done.2.sib_v) | copy-start | bytes 3145732
  140.1 1.2 copy-start.2
  177.6 55.9 %all-to-all-start.2 = ((bf16[32,32,1024]{2,1,0:T(8,128)(2,1)}), bf16[32,32,1024]{2,1,0:T(8,128)(2,1)}, u32[]{:S(2)}, u32[]{:S(2)}) async-start(bf16[32,32,1024]{2,1,0:T(8,128)(2,1)} %bitcast.84), calls=%async_computation.2 | async-start | bytes 4194304 | tf_op jit(solution)/shard_map/all_to_all | solution.py:301
  187.3 7.5 %collective-permute-start.27 = (bf16[512,1024]{1,0:T(8,128)(2,1)S(1)}, bf16[512,1024]{1,0:T(8,128)(2,1)}, u32[]{:S(2)}, u32[]{:S(2)}) collective-permute-start(bf16[512,1024]{1,0:T(8,128)(2,1)S(1)} %get-tuple-element.12), channel_id=1, source_target_pairs={{0,1},{1,0},{2,3},{3,2},{4,5},{5,4},{6,7},{7,6},{8,9},{9,8},{10,11... | collective-permute-start | bytes 3145736 | tf_op jit(solution)/shard_map/ppermute | solution.py:23
  191.9 49.2 %collective-permute-start.26 = (bf16[512,1024]{1,0:T(8,128)(2,1)S(1)}, bf16[512,1024]{1,0:T(8,128)(2,1)S(1)}, u32[]{:S(2)}, u32[]{:S(2)}) collective-permute-start(bf16[512,1024]{1,0:T(8,128)(2,1)S(1)} %get-tuple-element.10), channel_id=1, source_target_pairs={{0,1},{1,0},{2,3},{3,2},{4,5},{5,4},{6,7},{7,6},{8,9},{9,8},{10,11... | collective-permute-start | bytes 3145736 | tf_op jit(solution)/shard_map/ppermute | solution.py:23
  235.5 6.7 %collective-permute-start.25 = (bf16[16,1024]{1,0:T(8,128)(2,1)S(1)}, bf16[16,1024]{1,0:T(8,128)(2,1)S(1)}, u32[]{:S(2)}, u32[]{:S(2)}) collective-permute-start(bf16[16,1024]{1,0:T(8,128)(2,1)S(1)} %get-tuple-element.18), channel_id=1, source_target_pairs={{0,1},{1,0},{2,3},{3,2},{4,5},{5,4},{6,7},{7,6},{8,9},{9,8},{10,11... | collective-permute-start | bytes 98312 | tf_op jit(solution)/shard_map/ppermute | solution.py:23

commit v2 on v1

v2 whole, which is shorter than its diff:
```python
import functools

import jax
import jax.numpy as jnp
from jax import lax
from jax.experimental import pallas as pl
from jax.experimental.pallas import tpu as pltpu
from jax.sharding import Mesh
from jax.sharding import PartitionSpec as P

HDIM = 64
BKT = 64
QRY = 2
LANES = 128
F32 = jnp.float32
BF16 = jnp.bfloat16
CHIP = ("x", "z")


def swap_cores(value):
    return lax.ppermute(value, "core", [(0, 1), (1, 0)])


def repeated(value, count):
    return jnp.broadcast_to(value[None], (count,) + value.shape)


def gather_x_then_z(value, x_size):
    columns = lax.all_to_all(repeated(value, x_size), "x", 0, 0, tiled=True)
    return lax.all_gather(columns, "z", axis=0, tiled=False)


def gather_z_then_x(value, x_size, z_size):
    column = lax.all_to_all(repeated(value, z_size), "z", 0, 0, tiled=True)
    return lax.all_to_all(repeated(column, x_size), "x", 0, 0, tiled=True)


def dot_nt(a, b):
    return lax.dot_general(a, b, (((1,), (1,)), ((), ())), preferred_element_type=F32)


def dot_nn(a, b):
    return lax.dot_general(a, b, (((1,), (0,)), ((), ())), preferred_element_type=F32)


def over_chunks(buckets, step):
    fours = buckets // 4

    def body(i, carry):
        step(pl.multiple_of(i * (4 * BKT), 4 * BKT), 4 * BKT)
        return carry

    lax.fori_loop(0, fours, body, 0)
    start = fours * (4 * BKT)

    @pl.when((buckets & 2) != 0)
    def _():
        step(pl.multiple_of(start, 4 * BKT), 2 * BKT)

    @pl.when((buckets & 1) != 0)
    def _():
        step(pl.multiple_of(start + (buckets & 2) * BKT, BKT), BKT)


def load_keys(own_k, sib_k, own_v, sib_v, keys, vals):
    keys[0], keys[1] = own_k[...], sib_k[...]
    vals[0], vals[1] = own_v[...], sib_v[...]


def load_rows(owner, q_ref, g_ref, q_head, g_head):
    z_size, x_size, count, _ = q_ref.shape
    column = z_size * count
    lane = lax.broadcasted_iota(jnp.int32, (column, LANES), 1)
    for i in range(x_size // QRY):
        x = owner * (x_size // QRY) + i
        at = slice(i * column, (i + 1) * column)
        q_rows = q_ref[:, x].reshape(column, LANES)
        g_rows = g_ref[x].reshape(column, LANES)
        for h in range(2):
            mine = (lane < HDIM) if h == 0 else (lane >= HDIM)
            q_head[h, at, :] = jnp.where(mine, q_rows, jnp.zeros_like(q_rows))
            g_head[h, at, :] = jnp.where(mine, g_rows, jnp.zeros_like(g_rows))


def stats_kernel(info, own_k, sib_k, own_v, sib_v, q_ref, g_ref, out_ref,
                 keys, vals, q_head, g_head, top, total, dotted):
    rows = q_head.shape[1]
    load_keys(own_k, sib_k, own_v, sib_v, keys, vals)

    def passage(p, carry):
        load_rows(info[1 + p], q_ref, g_ref, q_head, g_head)
        top[...] = jnp.full(top.shape, -jnp.inf, F32)
        total[...] = jnp.zeros(total.shape, F32)
        dotted[...] = jnp.zeros(dotted.shape, F32)

        def step(start, count):
            k_part = keys[p, pl.ds(start, count), :]
            v_part = vals[p, pl.ds(start, count), :]
            for h in range(2):
                scores = dot_nt(k_part, q_head[h]).reshape(count // 8, 8, rows)
                upstream = dot_nt(v_part, g_head[h]).reshape(count // 8, 8, rows)
                old = top[h]
                new = jnp.maximum(old, jnp.max(scores, axis=0))
                weights = jnp.exp(scores - new[None])
                factor = jnp.exp(old - new)
                top[h] = new
                total[h] = total[h] * factor + jnp.sum(weights, axis=0)
                dotted[h] = dotted[h] * factor + jnp.sum(weights * upstream, axis=0)

        over_chunks(info[3 + p], step)
        half = rows // 2
        for h in range(2):
            peak = jnp.max(top[h], axis=0, keepdims=True)
            factor = jnp.exp(top[h] - peak)
            stats = (
                peak,
                jnp.sum(total[h] * factor, axis=0, keepdims=True),
                jnp.sum(dotted[h] * factor, axis=0, keepdims=True),
                jnp.full((1, rows), info[1 + p].astype(F32)),
            )
            for s in range(2):
                for t, stat in enumerate(stats):
                    out_ref[2 * h + s, pl.ds(2 * t + p, 1), :] = stat[:, s * half:(s + 1) * half]
        return carry

    lax.fori_loop(0, 2, passage, 0)


def merge_kernel(in_ref, out_ref):
    chips = in_ref.shape[0]
    merged = []
    tops = [in_ref[:, t, :] for t in range(2)]
    sums = [in_ref[:, 2 + t, :] for t in range(2)]
    dots = [in_ref[:, 4 + t, :] for t in range(2)]
    owners = [in_ref[:, 6 + t, :] for t in range(2)]
    for query in range(QRY):
        held = [jnp.where(owners[t] == query, tops[t], -jnp.inf) for t in range(2)]
        peak = jnp.max(jnp.maximum(held[0], held[1]), axis=0, keepdims=True)
        factors = [jnp.exp(held[t] - peak) for t in range(2)]
        total = jnp.sum(sums[0] * factors[0] + sums[1] * factors[1], axis=0, keepdims=True)
        dotted = jnp.sum(dots[0] * factors[0] + dots[1] * factors[1], axis=0, keepdims=True)
        merged.append((peak + jnp.log(total), dotted / total))
    table = jnp.concatenate(
        [merged[0][0], merged[1][0], merged[0][1], merged[1][1]]
        + [jnp.zeros_like(merged[0][0])] * 4, axis=0
    )
    out_ref[...] = jnp.broadcast_to(table[None], out_ref.shape)


def grads_kernel(info, own_k, sib_k, own_v, sib_v, q_ref, g_ref, st_ref, *rest):
    (own_dk, sib_dk, own_dv, sib_dv, dq_ref,
     keys, vals, q_head, g_head, dkeys, dvals, turned, dq_sum) = rest[-13:]
    rows = q_head.shape[1]
    load_keys(own_k, sib_k, own_v, sib_v, keys, vals)
    dkeys[...] = jnp.zeros(dkeys.shape, BF16)
    dvals[...] = jnp.zeros(dvals.shape, BF16)
    dq_sum[...] = jnp.zeros(dq_sum.shape, F32)

    def passage(p, carry):
        owner = info[1 + p]
        load_rows(owner, q_ref, g_ref, q_head, g_head)
        turned[...] = jnp.zeros(turned.shape, F32)

        def row_stat(h, t):
            return jnp.concatenate(
                [st_ref[2 * h + s, pl.ds(2 * t + owner, 1), :] for s in range(2)], axis=1
            )

        def step(start, count):
            at = pl.ds(start, count)
            k_part, v_part = keys[p, at, :], vals[p, at, :]
            k_turned = k_part.T
            dk_part = dv_part = None
            for h in range(2):
                probs = jnp.exp(dot_nt(k_part, q_head[h]) - row_stat(h, 0))
                dscore = (probs * (dot_nt(v_part, g_head[h]) - row_stat(h, 1))).astype(BF16)
                dv_term = dot_nn(probs.astype(BF16), g_head[h])
                dk_term = dot_nn(dscore, q_head[h])
                dv_part = dv_term if h == 0 else dv_part + dv_term
                dk_part = dk_term if h == 0 else dk_part + dk_term
                own = slice(h * HDIM, (h + 1) * HDIM)
                turned[own, :] += dot_nn(k_turned[own, :], dscore)
            dkeys[p, at, :] = dk_part.astype(BF16)
            dvals[p, at, :] = dv_part.astype(BF16)

        over_chunks(info[3 + p], step)
        at = pl.ds(pl.multiple_of(owner * rows, rows), rows)
        dq_sum[at, :] += turned[...].T
        return carry

    lax.fori_loop(0, 2, passage, 0)
    own_dk[...], sib_dk[...] = dkeys[0], dkeys[1]
    own_dv[...], sib_dv[...] = dvals[0], dvals[1]
    dq_ref[...] = dq_sum[...].astype(BF16)


def blocks(slots, pairs, q_shape, rows, first):
    z_size, x_size, count, _ = q_shape
    own = pl.BlockSpec((slots, LANES), lambda i, info: (0, info[0] * pairs + first + i))
    sib = pl.BlockSpec((slots, LANES), lambda i, info: (0, first + i))
    q_block = pl.BlockSpec((z_size, x_size, count, LANES), lambda i, info: (0, 0, 0, first + i))
    g_block = pl.BlockSpec((x_size, z_size, count, LANES), lambda i, info: (0, 0, 0, first + i))
    stat = pl.BlockSpec((4, 8, rows // 2), lambda i, info: (first + i, 0, 0))
    return own, [own, sib, own, sib, q_block, g_block], stat


def sizes(operands):
    info, keys, sib_k, values, sib_v, whole_q, whole_g = operands
    slots, half = sib_k.shape
    all_rows = whole_q.shape[0] * whole_q.shape[1] * whole_q.shape[2]
    return slots, half, half // LANES, all_rows, all_rows // QRY


LIMIT = pltpu.CompilerParams(
    dimension_semantics=("arbitrary",), vmem_limit_bytes=48 * 1024 * 1024
)


def key_scratch(slots):
    return [pltpu.VMEM((2, slots, LANES), BF16)] * 2


def row_stats(operands):
    slots, half, pairs, all_rows, rows = sizes(operands)
    own, in_blocks, stat = blocks(slots, pairs, operands[5].shape, rows, 0)
    return pl.pallas_call(
        stats_kernel,
        grid_spec=pltpu.PrefetchScalarGridSpec(
            num_scalar_prefetch=1,
            grid=(pairs,),
            in_specs=in_blocks,
            out_specs=stat,
            scratch_shapes=key_scratch(slots)
            + [pltpu.VMEM((2, rows, LANES), BF16)] * 2
            + [pltpu.VMEM((2, 8, rows), F32)] * 3,
        ),
        out_shape=jax.ShapeDtypeStruct((4 * pairs, 8, rows // 2), F32),
        compiler_params=LIMIT,
        cost_estimate=pl.CostEstimate(
            flops=4 * slots * rows * half * 2, bytes_accessed=10 << 20,
            transcendentals=slots * rows * half // HDIM * 2,
        ),
        name="row_stats",
    )(*operands)


def merge_stats(stats):
    return pl.pallas_call(
        merge_kernel,
        out_shape=jax.ShapeDtypeStruct(stats.shape, F32),
        in_specs=[pl.BlockSpec(memory_space=pltpu.VMEM)],
        out_specs=pl.BlockSpec(memory_space=pltpu.VMEM),
        name="merge_stats",
    )(stats)


def gradients(operands, stats, first, count, begun):
    slots, half, pairs, all_rows, rows = sizes(operands)
    own, in_blocks, stat = blocks(slots, pairs, operands[5].shape, rows, first)
    sib = pl.BlockSpec((slots, LANES), lambda i, info: (0, i))
    whole = jax.ShapeDtypeStruct((slots, 2 * half), BF16)
    part = jax.ShapeDtypeStruct((slots, count * LANES), BF16)
    given = list(begun)
    return pl.pallas_call(
        grads_kernel,
        grid_spec=pltpu.PrefetchScalarGridSpec(
            num_scalar_prefetch=1,
            grid=(count,),
            in_specs=in_blocks + [stat] + [pl.BlockSpec(memory_space=pl.ANY)] * len(given),
            out_specs=[own, sib, own, sib, pl.BlockSpec((all_rows, LANES), lambda i, info: (0, i))],
            scratch_shapes=key_scratch(slots)
            + [pltpu.VMEM((2, rows, LANES), BF16)] * 2
            + key_scratch(slots)
            + [pltpu.VMEM((LANES, rows), F32), pltpu.VMEM((all_rows, LANES), F32)],
        ),
        out_shape=[whole, part, whole, part,
                   jax.ShapeDtypeStruct((all_rows, count * LANES), BF16)],
        input_output_aliases={8: 0, 9: 2} if given else {},
        compiler_params=LIMIT,
        cost_estimate=pl.CostEstimate(
            flops=10 * slots * rows * count * LANES * 2, bytes_accessed=8 << 20,
            transcendentals=slots * rows * count * 4,
        ),
        name="gradients",
    )(*operands, stats, *given)


PARTS = 2


def per_device(x_size, z_size, queries, keys, values, grad_out, lengths, slot_query):
    chips = x_size * z_size
    core = lax.axis_index("core")
    width = keys.shape[2]
    half = width // 2
    keys, values = keys[0], values[0]

    mine = jnp.concatenate([slot_query, lengths])
    theirs = swap_cores(mine)
    info = jnp.stack([core, mine[0], theirs[0], mine[1], theirs[1]]).astype(jnp.int32)

    def features(value, of_core):
        return lax.dynamic_slice_in_dim(value, of_core * half, half, value.ndim - 1)

    both = lax.all_gather(jnp.stack([queries, grad_out]), "core", axis=1, tiled=True)
    both = features(both, core)
    whole_q = gather_x_then_z(both[0], x_size)
    whole_g = gather_z_then_x(both[1], x_size, z_size)
    sib_k = swap_cores(features(keys, 1 - core))
    sib_v = swap_cores(features(values, 1 - core))
    operands = (info, keys, sib_k, values, sib_v, whole_q, whole_g)
    slots, half, pairs, all_rows, rows = sizes(operands)

    stats = lax.all_to_all(row_stats(operands), CHIP, 0, 0, tiled=True)
    stats = lax.all_to_all(merge_stats(stats), CHIP, 0, 0, tiled=True)

    count = pairs // PARTS
    span = count * LANES
    held = all_rows // chips
    own_rows = held // 2
    begun, sibs, sums = [], [], []
    for part in range(PARTS):
        own_dk, sib_dk, own_dv, sib_dv, dq = gradients(operands, stats, part * count, count, begun)
        begun = [own_dk, own_dv]
        sibs.append((swap_cores(sib_dk), swap_cores(sib_dv)))
        terms = lax.all_to_all(dq.reshape(chips, held, span), CHIP, 0, 0, tiled=True)
        sums.append(jnp.sum(terms.astype(F32), axis=0).astype(BF16))

    own_dk, own_dv = begun
    for part, (sib_dk, sib_dv) in enumerate(sibs):
        at = (1 - core) * half + part * span
        own_dk = lax.dynamic_update_slice_in_dim(own_dk, sib_dk, at, 1)
        own_dv = lax.dynamic_update_slice_in_dim(own_dv, sib_dv, at, 1)

    summed = jnp.concatenate(sums, axis=1)
    kept = lax.dynamic_slice_in_dim(summed, core * own_rows, own_rows, 0)
    given = swap_cores(lax.dynamic_slice_in_dim(summed, (1 - core) * own_rows, own_rows, 0))
    grad_queries = jnp.where(
        core == 0, jnp.concatenate([kept, given], 1), jnp.concatenate([given, kept], 1)
    )
    return grad_queries, own_dk[None], own_dv[None]


def solution(mesh):
    groups = mesh.devices.shape[0]
    x_size, z_size = 4, 8
    fine = Mesh(
        mesh.devices.reshape(groups, x_size, z_size, 2), ("group", "x", "z", "core")
    )
    at = ("group", "x", "z", "core")
    return jax.shard_map(
        functools.partial(per_device, x_size, z_size),
        mesh=fine,
        in_specs=(P(at, None), P(at, None, None), P(at, None, None), P(at, None), P(at), P(at)),
        out_specs=(P(at, None), P(at, None, None), P(at, None, None)),
        check_vma=False,
    )
```

time: 243 us -> 219 us (0.901)
  the two profiles are of different devices: /device:TPU:17 before, /device:TPU:25 now
where the time goes in v2:
time: 219 us
  blocking collectives  74.7 us (34%)
  starting transfers between devices  54.2 us (25%)
  Pallas kernels  44.6 us (20%)
  between operations  15.5 us (7%)
  local copies, waits for them, and re-layouts  13.3 us (6%)
  waiting for transfers between devices  13.3 us (6%)
  other arithmetic  3.16 us (1%)
    pallas_call x2, Pallas kernels, gradients(): pl.pallas_call(grads_kernel, grid_spec=pltpu.PrefetchScalarGridSpec(num_s...  28.7 us
    ppermute x8, starting transfers between devices, swap_cores(): return lax.ppermute(value, 'core', [(0, 1), (1, 0)])  27.5 us
    all_to_all x1, blocking collectives, gather_z_then_x(): column = lax.all_to_all(repeated(value, z_size), 'z', 0, 0, tiled=True)  24.4 us
    all_to_all x1, blocking collectives, per_device(): stats = lax.all_to_all(row_stats(operands), CHIP, 0, 0, tiled=True)  24.2 us
    all_to_all x2, starting transfers between devices, per_device(): lax.all_to_all(dq.reshape(chips, held, span), CHIP, 0, 0, tiled=True)  22.1 us
    all_to_all x1, blocking collectives, per_device(): stats = lax.all_to_all(merge_stats(stats), CHIP, 0, 0, tiled=True)  14.1 us
    pallas_call x1, Pallas kernels, row_stats(): pl.pallas_call(stats_kernel, grid_spec=pltpu.PrefetchScalarGridSpec(num_s...  13.9 us
    all_to_all x1, blocking collectives, gather_x_then_z(): columns = lax.all_to_all(repeated(value, x_size), 'x', 0, 0, tiled=True)  9.74 us
  transfers between devices with their start and end apart: 12, of which 5 were waited for; matrix products, arithmetic and copies ran while one was open for 7% of the time, Pallas kernels for 7%

profile of v2, /device:TPU:25, one launch (start us, length us, event | category | flops | bytes accessed | tf_op | source)
XLA Modules:
  0.0 218.8 jit_solution(2252569875649867381)
XLA Ops:
  7.2 0.0 all-gather.3.cloned.1.call-start
  7.2 0.9 pad_maximum_fusion
  8.1 2.3 %all_gather.9 = bf16[2,32,2048]{2,1,0:T(8,128)(2,1)S(1)} all-gather(bf16[2,16,2048]{2,1,0:T(8,128)(2,1)S(1)} %pad_maximum_fusion), channel_id=1, replica_groups=mesh['group'=4,'x'=4,'z'=8,'core'=2] {'core'}, dimensions={1}, use_global_device_ids=true | all-gather | bytes 393216 | tf_op jit(solution)/shard_map/all_gather | solution.py:305
  10.5 9.7 %all_to_all.35 = bf16[4,32,1024]{2,1,0:T(8,128)(2,1)} all-to-all(bf16[4,32,1024]{2,1,0:T(8,128)(2,1)S(1)} %broadcast_in_dim.35), channel_id=1, replica_groups=mesh['group'=4,'x'=4,'z'=8,'core'=2] {'x'}, dimensions={0} | all-to-all | bytes 524288 | tf_op jit(solution)/shard_map/all_to_all | solution.py:29
  20.2 0.0 all-gather.3.cloned.1.call-update
  20.2 0.1 broadcast_in_dim.37
  20.3 24.4 %all_to_all.36 = bf16[8,32,1024]{2,1,0:T(8,128)(2,1)S(1)} all-to-all(bf16[8,32,1024]{2,1,0:T(8,128)(2,1)S(1)} %broadcast_in_dim.37), channel_id=1, replica_groups=mesh['group'=4,'x'=4,'z'=8,'core'=2] {'z'}, dimensions={0} | all-to-all | bytes 1048576 | tf_op jit(solution)/shard_map/all_to_all | solution.py:34
  44.6 1.6 broadcast_in_dim.38
  46.2 4.6 %all-to-all-start.2 = ((bf16[4,8,32,1024]{3,2,1,0:T(8,128)(2,1)}), bf16[4,8,32,1024]{3,2,1,0:T(8,128)(2,1)}, u32[]{:S(2)}, u32[]{:S(2)}) async-start(bf16[4,8,32,1024]{3,2,1,0:T(8,128)(2,1)} %broadcast_in_dim.38), calls=%async_computation.2 | async-start | bytes 4194304 | tf_op jit(solution)/shard_map/all_to_all | solution.py:35
  50.9 0.0 copy-start.3
  50.9 1.1 dynamic-slice_bitcast_fusion.1
  51.9 6.7 %collective-permute-start.1 = (bf16[512,1024]{1,0:T(8,128)(2,1)}, bf16[512,1024]{1,0:T(8,128)(2,1)S(1)}, u32[]{:S(2)}, u32[]{:S(2)}) collective-permute-start(bf16[512,1024]{1,0:T(8,128)(2,1)} %dynamic-slice_bitcast_fusion.1), channel_id=1, source_target_pairs={{0,1},{1,0},{2,3},{3,2},{4,5},{5,4},{6,7},{7,6},{8,9},{9,8},{10,11... | collective-permute-start | bytes 3145736 | tf_op jit(solution)/shard_map/ppermute | solution.py:21
  58.6 1.1 dynamic-slice_bitcast_fusion
  59.7 0.9 collective-permute-start.2
  61.9 0.1 pad_add_fusion
  62.0 0.0 collective-permute-start
  62.0 1.1 collective-permute-done
  63.1 0.6 fusion.2
  63.7 1.4 stack.16.info
  65.1 0.0 collective-permute-done.1.sib_k
  65.1 0.0 collective-permute-done.2.sib_v
  65.1 5.2 %all-to-all-done.2.g_ref = bf16[4,8,32,1024]{3,2,1,0:T(8,128)(2,1)} async-done(((bf16[4,8,32,1024]{3,2,1,0:T(8,128)(2,1)}), bf16[4,8,32,1024]{3,2,1,0:T(8,128)(2,1)}, u32[]{:S(2)}, u32[]{:S(2)}) %all-to-all-start.2) | async-done | bytes 2097184 | tf_op jit(solution)/shard_map/all_to_all | solution.py:35
  70.3 13.9 %row_stats.1 = f32[32,8,256]{2,1,0:T(8,128)S(1)} custom-call(s32[5]{0:T(128)S(1)} %stack.16.info, bf16[512,2048]{1,0:T(8,128)(2,1)S(1)} %bitcast.28, bf16[512,1024]{1,0:T(8,128)(2,1)S(1)} %collective-permute-done.1.sib_k, bf16[512,2048]{1,0:T(8,128)(2,1)} %bitcast.29, bf16[512,1024]{1,0:T(8,128)(2,1)} %collective-permute-done.2.sib_v, ...), custom_call_target="tpu_custom_call" | custom-call | flops 2147483648 | bytes 10485760 | tf_op jit(solution)/shard_map/row_stats/pallas_call | solution.py:226
  84.3 24.2 %all_to_all.37.in_ref = f32[32,8,256]{2,1,0:T(8,128)} all-to-all(f32[32,8,256]{2,1,0:T(8,128)S(1)} %row_stats.1), channel_id=1, replica_groups=mesh['group'=4,'x'=4,'z'=8,'core'=2] {'x','z'}, dimensions={0} | all-to-all | bytes 524288 | tf_op jit(solution)/shard_map/all_to_all | solution.py:314
  108.5 2.0 merge_stats.1
  110.5 14.1 %all_to_all.38.st_ref = f32[32,8,256]{2,1,0:T(8,128)S(1)} all-to-all(f32[32,8,256]{2,1,0:T(8,128)} %merge_stats.1), channel_id=1, replica_groups=mesh['group'=4,'x'=4,'z'=8,'core'=2] {'x','z'}, dimensions={0} | all-to-all | bytes 524288 | tf_op jit(solution)/shard_map/all_to_all | solution.py:315
  124.6 14.3 %gradients.2 = (bf16[512,2048]{1,0:T(8,128)(2,1)}, bf16[512,512]{1,0:T(8,128)(2,1)S(1)}, bf16[512,2048]{1,0:T(8,128)(2,1)}, bf16[512,512]{1,0:T(8,128)(2,1)S(1)}, bf16[1024,512]{1,0:T(8,128)(2,1)}) custom-call(s32[5]{0:T(128)S(1)} %stack.16.info, bf16[512,2048]{1,0:T(8,128)(2,1)} %bitcast.26, bf16[512,1024]{1,0:T(8,128)(2,1)S(1)} %collective-permute-done.1.sib_k, ...), custom_call_target="tpu_custom_call" | custom-call | flops 2684354560 | bytes 8388608 | tf_op jit(solution)/shard_map/gradients/pallas_call | solution.py:264
  138.9 11.3 %all-to-all-start.5 = ((bf16[32,32,512]{2,1,0:T(8,128)(2,1)}), bf16[32,32,512]{2,1,0:T(8,128)(2,1)}, u32[]{:S(2)}, u32[]{:S(2)}) async-start(bf16[32,32,512]{2,1,0:T(8,128)(2,1)} %bitcast.10), calls=%async_computation.5 | async-start | bytes 2097152 | tf_op jit(solution)/shard_map/all_to_all | solution.py:326
  150.2 14.4 %gradients.3 = (bf16[512,2048]{1,0:T(8,128)(2,1)}, bf16[512,512]{1,0:T(8,128)(2,1)S(1)}, bf16[512,2048]{1,0:T(8,128)(2,1)}, bf16[512,512]{1,0:T(8,128)(2,1)S(1)}, bf16[1024,512]{1,0:T(8,128)(2,1)}) custom-call(s32[5]{0:T(128)S(1)} %stack.16.info, bf16[512,2048]{1,0:T(8,128)(2,1)} %bitcast.27, ...), custom_call_target="tpu_custom_call", output_to_operand_aliasing={{0}: (8, {}), {2}: (9, {})} | custom-call | flops 2684354560 | bytes 8388608 | tf_op jit(solution)/shard_map/gradients/pallas_call | solution.py:264
  164.6 4.5 %all-to-all-done.5 = bf16[32,32,512]{2,1,0:T(8,128)(2,1)} async-done(((bf16[32,32,512]{2,1,0:T(8,128)(2,1)}), bf16[32,32,512]{2,1,0:T(8,128)(2,1)}, u32[]{:S(2)}, u32[]{:S(2)}) %all-to-all-start.5) | async-done | bytes 1048608 | tf_op jit(solution)/shard_map/all_to_all | solution.py:326
  169.1 10.8 %all-to-all-start.6 = ((bf16[32,32,512]{2,1,0:T(8,128)(2,1)}), bf16[32,32,512]{2,1,0:T(8,128)(2,1)S(1)}, u32[]{:S(2)}, u32[]{:S(2)}) async-start(bf16[32,32,512]{2,1,0:T(8,128)(2,1)} %bitcast.11), calls=%async_computation.6 | async-start | bytes 2097152 | tf_op jit(solution)/shard_map/all_to_all | solution.py:326
  179.9 8.1 %collective-permute-start.4 = (bf16[512,512]{1,0:T(8,128)(2,1)S(1)}, bf16[512,512]{1,0:T(8,128)(2,1)}, u32[]{:S(2)}, u32[]{:S(2)}) collective-permute-start(bf16[512,512]{1,0:T(8,128)(2,1)S(1)} %copy-done.2), channel_id=1, source_target_pairs={{0,1},{1,0},{2,3},{3,2},{4,5},{5,4},{6,7},{7,6},{8,9},{9,8},{10,11... | collective-permute-start | bytes 1572872 | tf_op jit(solution)/shard_map/ppermute | solution.py:21
  188.0 0.1 collective-permute-start.6
  188.1 0.4 collective-permute-start.5
  188.5 0.1 collective-permute-start.7
  188.6 1.1 collective-permute-done.4
  189.7 1.9 bitcast_dynamic-update-slice_fusion.3
  191.6 0.0 collective-permute-done.6
  191.6 1.9 bitcast_dynamic-update-slice_fusion.1
  193.4 0.0 collective-permute-done.5
  193.4 1.9 bitcast_dynamic-update-slice_fusion.2
  195.3 1.4 reduce_sum.24
  196.7 1.3 all-to-all-done.6
  198.0 0.2 reduce_sum.25
  198.2 11.2 %collective-permute-start.3 = (bf16[16,1024]{1,0:T(8,128)(2,1)S(1)}, bf16[16,1024]{1,0:T(8,128)(2,1)S(1)}, u32[]{:S(2)}, u32[]{:S(2)}) collective-permute-start(bf16[16,1024]{1,0:T(8,128)(2,1)S(1)} %get-tuple-element.26), channel_id=1, source_target_pairs={{0,1},{1,0},{2,3},{3,2},{4,5},{5,4},{6,7},{7,6},{8,9},{9,8},{10,11... | collective-permute-start | bytes 98312 | tf_op jit(solution)/shard_map/ppermute | solution.py:21
  209.4 1.9 bitcast_dynamic-update-slice_fusion
  211.3 0.0 collective-permute-done.3
  211.3 0.6 maximum_select_fusion
  (12 shorter events, 0.1 us)
Async XLA Ops:
  7.2 63.1 %all-gather.3.cloned.1.call-start = ((), (), s32[]{:S(2)}) async-start(), calls=%async_computation.7 | async-start | bytes 2359296 | tf_op jit(solution)/shard_map/all_gather | solution.py:30
  46.2 4.6 %copy-start = (bf16[1,512,2048]{2,1,0:T(8,128)(2,1)S(1)}, bf16[1,512,2048]{2,1,0:T(8,128)(2,1)}, u32[]{:S(2)}) copy-start(bf16[1,512,2048]{2,1,0:T(8,128)(2,1)} %param.7) | copy-start | bytes 6291460
  46.2 24.1 %all-to-all-start.2 = ((bf16[4,8,32,1024]{3,2,1,0:T(8,128)(2,1)}), bf16[4,8,32,1024]{3,2,1,0:T(8,128)(2,1)}, u32[]{:S(2)}, u32[]{:S(2)}) async-start(bf16[4,8,32,1024]{3,2,1,0:T(8,128)(2,1)} %broadcast_in_dim.38), calls=%async_computation.2 | async-start | bytes 4194304 | tf_op jit(solution)/shard_map/all_to_all | solution.py:35
  50.9 7.7 %copy-start.3 = (bf16[1,512,2048]{2,1,0:T(8,128)(2,1)S(1)}, bf16[1,512,2048]{2,1,0:T(8,128)(2,1)}, u32[]{:S(2)}) copy-start(bf16[1,512,2048]{2,1,0:T(8,128)(2,1)} %param.8) | copy-start | bytes 6291460
  51.9 13.2 %collective-permute-start.1 = (bf16[512,1024]{1,0:T(8,128)(2,1)}, bf16[512,1024]{1,0:T(8,128)(2,1)S(1)}, u32[]{:S(2)}, u32[]{:S(2)}) collective-permute-start(bf16[512,1024]{1,0:T(8,128)(2,1)} %dynamic-slice_bitcast_fusion.1), channel_id=1, source_target_pairs={{0,1},{1,0},{2,3},{3,2},{4,5},{5,4},{6,7},{7,6},{8,9},{9,8},{10,11... | collective-permute-start | bytes 3145736 | tf_op jit(solution)/shard_map/ppermute | solution.py:21
  59.7 5.4 %collective-permute-start.2 = (bf16[512,1024]{1,0:T(8,128)(2,1)}, bf16[512,1024]{1,0:T(8,128)(2,1)}, u32[]{:S(2)}, u32[]{:S(2)}) collective-permute-start(bf16[512,1024]{1,0:T(8,128)(2,1)} %dynamic-slice_bitcast_fusion), channel_id=1, source_target_pairs={{0,1},{1,0},{2,3},{3,2},{4,5},{5,4},{6,7},{7,6},{8,9},{9,8},{10,11... | collective-permute-start | bytes 3145736 | tf_op jit(solution)/shard_map/ppermute | solution.py:21
  62.0 1.1 collective-permute-start
  138.9 11.3 %copy-start.1 = (bf16[512,512]{1,0:T(8,128)(2,1)}, bf16[512,512]{1,0:T(8,128)(2,1)S(1)}, u32[]{:S(2)}) copy-start(bf16[512,512]{1,0:T(8,128)(2,1)S(1)} %get-tuple-element.18) | copy-start | bytes 1572868
  138.9 30.2 %all-to-all-start.5 = ((bf16[32,32,512]{2,1,0:T(8,128)(2,1)}), bf16[32,32,512]{2,1,0:T(8,128)(2,1)}, u32[]{:S(2)}, u32[]{:S(2)}) async-start(bf16[32,32,512]{2,1,0:T(8,128)(2,1)} %bitcast.10), calls=%async_computation.5 | async-start | bytes 2097152 | tf_op jit(solution)/shard_map/all_to_all | solution.py:326
  164.6 15.4 %copy-start.2 = (bf16[512,512]{1,0:T(8,128)(2,1)S(1)}, bf16[512,512]{1,0:T(8,128)(2,1)}, u32[]{:S(2)}) copy-start(bf16[512,512]{1,0:T(8,128)(2,1)} %copy-done.1) | copy-start | bytes 1572868
  169.1 28.9 %all-to-all-start.6 = ((bf16[32,32,512]{2,1,0:T(8,128)(2,1)}), bf16[32,32,512]{2,1,0:T(8,128)(2,1)S(1)}, u32[]{:S(2)}, u32[]{:S(2)}) async-start(bf16[32,32,512]{2,1,0:T(8,128)(2,1)} %bitcast.11), calls=%async_computation.6 | async-start | bytes 2097152 | tf_op jit(solution)/shard_map/all_to_all | solution.py:326
  179.9 9.8 %collective-permute-start.4 = (bf16[512,512]{1,0:T(8,128)(2,1)S(1)}, bf16[512,512]{1,0:T(8,128)(2,1)}, u32[]{:S(2)}, u32[]{:S(2)}) collective-permute-start(bf16[512,512]{1,0:T(8,128)(2,1)S(1)} %copy-done.2), channel_id=1, source_target_pairs={{0,1},{1,0},{2,3},{3,2},{4,5},{5,4},{6,7},{7,6},{8,9},{9,8},{10,11... | collective-permute-start | bytes 1572872 | tf_op jit(solution)/shard_map/ppermute | solution.py:21
  188.0 3.5 %collective-permute-start.6 = (bf16[512,512]{1,0:T(8,128)(2,1)S(1)}, bf16[512,512]{1,0:T(8,128)(2,1)}, u32[]{:S(2)}, u32[]{:S(2)}) collective-permute-start(bf16[512,512]{1,0:T(8,128)(2,1)S(1)} %get-tuple-element.21), channel_id=1, source_target_pairs={{0,1},{1,0},{2,3},{3,2},{4,5},{5,4},{6,7},{7,6},{8,9},{9,8},{10,11... | collective-permute-start | bytes 1572872 | tf_op jit(solution)/shard_map/ppermute | solution.py:21
  188.1 5.3 %collective-permute-start.5 = (bf16[512,512]{1,0:T(8,128)(2,1)S(1)}, bf16[512,512]{1,0:T(8,128)(2,1)}, u32[]{:S(2)}, u32[]{:S(2)}) collective-permute-start(bf16[512,512]{1,0:T(8,128)(2,1)S(1)} %get-tuple-element.19), channel_id=1, source_target_pairs={{0,1},{1,0},{2,3},{3,2},{4,5},{5,4},{6,7},{7,6},{8,9},{9,8},{10,11... | collective-permute-start | bytes 1572872 | tf_op jit(solution)/shard_map/ppermute | solution.py:21
  188.5 20.9 %collective-permute-start.7 = (bf16[512,512]{1,0:T(8,128)(2,1)S(1)}, bf16[512,512]{1,0:T(8,128)(2,1)}, u32[]{:S(2)}, u32[]{:S(2)}) collective-permute-start(bf16[512,512]{1,0:T(8,128)(2,1)S(1)} %get-tuple-element.22), channel_id=1, source_target_pairs={{0,1},{1,0},{2,3},{3,2},{4,5},{5,4},{6,7},{7,6},{8,9},{9,8},{10,11... | collective-permute-start | bytes 1572872 | tf_op jit(solution)/shard_map/ppermute | solution.py:21
  198.2 13.1 %collective-permute-start.3 = (bf16[16,1024]{1,0:T(8,128)(2,1)S(1)}, bf16[16,1024]{1,0:T(8,128)(2,1)S(1)}, u32[]{:S(2)}, u32[]{:S(2)}) collective-permute-start(bf16[16,1024]{1,0:T(8,128)(2,1)S(1)} %get-tuple-element.26), channel_id=1, source_target_pairs={{0,1},{1,0},{2,3},{3,2},{4,5},{5,4},{6,7},{7,6},{8,9},{9,8},{10,11... | collective-permute-start | bytes 98312 | tf_op jit(solution)/shard_map/ppermute | solution.py:21
Sparse Core Ops, SparseCore 0:
  20.3 45.5 all-gather.2

commit v3 on v2

v3 whole, which is shorter than its diff:
```python
import functools

import jax
import jax.numpy as jnp
from jax import lax
from jax.experimental import pallas as pl
from jax.experimental.pallas import tpu as pltpu
from jax.sharding import Mesh
from jax.sharding import PartitionSpec as P

HDIM = 64
BKT = 64
QRY = 2
LANES = 128
F32 = jnp.float32
BF16 = jnp.bfloat16
CHIP = ("x", "z")


def swap_cores(value):
    return lax.ppermute(value, "core", [(0, 1), (1, 0)])


def repeated(value, count):
    return jnp.broadcast_to(value[None], (count,) + value.shape)


def gather_x_then_z(value, x_size):
    columns = lax.all_to_all(repeated(value, x_size), "x", 0, 0, tiled=True)
    return lax.all_gather(columns, "z", axis=0, tiled=False)


def gather_z_then_x(value, x_size, z_size):
    column = lax.all_to_all(repeated(value, z_size), "z", 0, 0, tiled=True)
    return lax.all_to_all(repeated(column, x_size), "x", 0, 0, tiled=True)


def dot_nt(a, b):
    return lax.dot_general(a, b, (((1,), (1,)), ((), ())), preferred_element_type=F32)


def dot_nn(a, b):
    return lax.dot_general(a, b, (((1,), (0,)), ((), ())), preferred_element_type=F32)


def by_length(buckets, step):
    for most in range(2, 9, 2):

        @pl.when((buckets == most) | (buckets == most - 1))
        def _():
            step(most * BKT, buckets == most)


def masked(scores, tail_used):
    cut = scores.shape[0] - BKT
    tail = jnp.where(tail_used, scores[cut:], -jnp.inf)
    return jnp.concatenate([scores[:cut], tail], axis=0)


def load_keys(own_k, sib_k, own_v, sib_v, keys, vals):
    keys[0], keys[1] = own_k[...], sib_k[...]
    vals[0], vals[1] = own_v[...], sib_v[...]


def load_rows(z_first, owner, q_ref, g_ref, q_head, g_head):
    z_size, x_size = q_ref.shape[:2] if z_first else q_ref.shape[1::-1]
    column = z_size * q_ref.shape[3]
    lane = lax.broadcasted_iota(jnp.int32, (column, LANES), 1)
    for i in range(x_size // QRY):
        x = owner * (x_size // QRY) + i
        at = slice(i * column, (i + 1) * column)
        for ref, head in ((q_ref, q_head), (g_ref, g_head)):
            value = (ref[:, x, 0] if z_first else ref[x, :, 0]).reshape(column, LANES)
            for h in range(2):
                mine = (lane < HDIM) if h == 0 else (lane >= HDIM)
                head[h, at, :] = jnp.where(mine, value, jnp.zeros_like(value))


def over_pairs(body, info, wide, narrow, rest):
    count = wide[0].shape[-1] // LANES

    def pair(j, carry):
        lanes = pl.ds(pl.multiple_of(j * LANES, LANES), LANES)
        views = [ref.at[(slice(None),) * (len(ref.shape) - 1) + (lanes,)] for ref in wide]
        body(info, views, narrow.at[pl.ds(4 * j, 4)], *rest)
        return carry

    lax.fori_loop(0, count, pair, 0)


def stats_kernel(z_first, info, own_k, sib_k, own_v, sib_v, q_ref, g_ref, *rest):
    out_ref, scratch = rest[-5], rest[-4:]
    wide = [own_k, sib_k, own_v, sib_v, q_ref, g_ref]
    over_pairs(functools.partial(stats_pair, z_first), info, wide, out_ref, scratch)


def stats_pair(z_first, info, views, out_ref, keys, vals, q_head, g_head):
    own_k, sib_k, own_v, sib_v, q_ref, g_ref = views
    rows = q_head.shape[1]
    half = rows // 2
    load_keys(own_k, sib_k, own_v, sib_v, keys, vals)

    def passage(p, carry):
        load_rows(z_first, info[1 + p], q_ref, g_ref, q_head, g_head)

        def step(count, tail_used):
            k_part, v_part = keys[p, :count, :], vals[p, :count, :]
            heads = [(h, slice(s * half, (s + 1) * half)) for h in range(2) for s in range(2)]
            scores = [masked(dot_nt(k_part, q_head[h, at, :]), tail_used) for h, at in heads]
            upstream = [dot_nt(v_part, g_head[h, at, :]) for h, at in heads]
            for n in range(4):
                peak = jnp.max(scores[n], axis=0, keepdims=True)
                weights = jnp.exp(scores[n] - peak)
                stats = (
                    peak,
                    jnp.sum(weights, axis=0, keepdims=True),
                    jnp.sum(weights * upstream[n], axis=0, keepdims=True),
                    jnp.full((1, half), info[1 + p].astype(F32)),
                )
                for t, stat in enumerate(stats):
                    out_ref[n, pl.ds(2 * t + p, 1), :] = stat

        by_length(info[3 + p], step)
        return carry

    lax.fori_loop(0, 2, passage, 0)


def merge_kernel(in_ref, out_ref):
    chips = in_ref.shape[0]
    merged = []
    tops = [in_ref[:, t, :] for t in range(2)]
    sums = [in_ref[:, 2 + t, :] for t in range(2)]
    dots = [in_ref[:, 4 + t, :] for t in range(2)]
    owners = [in_ref[:, 6 + t, :] for t in range(2)]
    for query in range(QRY):
        held = [jnp.where(owners[t] == query, tops[t], -jnp.inf) for t in range(2)]
        peak = jnp.max(jnp.maximum(held[0], held[1]), axis=0, keepdims=True)
        factors = [jnp.exp(held[t] - peak) for t in range(2)]
        total = jnp.sum(sums[0] * factors[0] + sums[1] * factors[1], axis=0, keepdims=True)
        dotted = jnp.sum(dots[0] * factors[0] + dots[1] * factors[1], axis=0, keepdims=True)
        merged.append((peak + jnp.log(total), dotted / total))
    table = jnp.concatenate(
        [merged[0][0], merged[1][0], merged[0][1], merged[1][1]]
        + [jnp.zeros_like(merged[0][0])] * 4, axis=0
    )
    out_ref[...] = jnp.broadcast_to(table[None], out_ref.shape)


def grads_kernel(z_first, info, own_k, sib_k, own_v, sib_v, q_ref, g_ref, st_ref, *rest):
    outs, scratch = rest[-13:-8], rest[-8:]
    wide = [own_k, sib_k, own_v, sib_v, q_ref, g_ref, *outs]
    over_pairs(functools.partial(grads_pair, z_first), info, wide, st_ref, scratch)


def grads_pair(z_first, info, views, st_ref,
               keys, vals, q_head, g_head, dkeys, dvals, turned, dq_sum):
    (own_k, sib_k, own_v, sib_v, q_ref, g_ref,
     own_dk, sib_dk, own_dv, sib_dv, dq_ref) = views
    rows = q_head.shape[1]
    load_keys(own_k, sib_k, own_v, sib_v, keys, vals)
    dkeys[...] = jnp.zeros(dkeys.shape, BF16)
    dvals[...] = jnp.zeros(dvals.shape, BF16)
    dq_sum[...] = jnp.zeros(dq_sum.shape, F32)

    def passage(p, carry):
        owner = info[1 + p]
        load_rows(z_first, owner, q_ref, g_ref, q_head, g_head)

        def row_stat(h, t):
            return jnp.concatenate(
                [st_ref[2 * h + s, pl.ds(2 * t + owner, 1), :] for s in range(2)], axis=1
            )

        def step(count, tail_used):
            k_part, v_part = keys[p, :count, :], vals[p, :count, :]
            k_turned = k_part.T
            half = rows // 2
            heads = [(h, slice(s * half, (s + 1) * half)) for h in range(2) for s in range(2)]
            scores = [masked(dot_nt(k_part, q_head[h, at, :]), tail_used) for h, at in heads]
            upstream = [dot_nt(v_part, g_head[h, at, :]) for h, at in heads]
            probs = [jnp.exp(scores[n] - st_ref[n, pl.ds(owner, 1), :]) for n in range(4)]
            dscore = [(probs[n] * (upstream[n] - st_ref[n, pl.ds(2 + owner, 1), :])).astype(BF16) for n in range(4)]
            low = jnp.concatenate([x.astype(BF16) for x in probs], axis=1)
            dv_part = dot_nn(low, g_head[...].reshape(2 * rows, LANES))
            dk_part = dot_nn(jnp.concatenate(dscore, axis=1), q_head[...].reshape(2 * rows, LANES))
            dscore = [jnp.concatenate(dscore[2 * h:2 * h + 2], axis=1) for h in range(2)]
            for h in range(2):
                own = slice(h * HDIM, (h + 1) * HDIM)
                turned[own, :] = dot_nn(k_turned[own, :], dscore[h])
            dkeys[p, :count, :] = dk_part.astype(BF16)
            dvals[p, :count, :] = dv_part.astype(BF16)

        by_length(info[3 + p], step)
        at = pl.ds(pl.multiple_of(owner * rows, rows), rows)
        dq_sum[at, :] += turned[...].T
        return carry

    lax.fori_loop(0, 2, passage, 0)
    own_dk[...], sib_dk[...] = dkeys[0], dkeys[1]
    own_dv[...], sib_dv[...] = dvals[0], dvals[1]
    dq_ref[...] = dq_sum[...].astype(BF16)


PARTS = 2
PAIRS_A_STEP = 1


def blocks(slots, pairs, shape, part):
    span = PAIRS_A_STEP * LANES
    steps = pairs // PAIRS_A_STEP
    first = part * (steps // PARTS)
    own = pl.BlockSpec((slots, span), lambda i, info: (0, info[0] * steps + first + i))
    sib = pl.BlockSpec((slots, span), lambda i, info: (0, first + i))
    q_block = pl.BlockSpec(shape[:2] + (1, shape[3], span), lambda i, info: (0, 0, 0, 0, i))
    g_block = pl.BlockSpec(shape[:2] + (1, shape[3], span), lambda i, info: (0, 0, 1, 0, i))
    return own, [own, sib, own, sib, q_block, g_block], first, steps // PARTS


def sizes(operands):
    slots, half = operands[2].shape
    shape = operands[5].shape
    all_rows = shape[0] * shape[1] * shape[3]
    return slots, half, half // LANES, all_rows, all_rows // QRY


LIMIT = pltpu.CompilerParams(
    dimension_semantics=("arbitrary",), vmem_limit_bytes=48 * 1024 * 1024
)


def key_scratch(slots):
    return [pltpu.VMEM((2, slots, LANES), BF16)] * 2


def row_stats(operands, part, begun):
    slots, half, pairs, all_rows, rows = sizes(operands)
    own, in_blocks, first, steps = blocks(slots, pairs, operands[5].shape, part)
    return pl.pallas_call(
        functools.partial(stats_kernel, part == 0),
        grid_spec=pltpu.PrefetchScalarGridSpec(
            num_scalar_prefetch=1,
            grid=(steps,),
            in_specs=in_blocks + [pl.BlockSpec(memory_space=pl.ANY)] * len(begun),
            out_specs=pl.BlockSpec(
                (4 * PAIRS_A_STEP, 8, rows // 2), lambda i, info: (first + i, 0, 0)
            ),
            scratch_shapes=key_scratch(slots) + [pltpu.VMEM((2, rows, LANES), BF16)] * 2,
        ),
        out_shape=jax.ShapeDtypeStruct((4 * pairs, 8, rows // 2), F32),
        input_output_aliases={7: 0} if begun else {},
        compiler_params=LIMIT,
        cost_estimate=pl.CostEstimate(
            flops=4 * slots * rows * half, bytes_accessed=5 << 20,
            transcendentals=slots * rows * half // HDIM,
        ),
        name="row_stats",
    )(*operands, *begun)


def merge_stats(stats):
    return pl.pallas_call(
        merge_kernel,
        out_shape=jax.ShapeDtypeStruct(stats.shape, F32),
        in_specs=[pl.BlockSpec(memory_space=pltpu.VMEM)],
        out_specs=pl.BlockSpec(memory_space=pltpu.VMEM),
        name="merge_stats",
    )(stats)


def gradients(operands, stats, part, begun):
    slots, half, pairs, all_rows, rows = sizes(operands)
    own, in_blocks, first, steps = blocks(slots, pairs, operands[5].shape, part)
    span = PAIRS_A_STEP * LANES
    sib = pl.BlockSpec((slots, span), lambda i, info: (0, i))
    stat = pl.BlockSpec((4 * PAIRS_A_STEP, 8, rows // 2), lambda i, info: (first + i, 0, 0))
    whole = jax.ShapeDtypeStruct((slots, 2 * half), BF16)
    half_part = jax.ShapeDtypeStruct((slots, steps * span), BF16)
    return pl.pallas_call(
        functools.partial(grads_kernel, part == 0),
        grid_spec=pltpu.PrefetchScalarGridSpec(
            num_scalar_prefetch=1,
            grid=(steps,),
            in_specs=in_blocks + [stat] + [pl.BlockSpec(memory_space=pl.ANY)] * len(begun),
            out_specs=[own, sib, own, sib, pl.BlockSpec((all_rows, span), lambda i, info: (0, i))],
            scratch_shapes=key_scratch(slots)
            + [pltpu.VMEM((2, rows, LANES), BF16)] * 2
            + key_scratch(slots)
            + [pltpu.VMEM((LANES, rows), F32), pltpu.VMEM((all_rows, LANES), F32)],
        ),
        out_shape=[whole, half_part, whole, half_part,
                   jax.ShapeDtypeStruct((all_rows, steps * span), BF16)],
        input_output_aliases={8: 0, 9: 2} if begun else {},
        compiler_params=LIMIT,
        cost_estimate=pl.CostEstimate(
            flops=10 * slots * rows * half, bytes_accessed=8 << 20,
            transcendentals=slots * rows * half // HDIM,
        ),
        name="gradients",
    )(*operands, stats, *begun)


def per_device(x_size, z_size, queries, keys, values, grad_out, lengths, slot_query):
    chips = x_size * z_size
    core = lax.axis_index("core")
    width = keys.shape[2]
    half = width // 2
    span = half // PARTS
    keys, values = keys[0], values[0]

    mine = jnp.concatenate([slot_query, lengths])
    theirs = swap_cores(mine)
    info = jnp.stack([core, mine[0], theirs[0], mine[1], theirs[1]]).astype(jnp.int32)

    def features(value, at, count):
        return lax.dynamic_slice_in_dim(value, at, count, value.ndim - 1)

    both = lax.all_gather(jnp.stack([queries, grad_out]), "core", axis=1, tiled=True)
    gathered = (
        gather_x_then_z(features(both, core * half, span), x_size),
        gather_z_then_x(features(both, core * half + span, span), x_size, z_size),
    )
    sib_k = swap_cores(features(keys, (1 - core) * half, half))
    sib_v = swap_cores(features(values, (1 - core) * half, half))
    operands = [(info, keys, sib_k, values, sib_v, rows, rows) for rows in gathered]
    all_rows = sizes(operands[0])[3]

    stats = []
    for part in range(PARTS):
        stats = [row_stats(operands[part], part, stats)]
    stats = lax.all_to_all(stats[0], CHIP, 0, 0, tiled=True)
    stats = lax.all_to_all(merge_stats(stats), CHIP, 0, 0, tiled=True)

    held = all_rows // chips
    own_rows = held // 2
    begun, sibs, sums = [], [], []
    for part in range(PARTS):
        own_dk, sib_dk, own_dv, sib_dv, dq = gradients(operands[part], stats, part, begun)
        begun = [own_dk, own_dv]
        sibs.append((swap_cores(sib_dk), swap_cores(sib_dv)))
        terms = lax.all_to_all(dq.reshape(chips, held, span), CHIP, 0, 0, tiled=True)
        sums.append(jnp.sum(terms.astype(F32), axis=0).astype(BF16))

    own_dk, own_dv = begun
    for part, (sib_dk, sib_dv) in enumerate(sibs):
        at = (1 - core) * half + part * span
        own_dk = lax.dynamic_update_slice_in_dim(own_dk, sib_dk, at, 1)
        own_dv = lax.dynamic_update_slice_in_dim(own_dv, sib_dv, at, 1)

    summed = jnp.concatenate(sums, axis=1)
    kept = lax.dynamic_slice_in_dim(summed, core * own_rows, own_rows, 0)
    given = swap_cores(lax.dynamic_slice_in_dim(summed, (1 - core) * own_rows, own_rows, 0))
    grad_queries = jnp.where(
        core == 0, jnp.concatenate([kept, given], 1), jnp.concatenate([given, kept], 1)
    )
    return grad_queries, own_dk[None], own_dv[None]


def solution(mesh):
    groups = mesh.devices.shape[0]
    x_size, z_size = 4, 8
    fine = Mesh(
        mesh.devices.reshape(groups, x_size, z_size, 2), ("group", "x", "z", "core")
    )
    at = ("group", "x", "z", "core")
    return jax.shard_map(
        functools.partial(per_device, x_size, z_size),
        mesh=fine,
        in_specs=(P(at, None), P(at, None, None), P(at, None, None), P(at, None), P(at), P(at)),
        out_specs=(P(at, None), P(at, None, None), P(at, None, None)),
        check_vma=False,
    )
```

time: 219 us -> 204 us (0.932)
  Pallas kernels: 44.6 us -> 36.6 us
  starting transfers between devices: 54.2 us -> 48.1 us
  blocking collectives: 74.7 us -> 70.2 us
    pallas_call x3 -> x4, Pallas kernels: 42.6 us -> 34.7 us  [the longest x2 21.6 us: gradients(): pl.pallas_call(functools.partial(grads_kernel, part == 0), grid_spec=pltp...]
    all_to_all x2, waiting for transfers between devices: 5.87 us -> 11.7 us  [per_device(): lax.all_to_all(dq.reshape(chips, held, span), CHIP, 0, 0, tiled=True)]
    all_to_all x1, waiting for transfers between devices: 5.21 us -> 0.01 us  [gather_z_then_x(): return lax.all_to_all(repeated(column, x_size), 'x', 0, 0, tiled=True)]
    all_to_all x1, blocking collectives: 24.2 us -> 19.6 us  [per_device(): stats = lax.all_to_all(stats[0], CHIP, 0, 0, tiled=True)]
    all_to_all x2, starting transfers between devices: 22.1 us -> 18.5 us  [per_device(): lax.all_to_all(dq.reshape(chips, held, span), CHIP, 0, 0, tiled=True)]
    ppermute x8, starting transfers between devices: 27.5 us -> 25.1 us  [swap_cores(): return lax.ppermute(value, 'core', [(0, 1), (1, 0)])]
  transfers between devices with their start and end apart: 12 -> 12, of which waited for: 5 -> 5; matrix products, arithmetic and copies ran while one was open for 7% -> 8% of each run, Pallas kernels for 7% -> 9%
where the time goes in v3:
time: 204 us; the launch traced here: 202 us
  blocking collectives  70.2 us (34%)
  starting transfers between devices  48.1 us (24%)
  Pallas kernels  36.6 us (18%)
  between operations  15.5 us (8%)
  local copies, waits for them, and re-layouts  14.5 us (7%)
  waiting for transfers between devices  14.1 us (7%)
  other arithmetic  3.16 us (2%)
    ppermute x8, starting transfers between devices, swap_cores(): return lax.ppermute(value, 'core', [(0, 1), (1, 0)])  25.1 us
    all_to_all x1, blocking collectives, gather_z_then_x(): column = lax.all_to_all(repeated(value, z_size), 'z', 0, 0, tiled=True)  24.3 us
    pallas_call x2, Pallas kernels, gradients(): pl.pallas_call(functools.partial(grads_kernel, part == 0), grid_spec=pltp...  21.6 us
    all_to_all x1, blocking collectives, per_device(): stats = lax.all_to_all(stats[0], CHIP, 0, 0, tiled=True)  19.6 us
    all_to_all x2, starting transfers between devices, per_device(): lax.all_to_all(dq.reshape(chips, held, span), CHIP, 0, 0, tiled=True)  18.5 us
    all_to_all x1, blocking collectives, per_device(): stats = lax.all_to_all(merge_stats(stats), CHIP, 0, 0, tiled=True)  14.3 us
    pallas_call x2, Pallas kernels, row_stats(): pl.pallas_call(functools.partial(stats_kernel, part == 0), grid_spec=pltp...  13.1 us
    all_to_all x2, waiting for transfers between devices, per_device(): lax.all_to_all(dq.reshape(chips, held, span), CHIP, 0, 0, tiled=True)  11.7 us
  transfers between devices with their start and end apart: 12, of which 5 were waited for; matrix products, arithmetic and copies ran while one was open for 8% of the time, Pallas kernels for 9%

profile of v3, /device:TPU:25, one launch (start us, length us, event | category | flops | bytes accessed | tf_op | source)
XLA Modules:
  0.0 202.2 jit_solution(1715247980194932959)
XLA Ops:
  7.2 0.0 all-gather.3.cloned.1.call-start
  7.2 0.9 pad_maximum_fusion
  8.1 2.3 %all_gather.9 = bf16[2,32,2048]{2,1,0:T(8,128)(2,1)S(1)} all-gather(bf16[2,16,2048]{2,1,0:T(8,128)(2,1)S(1)} %pad_maximum_fusion), channel_id=1, replica_groups=mesh['group'=4,'x'=4,'z'=8,'core'=2] {'core'}, dimensions={1}, use_global_device_ids=true | all-gather | bytes 393216 | tf_op jit(solution)/shard_map/all_gather | solution.py:318
  10.5 9.7 %all_to_all.35 = bf16[4,2,32,512]{3,2,1,0:T(8,128)(2,1)} all-to-all(bf16[4,2,32,512]{3,2,1,0:T(8,128)(2,1)S(1)} %broadcast_in_dim.32), channel_id=1, replica_groups=mesh['group'=4,'x'=4,'z'=8,'core'=2] {'x'}, dimensions={0} | all-to-all | bytes 524288 | tf_op jit(solution)/shard_map/all_to_all | solution.py:29
  20.2 0.0 all-gather.3.cloned.1.call-update
  20.3 24.3 %all_to_all.36 = bf16[8,2,32,512]{3,2,1,0:T(8,128)(2,1)S(1)} all-to-all(bf16[8,2,32,512]{3,2,1,0:T(8,128)(2,1)S(1)} %broadcast_in_dim.33), channel_id=1, replica_groups=mesh['group'=4,'x'=4,'z'=8,'core'=2] {'z'}, dimensions={0} | all-to-all | bytes 1048576 | tf_op jit(solution)/shard_map/all_to_all | solution.py:34
  44.6 1.6 broadcast_in_dim.34
  46.2 4.5 %all-to-all-start.2 = ((bf16[4,8,2,32,512]{4,3,2,1,0:T(8,128)(2,1)}), bf16[4,8,2,32,512]{4,3,2,1,0:T(8,128)(2,1)}, u32[]{:S(2)}, u32[]{:S(2)}) async-start(bf16[4,8,2,32,512]{4,3,2,1,0:T(8,128)(2,1)} %broadcast_in_dim.34), calls=%async_computation.2 | async-start | bytes 4194304 | tf_op jit(solution)/shard_map/all_to_all | solution.py:35
  50.7 0.0 copy-start
  50.7 2.5 %dynamic-slice_bitcast_fusion = bf16[512,1024]{1,0:T(8,128)(2,1)} fusion(bf16[1,512,2048]{2,1,0:T(8,128)(2,1)} %param.8, s32[]{:T(128)S(6)} %select_n.31), kind=kLoop, calls=%fused_computation | loop fusion | bytes 2097156 | tf_op jit(solution)/shard_map/dynamic_slice | solution.py:316
  53.1 6.7 %collective-permute-start.2 = (bf16[512,1024]{1,0:T(8,128)(2,1)}, bf16[512,1024]{1,0:T(8,128)(2,1)S(1)}, u32[]{:S(2)}, u32[]{:S(2)}) collective-permute-start(bf16[512,1024]{1,0:T(8,128)(2,1)} %dynamic-slice_bitcast_fusion), channel_id=1, source_target_pairs={{0,1},{1,0},{2,3},{3,2},{4,5},{5,4},{6,7},{7,6},{8,9},{9,8},{10,11... | collective-permute-start | bytes 3145736 | tf_op jit(solution)/shard_map/ppermute | solution.py:21
  59.8 1.1 dynamic-slice_bitcast_fusion.1
  60.9 0.0 collective-permute-start.1
  62.2 0.1 pad_add_fusion
  62.3 0.5 collective-permute-start
  62.8 0.8 collective-permute-done
  63.6 0.6 fusion.2
  64.2 1.3 stack.16.info
  65.4 0.0 collective-permute-done.2.sib_v
  65.4 0.0 collective-permute-done.1.sib_k
  65.4 0.5 all-gather.3.cloned.1.call-done
  66.0 6.5 %row_stats.2.rest_0_ = f32[32,8,256]{2,1,0:T(8,128)S(1)} custom-call(s32[5]{0:T(128)S(1)} %stack.16.info, bf16[512,2048]{1,0:T(8,128)(2,1)S(1)} %bitcast.24, bf16[512,1024]{1,0:T(8,128)(2,1)} %collective-permute-done.1.sib_k, bf16[512,2048]{1,0:T(8,128)(2,1)} %bitcast.26, bf16[512,1024]{1,0:T(8,128)(2,1)S(1)} %collective-permute-done.2.sib_v, ...), custom_call_target="tpu_custom_call" | custom-call | flops 1073741824 | bytes 5242880 | tf_op jit(solution)/shard_map/row_stats/pallas_call | solution.py:239
  72.5 6.6 %row_stats.3 = f32[32,8,256]{2,1,0:T(8,128)S(1)} custom-call(s32[5]{0:T(128)S(1)} %stack.16.info, bf16[512,2048]{1,0:T(8,128)(2,1)S(1)} %bitcast.25, bf16[512,1024]{1,0:T(8,128)(2,1)} %collective-permute-done.1.sib_k, bf16[512,2048]{1,0:T(8,128)(2,1)} %bitcast.27, ...), custom_call_target="tpu_custom_call", output_to_operand_aliasing={{}: (7, {})} | custom-call | flops 1073741824 | bytes 5242880 | tf_op jit(solution)/shard_map/row_stats/pallas_call | solution.py:239
  79.1 19.6 %all_to_all.37.in_ref = f32[32,8,256]{2,1,0:T(8,128)} all-to-all(f32[32,8,256]{2,1,0:T(8,128)S(1)} %row_stats.3), channel_id=1, replica_groups=mesh['group'=4,'x'=4,'z'=8,'core'=2] {'x','z'}, dimensions={0} | all-to-all | bytes 524288 | tf_op jit(solution)/shard_map/all_to_all | solution.py:331
  98.7 2.0 merge_stats.1
  100.7 14.3 %all_to_all.38.st_ref = f32[32,8,256]{2,1,0:T(8,128)S(1)} all-to-all(f32[32,8,256]{2,1,0:T(8,128)} %merge_stats.1), channel_id=1, replica_groups=mesh['group'=4,'x'=4,'z'=8,'core'=2] {'x','z'}, dimensions={0} | all-to-all | bytes 524288 | tf_op jit(solution)/shard_map/all_to_all | solution.py:332
  114.9 10.8 %gradients.2 = (bf16[512,2048]{1,0:T(8,128)(2,1)}, bf16[512,512]{1,0:T(8,128)(2,1)S(1)}, bf16[512,2048]{1,0:T(8,128)(2,1)}, bf16[512,512]{1,0:T(8,128)(2,1)S(1)}, bf16[1024,512]{1,0:T(8,128)(2,1)}) custom-call(s32[5]{0:T(128)S(1)} %stack.16.info, bf16[512,2048]{1,0:T(8,128)(2,1)} %bitcast.22, bf16[512,1024]{1,0:T(8,128)(2,1)} %collective-permute-done.1.sib_k, ...), custom_call_target="tpu_custom_call" | custom-call | flops 2684354560 | bytes 8388608 | tf_op jit(solution)/shard_map/gradients/pallas_call | solution.py:279
  125.7 10.6 %all-to-all-start.5 = ((bf16[32,32,512]{2,1,0:T(8,128)(2,1)}), bf16[32,32,512]{2,1,0:T(8,128)(2,1)}, u32[]{:S(2)}, u32[]{:S(2)}) async-start(bf16[32,32,512]{2,1,0:T(8,128)(2,1)} %bitcast.8), calls=%async_computation.5 | async-start | bytes 2097152 | tf_op jit(solution)/shard_map/all_to_all | solution.py:341
  136.3 10.8 %gradients.3 = (bf16[512,2048]{1,0:T(8,128)(2,1)}, bf16[512,512]{1,0:T(8,128)(2,1)S(1)}, bf16[512,2048]{1,0:T(8,128)(2,1)}, bf16[512,512]{1,0:T(8,128)(2,1)S(1)}, bf16[1024,512]{1,0:T(8,128)(2,1)}) custom-call(s32[5]{0:T(128)S(1)} %stack.16.info, bf16[512,2048]{1,0:T(8,128)(2,1)} %bitcast.23, ...), custom_call_target="tpu_custom_call", output_to_operand_aliasing={{0}: (8, {}), {2}: (9, {})} | custom-call | flops 2684354560 | bytes 8388608 | tf_op jit(solution)/shard_map/gradients/pallas_call | solution.py:279
  147.1 8.8 %all-to-all-done.5 = bf16[32,32,512]{2,1,0:T(8,128)(2,1)} async-done(((bf16[32,32,512]{2,1,0:T(8,128)(2,1)}), bf16[32,32,512]{2,1,0:T(8,128)(2,1)}, u32[]{:S(2)}, u32[]{:S(2)}) %all-to-all-start.5) | async-done | bytes 1048608 | tf_op jit(solution)/shard_map/all_to_all | solution.py:341
  156.0 7.8 %all-to-all-start.6 = ((bf16[32,32,512]{2,1,0:T(8,128)(2,1)}), bf16[32,32,512]{2,1,0:T(8,128)(2,1)S(1)}, u32[]{:S(2)}, u32[]{:S(2)}) async-start(bf16[32,32,512]{2,1,0:T(8,128)(2,1)} %bitcast.9), calls=%async_computation.6 | async-start | bytes 2097152 | tf_op jit(solution)/shard_map/all_to_all | solution.py:341
  163.8 7.3 %collective-permute-start.4 = (bf16[512,512]{1,0:T(8,128)(2,1)S(1)}, bf16[512,512]{1,0:T(8,128)(2,1)}, u32[]{:S(2)}, u32[]{:S(2)}) collective-permute-start(bf16[512,512]{1,0:T(8,128)(2,1)S(1)} %copy-done.2), channel_id=1, source_target_pairs={{0,1},{1,0},{2,3},{3,2},{4,5},{5,4},{6,7},{7,6},{8,9},{9,8},{10,11... | collective-permute-start | bytes 1572872 | tf_op jit(solution)/shard_map/ppermute | solution.py:21
  171.1 0.1 collective-permute-start.6
  171.2 0.4 collective-permute-start.5
  171.6 0.1 collective-permute-start.7
  171.7 1.1 collective-permute-done.4
  172.8 1.9 bitcast_dynamic-update-slice_fusion.3
  174.6 0.0 collective-permute-done.6
  174.6 1.9 bitcast_dynamic-update-slice_fusion.1
  176.5 1.9 bitcast_dynamic-update-slice_fusion.2
  178.4 1.4 reduce_sum.24
  179.8 2.8 %all-to-all-done.6 = bf16[32,32,512]{2,1,0:T(8,128)(2,1)S(1)} async-done(((bf16[32,32,512]{2,1,0:T(8,128)(2,1)}), bf16[32,32,512]{2,1,0:T(8,128)(2,1)S(1)}, u32[]{:S(2)}, u32[]{:S(2)}) %all-to-all-start.6) | async-done | bytes 1048608 | tf_op jit(solution)/shard_map/all_to_all | solution.py:341
  182.6 0.2 reduce_sum.25
  182.8 10.0 %collective-permute-start.3 = (bf16[16,1024]{1,0:T(8,128)(2,1)S(1)}, bf16[16,1024]{1,0:T(8,128)(2,1)S(1)}, u32[]{:S(2)}, u32[]{:S(2)}) collective-permute-start(bf16[16,1024]{1,0:T(8,128)(2,1)S(1)} %get-tuple-element.26), channel_id=1, source_target_pairs={{0,1},{1,0},{2,3},{3,2},{4,5},{5,4},{6,7},{7,6},{8,9},{9,8},{10,11... | collective-permute-start | bytes 98312 | tf_op jit(solution)/shard_map/ppermute | solution.py:21
  192.8 0.0 collective-permute-done.7
  192.8 1.9 bitcast_dynamic-update-slice_fusion
  194.7 0.0 collective-permute-done.3
  194.7 0.6 maximum_select_fusion
  (11 shorter events, 0.1 us)
Async XLA Ops:
  7.2 58.8 %all-gather.3.cloned.1.call-start = ((), (), s32[]{:S(2)}) async-start(), calls=%async_computation.7 | async-start | bytes 2359296 | tf_op jit(solution)/shard_map/all_gather | solution.py:30
  46.2 26.3 %all-to-all-start.2 = ((bf16[4,8,2,32,512]{4,3,2,1,0:T(8,128)(2,1)}), bf16[4,8,2,32,512]{4,3,2,1,0:T(8,128)(2,1)}, u32[]{:S(2)}, u32[]{:S(2)}) async-start(bf16[4,8,2,32,512]{4,3,2,1,0:T(8,128)(2,1)} %broadcast_in_dim.34), calls=%async_computation.2 | async-start | bytes 4194304 | tf_op jit(solution)/shard_map/all_to_all | solution.py:35
  50.7 9.1 %copy-start = (bf16[1,512,2048]{2,1,0:T(8,128)(2,1)S(1)}, bf16[1,512,2048]{2,1,0:T(8,128)(2,1)}, u32[]{:S(2)}) copy-start(bf16[1,512,2048]{2,1,0:T(8,128)(2,1)} %param.7) | copy-start | bytes 6291460
  53.1 12.3 %collective-permute-start.2 = (bf16[512,1024]{1,0:T(8,128)(2,1)}, bf16[512,1024]{1,0:T(8,128)(2,1)S(1)}, u32[]{:S(2)}, u32[]{:S(2)}) collective-permute-start(bf16[512,1024]{1,0:T(8,128)(2,1)} %dynamic-slice_bitcast_fusion), channel_id=1, source_target_pairs={{0,1},{1,0},{2,3},{3,2},{4,5},{5,4},{6,7},{7,6},{8,9},{9,8},{10,11... | collective-permute-start | bytes 3145736 | tf_op jit(solution)/shard_map/ppermute | solution.py:21
  60.9 4.6 %collective-permute-start.1 = (bf16[512,1024]{1,0:T(8,128)(2,1)}, bf16[512,1024]{1,0:T(8,128)(2,1)}, u32[]{:S(2)}, u32[]{:S(2)}) collective-permute-start(bf16[512,1024]{1,0:T(8,128)(2,1)} %dynamic-slice_bitcast_fusion.1), channel_id=1, source_target_pairs={{0,1},{1,0},{2,3},{3,2},{4,5},{5,4},{6,7},{7,6},{8,9},{9,8},{10,11... | collective-permute-start | bytes 3145736 | tf_op jit(solution)/shard_map/ppermute | solution.py:21
  62.3 1.4 collective-permute-start
  125.7 10.7 %copy-start.1 = (bf16[512,512]{1,0:T(8,128)(2,1)}, bf16[512,512]{1,0:T(8,128)(2,1)S(1)}, u32[]{:S(2)}) copy-start(bf16[512,512]{1,0:T(8,128)(2,1)S(1)} %get-tuple-element.18) | copy-start | bytes 1572868
  125.7 30.3 %all-to-all-start.5 = ((bf16[32,32,512]{2,1,0:T(8,128)(2,1)}), bf16[32,32,512]{2,1,0:T(8,128)(2,1)}, u32[]{:S(2)}, u32[]{:S(2)}) async-start(bf16[32,32,512]{2,1,0:T(8,128)(2,1)} %bitcast.8), calls=%async_computation.5 | async-start | bytes 2097152 | tf_op jit(solution)/shard_map/all_to_all | solution.py:341
  147.1 16.7 %copy-start.2 = (bf16[512,512]{1,0:T(8,128)(2,1)S(1)}, bf16[512,512]{1,0:T(8,128)(2,1)}, u32[]{:S(2)}) copy-start(bf16[512,512]{1,0:T(8,128)(2,1)} %copy-done.1) | copy-start | bytes 1572868
  156.0 26.6 %all-to-all-start.6 = ((bf16[32,32,512]{2,1,0:T(8,128)(2,1)}), bf16[32,32,512]{2,1,0:T(8,128)(2,1)S(1)}, u32[]{:S(2)}, u32[]{:S(2)}) async-start(bf16[32,32,512]{2,1,0:T(8,128)(2,1)} %bitcast.9), calls=%async_computation.6 | async-start | bytes 2097152 | tf_op jit(solution)/shard_map/all_to_all | solution.py:341
  163.8 8.9 %collective-permute-start.4 = (bf16[512,512]{1,0:T(8,128)(2,1)S(1)}, bf16[512,512]{1,0:T(8,128)(2,1)}, u32[]{:S(2)}, u32[]{:S(2)}) collective-permute-start(bf16[512,512]{1,0:T(8,128)(2,1)S(1)} %copy-done.2), channel_id=1, source_target_pairs={{0,1},{1,0},{2,3},{3,2},{4,5},{5,4},{6,7},{7,6},{8,9},{9,8},{10,11... | collective-permute-start | bytes 1572872 | tf_op jit(solution)/shard_map/ppermute | solution.py:21
  171.1 3.5 %collective-permute-start.6 = (bf16[512,512]{1,0:T(8,128)(2,1)S(1)}, bf16[512,512]{1,0:T(8,128)(2,1)}, u32[]{:S(2)}, u32[]{:S(2)}) collective-permute-start(bf16[512,512]{1,0:T(8,128)(2,1)S(1)} %get-tuple-element.21), channel_id=1, source_target_pairs={{0,1},{1,0},{2,3},{3,2},{4,5},{5,4},{6,7},{7,6},{8,9},{9,8},{10,11... | collective-permute-start | bytes 1572872 | tf_op jit(solution)/shard_map/ppermute | solution.py:21
  171.2 5.3 %collective-permute-start.5 = (bf16[512,512]{1,0:T(8,128)(2,1)S(1)}, bf16[512,512]{1,0:T(8,128)(2,1)}, u32[]{:S(2)}, u32[]{:S(2)}) collective-permute-start(bf16[512,512]{1,0:T(8,128)(2,1)S(1)} %get-tuple-element.19), channel_id=1, source_target_pairs={{0,1},{1,0},{2,3},{3,2},{4,5},{5,4},{6,7},{7,6},{8,9},{9,8},{10,11... | collective-permute-start | bytes 1572872 | tf_op jit(solution)/shard_map/ppermute | solution.py:21
  171.6 21.2 %collective-permute-start.7 = (bf16[512,512]{1,0:T(8,128)(2,1)S(1)}, bf16[512,512]{1,0:T(8,128)(2,1)}, u32[]{:S(2)}, u32[]{:S(2)}) collective-permute-start(bf16[512,512]{1,0:T(8,128)(2,1)S(1)} %get-tuple-element.22), channel_id=1, source_target_pairs={{0,1},{1,0},{2,3},{3,2},{4,5},{5,4},{6,7},{7,6},{8,9},{9,8},{10,11... | collective-permute-start | bytes 1572872 | tf_op jit(solution)/shard_map/ppermute | solution.py:21
  182.8 11.9 %collective-permute-start.3 = (bf16[16,1024]{1,0:T(8,128)(2,1)S(1)}, bf16[16,1024]{1,0:T(8,128)(2,1)S(1)}, u32[]{:S(2)}, u32[]{:S(2)}) collective-permute-start(bf16[16,1024]{1,0:T(8,128)(2,1)S(1)} %get-tuple-element.26), channel_id=1, source_target_pairs={{0,1},{1,0},{2,3},{3,2},{4,5},{5,4},{6,7},{7,6},{8,9},{9,8},{10,11... | collective-permute-start | bytes 98312 | tf_op jit(solution)/shard_map/ppermute | solution.py:21
Sparse Core Ops, SparseCore 0:
  20.3 45.5 all-gather.2

commit v4 on v3

--- a/solution.py
+++ b/solution.py
@@ -25,13 +25,18 @@
     return jnp.broadcast_to(value[None], (count,) + value.shape)
 
 
+def across(value, axes):
+    flat = value.reshape((-1,) + value.shape[2:])
+    return lax.all_to_all(flat, axes, 0, 0, tiled=True).reshape(value.shape)
+
+
 def gather_x_then_z(value, x_size):
-    columns = lax.all_to_all(repeated(value, x_size), "x", 0, 0, tiled=True)
+    columns = across(repeated(value, x_size), ("x", "core"))
     return lax.all_gather(columns, "z", axis=0, tiled=False)
 
 
 def gather_z_then_x(value, x_size, z_size):
-    column = lax.all_to_all(repeated(value, z_size), "z", 0, 0, tiled=True)
+    column = across(repeated(value, z_size), ("z", "core"))
     return lax.all_to_all(repeated(column, x_size), "x", 0, 0, tiled=True)
 
 
@@ -57,54 +62,36 @@
     return jnp.concatenate([scores[:cut], tail], axis=0)
 
 
-def load_keys(own_k, sib_k, own_v, sib_v, keys, vals):
-    keys[0], keys[1] = own_k[...], sib_k[...]
-    vals[0], vals[1] = own_v[...], sib_v[...]
-
-
 def load_rows(z_first, owner, q_ref, g_ref, q_head, g_head):
     z_size, x_size = q_ref.shape[:2] if z_first else q_ref.shape[1::-1]
-    column = z_size * q_ref.shape[3]
+    column = z_size * q_ref.shape[2] * q_ref.shape[4]
     lane = lax.broadcasted_iota(jnp.int32, (column, LANES), 1)
     for i in range(x_size // QRY):
         x = owner * (x_size // QRY) + i
         at = slice(i * column, (i + 1) * column)
         for ref, head in ((q_ref, q_head), (g_ref, g_head)):
-            value = (ref[:, x, 0] if z_first else ref[x, :, 0]).reshape(column, LANES)
+            value = (ref[:, x, :, 0] if z_first else ref[x, :, :, 0]).reshape(column, LANES)
             for h in range(2):
                 mine = (lane < HDIM) if h == 0 else (lane >= HDIM)
                 head[h, at, :] = jnp.where(mine, value, jnp.zeros_like(value))
 
 
-def over_pairs(body, info, wide, narrow, rest):
-    count = wide[0].shape[-1] // LANES
-
-    def pair(j, carry):
-        lanes = pl.ds(pl.multiple_of(j * LANES, LANES), LANES)
-        views = [ref.at[(slice(None),) * (len(ref.shape) - 1) + (lanes,)] for ref in wide]
-        body(info, views, narrow.at[pl.ds(4 * j, 4)], *rest)
-        return carry
-
-    lax.fori_loop(0, count, pair, 0)
+def with_rows(p, z_first, info, q_ref, g_ref, q_head, g_head):
+    @pl.when((p == 0) | (info[1] != info[2]))
+    def _():
+        load_rows(z_first, info[1 + p], q_ref, g_ref, q_head, g_head)
 
 
 def stats_kernel(z_first, info, own_k, sib_k, own_v, sib_v, q_ref, g_ref, *rest):
-    out_ref, scratch = rest[-5], rest[-4:]
-    wide = [own_k, sib_k, own_v, sib_v, q_ref, g_ref]
-    over_pairs(functools.partial(stats_pair, z_first), info, wide, out_ref, scratch)
-
-
-def stats_pair(z_first, info, views, out_ref, keys, vals, q_head, g_head):
-    own_k, sib_k, own_v, sib_v, q_ref, g_ref = views
+    out_ref, q_head, g_head = rest[-3:]
     rows = q_head.shape[1]
     half = rows // 2
-    load_keys(own_k, sib_k, own_v, sib_v, keys, vals)
-
-    def passage(p, carry):
-        load_rows(z_first, info[1 + p], q_ref, g_ref, q_head, g_head)
-
-        def step(count, tail_used):
-            k_part, v_part = keys[p, :count, :], vals[p, :count, :]
+
+    for p, (k_ref, v_ref) in enumerate(((own_k, own_v), (sib_k, sib_v))):
+        with_rows(p, z_first, info, q_ref, g_ref, q_head, g_head)
+
+        def step(count, tail_used, p=p, k_ref=k_ref, v_ref=v_ref):
+            k_part, v_part = k_ref[:count, :], v_ref[:count, :]
             heads = [(h, slice(s * half, (s + 1) * half)) for h in range(2) for s in range(2)]
             scores = [masked(dot_nt(k_part, q_head[h, at, :]), tail_used) for h, at in heads]
             upstream = [dot_nt(v_part, g_head[h, at, :]) for h, at in heads]
@@ -118,12 +105,9 @@
                     jnp.full((1, half), info[1 + p].astype(F32)),
                 )
                 for t, stat in enumerate(stats):
-                    out_ref[n, pl.ds(2 * t + p, 1), :] = stat
+                    out_ref[n, 2 * t + p:2 * t + p + 1, :] = stat
 
         by_length(info[3 + p], step)
-        return carry
-
-    lax.fori_loop(0, 2, passage, 0)
 
 
 def merge_kernel(in_ref, out_ref):
@@ -148,89 +132,81 @@
 
 
 def grads_kernel(z_first, info, own_k, sib_k, own_v, sib_v, q_ref, g_ref, st_ref, *rest):
-    outs, scratch = rest[-13:-8], rest[-8:]
-    wide = [own_k, sib_k, own_v, sib_v, q_ref, g_ref, *outs]
-    over_pairs(functools.partial(grads_pair, z_first), info, wide, st_ref, scratch)
-
-
-def grads_pair(z_first, info, views, st_ref,
-               keys, vals, q_head, g_head, dkeys, dvals, turned, dq_sum):
-    (own_k, sib_k, own_v, sib_v, q_ref, g_ref,
-     own_dk, sib_dk, own_dv, sib_dv, dq_ref) = views
+    own_dk, sib_dk, own_dv, sib_dv, dq_ref, q_head, g_head, turned = rest[-8:]
     rows = q_head.shape[1]
-    load_keys(own_k, sib_k, own_v, sib_v, keys, vals)
-    dkeys[...] = jnp.zeros(dkeys.shape, BF16)
-    dvals[...] = jnp.zeros(dvals.shape, BF16)
-    dq_sum[...] = jnp.zeros(dq_sum.shape, F32)
-
-    def passage(p, carry):
-        owner = info[1 + p]
-        load_rows(z_first, owner, q_ref, g_ref, q_head, g_head)
-
-        def row_stat(h, t):
-            return jnp.concatenate(
-                [st_ref[2 * h + s, pl.ds(2 * t + owner, 1), :] for s in range(2)], axis=1
-            )
-
-        def step(count, tail_used):
-            k_part, v_part = keys[p, :count, :], vals[p, :count, :]
+    half = rows // 2
+    sides = ((own_k, own_v, own_dk, own_dv), (sib_k, sib_v, sib_dk, sib_dv))
+
+    for p, refs in enumerate(sides):
+        with_rows(p, z_first, info, q_ref, g_ref, q_head, g_head)
+
+        def step(count, tail_used, p=p, refs=refs, owner=info[1 + p]):
+            k_ref, v_ref, dk_ref, dv_ref = refs
+            k_part, v_part = k_ref[:count, :], v_ref[:count, :]
             k_turned = k_part.T
-            half = rows // 2
             heads = [(h, slice(s * half, (s + 1) * half)) for h in range(2) for s in range(2)]
             scores = [masked(dot_nt(k_part, q_head[h, at, :]), tail_used) for h, at in heads]
             upstream = [dot_nt(v_part, g_head[h, at, :]) for h, at in heads]
             probs = [jnp.exp(scores[n] - st_ref[n, pl.ds(owner, 1), :]) for n in range(4)]
-            dscore = [(probs[n] * (upstream[n] - st_ref[n, pl.ds(2 + owner, 1), :])).astype(BF16) for n in range(4)]
+            dscore = [
+                (probs[n] * (upstream[n] - st_ref[n, pl.ds(2 + owner, 1), :])).astype(BF16)
+                for n in range(4)
+            ]
             low = jnp.concatenate([x.astype(BF16) for x in probs], axis=1)
             dv_part = dot_nn(low, g_head[...].reshape(2 * rows, LANES))
             dk_part = dot_nn(jnp.concatenate(dscore, axis=1), q_head[...].reshape(2 * rows, LANES))
-            dscore = [jnp.concatenate(dscore[2 * h:2 * h + 2], axis=1) for h in range(2)]
             for h in range(2):
                 own = slice(h * HDIM, (h + 1) * HDIM)
-                turned[own, :] = dot_nn(k_turned[own, :], dscore[h])
-            dkeys[p, :count, :] = dk_part.astype(BF16)
-            dvals[p, :count, :] = dv_part.astype(BF16)
+                both = jnp.concatenate(dscore[2 * h:2 * h + 2], axis=1)
+                turned[p, own, :] = dot_nn(k_turned[own, :], both)
+            for ref, part in ((dk_ref, dk_part), (dv_ref, dv_part)):
+                ref[:count, :] = part.astype(BF16)
+                unused = ref.shape[0] - count
+                if unused:
+                    ref[count:, :] = jnp.zeros((unused, LANES), BF16)
 
         by_length(info[3 + p], step)
-        at = pl.ds(pl.multiple_of(owner * rows, rows), rows)
-        dq_sum[at, :] += turned[...].T
-        return carry
-
-    lax.fori_loop(0, 2, passage, 0)
-    own_dk[...], sib_dk[...] = dkeys[0], dkeys[1]
-    own_dv[...], sib_dv[...] = dvals[0], dvals[1]
-    dq_ref[...] = dq_sum[...].astype(BF16)
+
+    first = pl.ds(pl.multiple_of(info[1] * rows, rows), rows)
+    other = pl.ds(pl.multiple_of((1 - info[1]) * rows, rows), rows)
+    same = info[1] == info[2]
+
+    @pl.when(same)
+    def _():
+        dq_ref[first, :] = (turned[0] + turned[1]).astype(BF16).T
+        dq_ref[other, :] = jnp.zeros((rows, LANES), BF16)
+
+    @pl.when(jnp.logical_not(same))
+    def _():
+        dq_ref[first, :] = turned[0].astype(BF16).T
+        dq_ref[other, :] = turned[1].astype(BF16).T
 
 
 PARTS = 2
-PAIRS_A_STEP = 1
 
 
 def blocks(slots, pairs, shape, part):
-    span = PAIRS_A_STEP * LANES
-    steps = pairs // PAIRS_A_STEP
+    span, steps = LANES, pairs
     first = part * (steps // PARTS)
     own = pl.BlockSpec((slots, span), lambda i, info: (0, info[0] * steps + first + i))
     sib = pl.BlockSpec((slots, span), lambda i, info: (0, first + i))
-    q_block = pl.BlockSpec(shape[:2] + (1, shape[3], span), lambda i, info: (0, 0, 0, 0, i))
-    g_block = pl.BlockSpec(shape[:2] + (1, shape[3], span), lambda i, info: (0, 0, 1, 0, i))
+    q_block, g_block = (
+        pl.BlockSpec(shape[:3] + (1, shape[4], span), lambda i, info, t=t: (0, 0, 0, t, 0, i))
+        for t in range(2)
+    )
     return own, [own, sib, own, sib, q_block, g_block], first, steps // PARTS
 
 
 def sizes(operands):
     slots, half = operands[2].shape
     shape = operands[5].shape
-    all_rows = shape[0] * shape[1] * shape[3]
+    all_rows = shape[0] * shape[1] * shape[2] * shape[4]
     return slots, half, half // LANES, all_rows, all_rows // QRY
 
 
 LIMIT = pltpu.CompilerParams(
     dimension_semantics=("arbitrary",), vmem_limit_bytes=48 * 1024 * 1024
 )
-
-
-def key_scratch(slots):
-    return [pltpu.VMEM((2, slots, LANES), BF16)] * 2
 
 
 def row_stats(operands, part, begun):
@@ -243,9 +219,9 @@
             grid=(steps,),
             in_specs=in_blocks + [pl.BlockSpec(memory_space=pl.ANY)] * len(begun),
             out_specs=pl.BlockSpec(
-                (4 * PAIRS_A_STEP, 8, rows // 2), lambda i, info: (first + i, 0, 0)
+                (4, 8, rows // 2), lambda i, info: (first + i, 0, 0)
             ),
-            scratch_shapes=key_scratch(slots) + [pltpu.VMEM((2, rows, LANES), BF16)] * 2,
+            scratch_shapes=[pltpu.VMEM((2, rows, LANES), BF16)] * 2,
         ),
         out_shape=jax.ShapeDtypeStruct((4 * pairs, 8, rows // 2), F32),
         input_output_aliases={7: 0} if begun else {},
@@ -271,9 +247,9 @@
 def gradients(operands, stats, part, begun):
     slots, half, pairs, all_rows, rows = sizes(operands)
     own, in_blocks, first, steps = blocks(slots, pairs, operands[5].shape, part)
-    span = PAIRS_A_STEP * LANES
+    span = LANES
     sib = pl.BlockSpec((slots, span), lambda i, info: (0, i))
-    stat = pl.BlockSpec((4 * PAIRS_A_STEP, 8, rows // 2), lambda i, info: (first + i, 0, 0))
+    stat = pl.BlockSpec((4, 8, rows // 2), lambda i, info: (first + i, 0, 0))
     whole = jax.ShapeDtypeStruct((slots, 2 * half), BF16)
     half_part = jax.ShapeDtypeStruct((slots, steps * span), BF16)
     return pl.pallas_call(
@@ -283,10 +259,8 @@
             grid=(steps,),
             in_specs=in_blocks + [stat] + [pl.BlockSpec(memory_space=pl.ANY)] * len(begun),
             out_specs=[own, sib, own, sib, pl.BlockSpec((all_rows, span), lambda i, info: (0, i))],
-            scratch_shapes=key_scratch(slots)
-            + [pltpu.VMEM((2, rows, LANES), BF16)] * 2
-            + key_scratch(slots)
-            + [pltpu.VMEM((LANES, rows), F32), pltpu.VMEM((all_rows, LANES), F32)],
+            scratch_shapes=[pltpu.VMEM((2, rows, LANES), BF16)] * 2
+            + [pltpu.VMEM((2, LANES, rows), F32)],
         ),
         out_shape=[whole, half_part, whole, half_part,
                    jax.ShapeDtypeStruct((all_rows, steps * span), BF16)],
@@ -315,10 +289,16 @@
     def features(value, at, count):
         return lax.dynamic_slice_in_dim(value, at, count, value.ndim - 1)
 
-    both = lax.all_gather(jnp.stack([queries, grad_out]), "core", axis=1, tiled=True)
+    own = []
+    for part in range(PARTS):
+        cuts = [
+            lax.slice_in_dim(value, c * half + part * span, c * half + (part + 1) * span, axis=1)
+            for c in range(2) for value in (queries, grad_out)
+        ]
+        own.append(jnp.concatenate(cuts, axis=0).reshape(2, 2, queries.shape[0], span))
     gathered = (
-        gather_x_then_z(features(both, core * half, span), x_size),
-        gather_z_then_x(features(both, core * half + span, span), x_size, z_size),
+        gather_x_then_z(own[0], x_size),
+        gather_z_then_x(own[1], x_size, z_size),
     )
     sib_k = swap_cores(features(keys, (1 - core) * half, half))
     sib_v = swap_cores(features(values, (1 - core) * half, half))

time: 204 us -> 217 us (1.064)
  starting transfers between devices: 48.1 us -> 30.9 us
  waiting for transfers between devices: 14.1 us -> 28.6 us
  Pallas kernels: 36.6 us -> 48.5 us
    ppermute x8, starting transfers between devices: 25.1 us -> 12.9 us  [swap_cores(): return lax.ppermute(value, 'core', [(0, 1), (1, 0)])]
    all_to_all x2, blocking collectives: 34.1 us -> 41.6 us  [across(): return lax.all_to_all(flat, axes, 0, 0, tiled=True).reshape(value.shape)]
    pallas_call x2, Pallas kernels: 21.6 us -> 28.9 us  [gradients(): pl.pallas_call(functools.partial(grads_kernel, part == 0), grid_spec=pltp...]
    all_to_all x2, waiting for transfers between devices: 11.7 us -> 18.4 us  [per_device(): lax.all_to_all(dq.reshape(chips, held, span), CHIP, 0, 0, tiled=True)]
    all_to_all x1, waiting for transfers between devices: 0.01 us -> 6.07 us  [gather_z_then_x(): return lax.all_to_all(repeated(column, x_size), 'x', 0, 0, tiled=True)]
    all_to_all x1, blocking collectives: 19.6 us -> 14.4 us  [per_device(): stats = lax.all_to_all(stats[0], CHIP, 0, 0, tiled=True)]
    all_to_all x2, starting transfers between devices: 18.5 us -> 13.5 us  [per_device(): lax.all_to_all(dq.reshape(chips, held, span), CHIP, 0, 0, tiled=True)]
    pallas_call x2, Pallas kernels: 13.1 us -> 17.6 us  [row_stats(): pl.pallas_call(functools.partial(stats_kernel, part == 0), grid_spec=pltp...]
  transfers between devices with their start and end apart: 12 -> 12, of which waited for: 5 -> 6; matrix products, arithmetic and copies ran while one was open for 8% -> 8% of each run, Pallas kernels for 9% -> 11%
where the time goes in v4:
time: 217 us; the launch traced here: 214 us
  blocking collectives  71.7 us (33%)
  Pallas kernels  48.5 us (22%)
  starting transfers between devices  30.9 us (14%)
  waiting for transfers between devices  28.6 us (13%)
  local copies, waits for them, and re-layouts  16.2 us (7%)
  between operations  15.5 us (7%)
  other arithmetic  2.29 us (1%)
    all_to_all x2, blocking collectives, across(): return lax.all_to_all(flat, axes, 0, 0, tiled=True).reshape(value.shape)  41.6 us
    pallas_call x2, Pallas kernels, gradients(): pl.pallas_call(functools.partial(grads_kernel, part == 0), grid_spec=pltp...  28.9 us
    all_to_all x2, waiting for transfers between devices, per_device(): lax.all_to_all(dq.reshape(chips, held, span), CHIP, 0, 0, tiled=True)  18.4 us
    pallas_call x2, Pallas kernels, row_stats(): pl.pallas_call(functools.partial(stats_kernel, part == 0), grid_spec=pltp...  17.6 us
    all_to_all x1, blocking collectives, per_device(): stats = lax.all_to_all(merge_stats(stats), CHIP, 0, 0, tiled=True)  15.7 us
    all_to_all x1, blocking collectives, per_device(): stats = lax.all_to_all(stats[0], CHIP, 0, 0, tiled=True)  14.4 us
    all_to_all x2, starting transfers between devices, per_device(): lax.all_to_all(dq.reshape(chips, held, span), CHIP, 0, 0, tiled=True)  13.5 us
    ppermute x8, starting transfers between devices, swap_cores(): return lax.ppermute(value, 'core', [(0, 1), (1, 0)])  12.9 us
  transfers between devices with their start and end apart: 12, of which 6 were waited for; matrix products, arithmetic and copies ran while one was open for 8% of the time, Pallas kernels for 11%

profile of v4, /device:TPU:25, one launch (start us, length us, event | category | flops | bytes accessed | tf_op | source)
XLA Modules:
  0.0 213.6 jit_solution(15178561467007046267)
XLA Ops:
  7.2 0.0 all-gather.2.cloned.1.call-start
  7.2 0.8 fusion.2
  8.0 0.8 fusion.3
  8.8 11.4 %all_to_all.35 = bf16[8,2,16,512]{3,2,1,0:T(8,128)(2,1)} all-to-all(bf16[8,2,16,512]{3,2,1,0:T(8,128)(2,1)S(1)} %bitcast.37), channel_id=1, replica_groups=mesh['group'=4,'x'=4,'z'=8,'core'=2] {'x','core'}, dimensions={0} | all-to-all | bytes 524288 | tf_op jit(solution)/shard_map/all_to_all | solution.py:30
  20.2 0.0 all-gather.2.cloned.1.call-update
  20.2 0.1 broadcast_in_dim.38
  20.3 30.2 %all_to_all.36 = bf16[16,2,16,512]{3,2,1,0:T(8,128)(2,1)S(1)} all-to-all(bf16[16,2,16,512]{3,2,1,0:T(8,128)(2,1)S(1)} %bitcast.34), channel_id=1, replica_groups=mesh['group'=4,'x'=4,'z'=8,'core'=2] {'z','core'}, dimensions={0} | all-to-all | bytes 1048576 | tf_op jit(solution)/shard_map/all_to_all | solution.py:30
  50.4 1.6 broadcast_in_dim.40
  52.0 4.5 %all-to-all-start.2 = ((bf16[4,8,2,2,16,512]{5,4,3,2,1,0:T(8,128)(2,1)}), bf16[4,8,2,2,16,512]{5,4,3,2,1,0:T(8,128)(2,1)}, u32[]{:S(2)}, u32[]{:S(2)}) async-start(bf16[4,8,2,2,16,512]{5,4,3,2,1,0:T(8,128)(2,1)} %broadcast_in_dim.40), calls=%async_computation.2 | async-start | bytes 4194304 | tf_op jit(solution)/shard_map/all_to_all | solution.py:40
  56.5 0.0 copy-start
  56.5 2.5 %dynamic-slice_bitcast_fusion = bf16[512,1024]{1,0:T(8,128)(2,1)} fusion(bf16[1,512,2048]{2,1,0:T(8,128)(2,1)} %param.8, s32[]{:T(128)S(6)} %select_n.25), kind=kLoop, calls=%fused_computation | loop fusion | bytes 2097156 | tf_op jit(solution)/shard_map/dynamic_slice | solution.py:290
  59.0 0.0 collective-permute-start.2
  59.0 1.1 dynamic-slice_bitcast_fusion.1
  60.0 0.5 collective-permute-start.1
  61.8 0.1 pad_add_fusion
  61.9 0.0 collective-permute-start
  62.0 1.1 collective-permute-done
  63.1 0.6 fusion.4
  63.7 1.4 stack.7.info
  65.1 0.0 collective-permute-done.2.sib_v
  65.1 0.0 collective-permute-done.1.sib_k
  65.1 2.0 all-gather.2.cloned.1.call-done.q_ref.g_ref
  67.1 8.8 %row_stats.2.rest_0_ = f32[32,8,256]{2,1,0:T(8,128)S(1)} custom-call(s32[5]{0:T(128)S(1)} %stack.7.info, bf16[512,2048]{1,0:T(8,128)(2,1)S(1)} %bitcast.27, bf16[512,1024]{1,0:T(8,128)(2,1)} %collective-permute-done.1.sib_k, bf16[512,2048]{1,0:T(8,128)(2,1)} %bitcast.29, bf16[512,1024]{1,0:T(8,128)(2,1)S(1)} %collective-permute-done.2.sib_v, ...), custom_call_target="tpu_custom_call" | custom-call | flops 1073741824 | bytes 5242880 | tf_op jit(solution)/shard_map/row_stats/pallas_call | solution.py:215
  75.9 6.1 %all-to-all-done.2.q_ref.g_ref = bf16[4,8,2,2,16,512]{5,4,3,2,1,0:T(8,128)(2,1)} async-done(((bf16[4,8,2,2,16,512]{5,4,3,2,1,0:T(8,128)(2,1)}), bf16[4,8,2,2,16,512]{5,4,3,2,1,0:T(8,128)(2,1)}, u32[]{:S(2)}, u32[]{:S(2)}) %all-to-all-start.2) | async-done | bytes 2097184 | tf_op jit(solution)/shard_map/all_to_all | solution.py:40
  82.0 8.8 %row_stats.3 = f32[32,8,256]{2,1,0:T(8,128)S(1)} custom-call(s32[5]{0:T(128)S(1)} %stack.7.info, bf16[512,2048]{1,0:T(8,128)(2,1)S(1)} %bitcast.28, bf16[512,1024]{1,0:T(8,128)(2,1)} %collective-permute-done.1.sib_k, bf16[512,2048]{1,0:T(8,128)(2,1)} %bitcast.30, bf16[512,1024]{1,0:T(8,128)(2,1)S(1)} %collective-permute-done.2.sib_v, ...), custom_call_target="tpu_custom_call", output_to_operand_aliasing={{}: (7, {})} | custom-call | flops 1073741824 | bytes 5242880 | tf_op jit(solution)/shard_map/row_stats/pallas_call | solution.py:215
  90.8 14.4 %all_to_all.37.in_ref = f32[32,8,256]{2,1,0:T(8,128)} all-to-all(f32[32,8,256]{2,1,0:T(8,128)S(1)} %row_stats.3), channel_id=1, replica_groups=mesh['group'=4,'x'=4,'z'=8,'core'=2] {'x','z'}, dimensions={0} | all-to-all | bytes 524288 | tf_op jit(solution)/shard_map/all_to_all | solution.py:311
  105.2 2.0 merge_stats.1
  107.2 15.7 %all_to_all.38.st_ref = f32[32,8,256]{2,1,0:T(8,128)S(1)} all-to-all(f32[32,8,256]{2,1,0:T(8,128)} %merge_stats.1), channel_id=1, replica_groups=mesh['group'=4,'x'=4,'z'=8,'core'=2] {'x','z'}, dimensions={0} | all-to-all | bytes 524288 | tf_op jit(solution)/shard_map/all_to_all | solution.py:312
  122.9 14.4 %gradients.2 = (bf16[512,2048]{1,0:T(8,128)(2,1)}, bf16[512,512]{1,0:T(8,128)(2,1)S(1)}, bf16[512,2048]{1,0:T(8,128)(2,1)}, bf16[512,512]{1,0:T(8,128)(2,1)S(1)}, bf16[1024,512]{1,0:T(8,128)(2,1)}) custom-call(s32[5]{0:T(128)S(1)} %stack.7.info, bf16[512,2048]{1,0:T(8,128)(2,1)} %bitcast.25, bf16[512,1024]{1,0:T(8,128)(2,1)} %collective-permute-done.1.sib_k, ...), custom_call_target="tpu_custom_call" | custom-call | flops 2684354560 | bytes 8388608 | tf_op jit(solution)/shard_map/gradients/pallas_call | solution.py:255
  137.3 6.1 %all-to-all-start.5 = ((bf16[32,32,512]{2,1,0:T(8,128)(2,1)}), bf16[32,32,512]{2,1,0:T(8,128)(2,1)}, u32[]{:S(2)}, u32[]{:S(2)}) async-start(bf16[32,32,512]{2,1,0:T(8,128)(2,1)} %bitcast.11), calls=%async_computation.5 | async-start | bytes 2097152 | tf_op jit(solution)/shard_map/all_to_all | solution.py:321
  143.4 14.5 %gradients.3 = (bf16[512,2048]{1,0:T(8,128)(2,1)}, bf16[512,512]{1,0:T(8,128)(2,1)S(1)}, bf16[512,2048]{1,0:T(8,128)(2,1)}, bf16[512,512]{1,0:T(8,128)(2,1)S(1)}, bf16[1024,512]{1,0:T(8,128)(2,1)}) custom-call(s32[5]{0:T(128)S(1)} %stack.7.info, bf16[512,2048]{1,0:T(8,128)(2,1)} %bitcast.26, ...), custom_call_target="tpu_custom_call", output_to_operand_aliasing={{0}: (8, {}), {2}: (9, {})} | custom-call | flops 2684354560 | bytes 8388608 | tf_op jit(solution)/shard_map/gradients/pallas_call | solution.py:255
  157.9 9.1 %all-to-all-done.5 = bf16[32,32,512]{2,1,0:T(8,128)(2,1)} async-done(((bf16[32,32,512]{2,1,0:T(8,128)(2,1)}), bf16[32,32,512]{2,1,0:T(8,128)(2,1)}, u32[]{:S(2)}, u32[]{:S(2)}) %all-to-all-start.5) | async-done | bytes 1048608 | tf_op jit(solution)/shard_map/all_to_all | solution.py:321
  167.0 7.4 %all-to-all-start.6 = ((bf16[32,32,512]{2,1,0:T(8,128)(2,1)}), bf16[32,32,512]{2,1,0:T(8,128)(2,1)S(1)}, u32[]{:S(2)}, u32[]{:S(2)}) async-start(bf16[32,32,512]{2,1,0:T(8,128)(2,1)} %bitcast.12), calls=%async_computation.6 | async-start | bytes 2097152 | tf_op jit(solution)/shard_map/all_to_all | solution.py:321
  174.4 3.6 %collective-permute-start.4 = (bf16[512,512]{1,0:T(8,128)(2,1)S(1)}, bf16[512,512]{1,0:T(8,128)(2,1)}, u32[]{:S(2)}, u32[]{:S(2)}) collective-permute-start(bf16[512,512]{1,0:T(8,128)(2,1)S(1)} %copy-done.2), channel_id=1, source_target_pairs={{0,1},{1,0},{2,3},{3,2},{4,5},{5,4},{6,7},{7,6},{8,9},{9,8},{10,11... | collective-permute-start | bytes 1572872 | tf_op jit(solution)/shard_map/ppermute | solution.py:21
  178.0 0.1 collective-permute-start.6
  178.1 0.4 collective-permute-start.5
  178.5 0.1 collective-permute-start.7
  178.6 1.1 collective-permute-done.4
  179.6 1.9 bitcast_dynamic-update-slice_fusion.3
  181.5 1.9 bitcast_dynamic-update-slice_fusion.1
  183.4 0.0 collective-permute-done.5
  183.4 1.9 bitcast_dynamic-update-slice_fusion.2
  185.2 1.4 reduce_sum.24
  186.6 9.3 %all-to-all-done.6 = bf16[32,32,512]{2,1,0:T(8,128)(2,1)S(1)} async-done(((bf16[32,32,512]{2,1,0:T(8,128)(2,1)}), bf16[32,32,512]{2,1,0:T(8,128)(2,1)S(1)}, u32[]{:S(2)}, u32[]{:S(2)}) %all-to-all-start.6) | async-done | bytes 1048608 | tf_op jit(solution)/shard_map/all_to_all | solution.py:321
  195.9 0.2 reduce_sum.25
  196.1 8.2 %collective-permute-start.3 = (bf16[16,1024]{1,0:T(8,128)(2,1)S(1)}, bf16[16,1024]{1,0:T(8,128)(2,1)S(1)}, u32[]{:S(2)}, u32[]{:S(2)}) collective-permute-start(bf16[16,1024]{1,0:T(8,128)(2,1)S(1)} %get-tuple-element.24), channel_id=1, source_target_pairs={{0,1},{1,0},{2,3},{3,2},{4,5},{5,4},{6,7},{7,6},{8,9},{9,8},{10,11... | collective-permute-start | bytes 98312 | tf_op jit(solution)/shard_map/ppermute | solution.py:21
  204.3 1.9 bitcast_dynamic-update-slice_fusion
  206.1 0.6 maximum_select_fusion
  (11 shorter events, 0.1 us)
Async XLA Ops:
  7.2 60.0 %all-gather.2.cloned.1.call-start = ((), (), s32[]{:S(2)}) async-start(), calls=%async_computation.7 | async-start | bytes 2359296 | tf_op jit(solution)/shard_map/all_gather | solution.py:35
  52.0 29.9 %all-to-all-start.2 = ((bf16[4,8,2,2,16,512]{5,4,3,2,1,0:T(8,128)(2,1)}), bf16[4,8,2,2,16,512]{5,4,3,2,1,0:T(8,128)(2,1)}, u32[]{:S(2)}, u32[]{:S(2)}) async-start(bf16[4,8,2,2,16,512]{5,4,3,2,1,0:T(8,128)(2,1)} %broadcast_in_dim.40), calls=%async_computation.2 | async-start | bytes 4194304 | tf_op jit(solution)/shard_map/all_to_all | solution.py:40
  56.5 2.5 %copy-start = (bf16[1,512,2048]{2,1,0:T(8,128)(2,1)S(1)}, bf16[1,512,2048]{2,1,0:T(8,128)(2,1)}, u32[]{:S(2)}) copy-start(bf16[1,512,2048]{2,1,0:T(8,128)(2,1)} %param.7) | copy-start | bytes 6291460
  59.0 6.2 %collective-permute-start.2 = (bf16[512,1024]{1,0:T(8,128)(2,1)}, bf16[512,1024]{1,0:T(8,128)(2,1)S(1)}, u32[]{:S(2)}, u32[]{:S(2)}) collective-permute-start(bf16[512,1024]{1,0:T(8,128)(2,1)} %dynamic-slice_bitcast_fusion), channel_id=1, source_target_pairs={{0,1},{1,0},{2,3},{3,2},{4,5},{5,4},{6,7},{7,6},{8,9},{9,8},{10,11... | collective-permute-start | bytes 3145736 | tf_op jit(solution)/shard_map/ppermute | solution.py:21
  60.0 5.1 %collective-permute-start.1 = (bf16[512,1024]{1,0:T(8,128)(2,1)}, bf16[512,1024]{1,0:T(8,128)(2,1)}, u32[]{:S(2)}, u32[]{:S(2)}) collective-permute-start(bf16[512,1024]{1,0:T(8,128)(2,1)} %dynamic-slice_bitcast_fusion.1), channel_id=1, source_target_pairs={{0,1},{1,0},{2,3},{3,2},{4,5},{5,4},{6,7},{7,6},{8,9},{9,8},{10,11... | collective-permute-start | bytes 3145736 | tf_op jit(solution)/shard_map/ppermute | solution.py:21
  61.9 1.2 collective-permute-start
  137.3 6.1 %copy-start.1 = (bf16[512,512]{1,0:T(8,128)(2,1)}, bf16[512,512]{1,0:T(8,128)(2,1)S(1)}, u32[]{:S(2)}) copy-start(bf16[512,512]{1,0:T(8,128)(2,1)S(1)} %get-tuple-element.18) | copy-start | bytes 1572868
  137.3 29.6 %all-to-all-start.5 = ((bf16[32,32,512]{2,1,0:T(8,128)(2,1)}), bf16[32,32,512]{2,1,0:T(8,128)(2,1)}, u32[]{:S(2)}, u32[]{:S(2)}) async-start(bf16[32,32,512]{2,1,0:T(8,128)(2,1)} %bitcast.11), calls=%async_computation.5 | async-start | bytes 2097152 | tf_op jit(solution)/shard_map/all_to_all | solution.py:321
  157.9 16.5 %copy-start.2 = (bf16[512,512]{1,0:T(8,128)(2,1)S(1)}, bf16[512,512]{1,0:T(8,128)(2,1)}, u32[]{:S(2)}) copy-start(bf16[512,512]{1,0:T(8,128)(2,1)} %copy-done.1) | copy-start | bytes 1572868
  167.0 28.9 %all-to-all-start.6 = ((bf16[32,32,512]{2,1,0:T(8,128)(2,1)}), bf16[32,32,512]{2,1,0:T(8,128)(2,1)S(1)}, u32[]{:S(2)}, u32[]{:S(2)}) async-start(bf16[32,32,512]{2,1,0:T(8,128)(2,1)} %bitcast.12), calls=%async_computation.6 | async-start | bytes 2097152 | tf_op jit(solution)/shard_map/all_to_all | solution.py:321
  174.4 5.2 %collective-permute-start.4 = (bf16[512,512]{1,0:T(8,128)(2,1)S(1)}, bf16[512,512]{1,0:T(8,128)(2,1)}, u32[]{:S(2)}, u32[]{:S(2)}) collective-permute-start(bf16[512,512]{1,0:T(8,128)(2,1)S(1)} %copy-done.2), channel_id=1, source_target_pairs={{0,1},{1,0},{2,3},{3,2},{4,5},{5,4},{6,7},{7,6},{8,9},{9,8},{10,11... | collective-permute-start | bytes 1572872 | tf_op jit(solution)/shard_map/ppermute | solution.py:21
  178.0 3.5 %collective-permute-start.6 = (bf16[512,512]{1,0:T(8,128)(2,1)S(1)}, bf16[512,512]{1,0:T(8,128)(2,1)}, u32[]{:S(2)}, u32[]{:S(2)}) collective-permute-start(bf16[512,512]{1,0:T(8,128)(2,1)S(1)} %get-tuple-element.21), channel_id=1, source_target_pairs={{0,1},{1,0},{2,3},{3,2},{4,5},{5,4},{6,7},{7,6},{8,9},{9,8},{10,11... | collective-permute-start | bytes 1572872 | tf_op jit(solution)/shard_map/ppermute | solution.py:21
  178.1 5.3 %collective-permute-start.5 = (bf16[512,512]{1,0:T(8,128)(2,1)S(1)}, bf16[512,512]{1,0:T(8,128)(2,1)}, u32[]{:S(2)}, u32[]{:S(2)}) collective-permute-start(bf16[512,512]{1,0:T(8,128)(2,1)S(1)} %get-tuple-element.19), channel_id=1, source_target_pairs={{0,1},{1,0},{2,3},{3,2},{4,5},{5,4},{6,7},{7,6},{8,9},{9,8},{10,11... | collective-permute-start | bytes 1572872 | tf_op jit(solution)/shard_map/ppermute | solution.py:21
  178.5 25.8 %collective-permute-start.7 = (bf16[512,512]{1,0:T(8,128)(2,1)S(1)}, bf16[512,512]{1,0:T(8,128)(2,1)}, u32[]{:S(2)}, u32[]{:S(2)}) collective-permute-start(bf16[512,512]{1,0:T(8,128)(2,1)S(1)} %get-tuple-element.22), channel_id=1, source_target_pairs={{0,1},{1,0},{2,3},{3,2},{4,5},{5,4},{6,7},{7,6},{8,9},{9,8},{10,11... | collective-permute-start | bytes 1572872 | tf_op jit(solution)/shard_map/ppermute | solution.py:21
  196.1 10.1 %collective-permute-start.3 = (bf16[16,1024]{1,0:T(8,128)(2,1)S(1)}, bf16[16,1024]{1,0:T(8,128)(2,1)S(1)}, u32[]{:S(2)}, u32[]{:S(2)}) collective-permute-start(bf16[16,1024]{1,0:T(8,128)(2,1)S(1)} %get-tuple-element.24), channel_id=1, source_target_pairs={{0,1},{1,0},{2,3},{3,2},{4,5},{5,4},{6,7},{7,6},{8,9},{9,8},{10,11... | collective-permute-start | bytes 98312 | tf_op jit(solution)/shard_map/ppermute | solution.py:21
Sparse Core Ops, SparseCore 0:
  20.3 46.7 all-gather.1

commit v5 on v4

--- a/solution.py
+++ b/solution.py
@@ -25,18 +25,13 @@
     return jnp.broadcast_to(value[None], (count,) + value.shape)
 
 
-def across(value, axes):
-    flat = value.reshape((-1,) + value.shape[2:])
-    return lax.all_to_all(flat, axes, 0, 0, tiled=True).reshape(value.shape)
-
-
 def gather_x_then_z(value, x_size):
-    columns = across(repeated(value, x_size), ("x", "core"))
+    columns = lax.all_to_all(repeated(value, x_size), "x", 0, 0, tiled=True)
     return lax.all_gather(columns, "z", axis=0, tiled=False)
 
 
 def gather_z_then_x(value, x_size, z_size):
-    column = across(repeated(value, z_size), ("z", "core"))
+    column = lax.all_to_all(repeated(value, z_size), "z", 0, 0, tiled=True)
     return lax.all_to_all(repeated(column, x_size), "x", 0, 0, tiled=True)
 
 
@@ -289,13 +284,10 @@
     def features(value, at, count):
         return lax.dynamic_slice_in_dim(value, at, count, value.ndim - 1)
 
-    own = []
-    for part in range(PARTS):
-        cuts = [
-            lax.slice_in_dim(value, c * half + part * span, c * half + (part + 1) * span, axis=1)
-            for c in range(2) for value in (queries, grad_out)
-        ]
-        own.append(jnp.concatenate(cuts, axis=0).reshape(2, 2, queries.shape[0], span))
+    both = lax.all_gather(jnp.stack([queries, grad_out]), "core", axis=0, tiled=False)
+    own = [
+        lax.dynamic_slice_in_dim(both, core * half + part * span, span, 3) for part in range(PARTS)
+    ]
     gathered = (
         gather_x_then_z(own[0], x_size),
         gather_z_then_x(own[1], x_size, z_size),

time: 217 us -> 203 us (0.935)
  Pallas kernels: 48.5 us -> 29.5 us
  starting transfers between devices: 30.9 us -> 48.2 us
  waiting for transfers between devices: 28.6 us -> 17.1 us
    pallas_call x2, Pallas kernels: 28.9 us -> 16.1 us  [gradients(): pl.pallas_call(functools.partial(grads_kernel, part == 0), grid_spec=pltp...]
    ppermute x8, starting transfers between devices: 12.9 us -> 24.5 us  [swap_cores(): return lax.ppermute(value, 'core', [(0, 1), (1, 0)])]
    all_to_all x2, blocking collectives: 41.6 us -> 34.1 us  [the longest x1 24.4 us: gather_z_then_x(): column = lax.all_to_all(repeated(value, z_size), 'z', 0, 0, tiled=True)]
    all_to_all x1, blocking collectives: 14.4 us -> 21.3 us  [per_device(): stats = lax.all_to_all(stats[0], CHIP, 0, 0, tiled=True)]
    pallas_call x2, Pallas kernels: 17.6 us -> 11.4 us  [row_stats(): pl.pallas_call(functools.partial(stats_kernel, part == 0), grid_spec=pltp...]
    all_to_all x1, waiting for transfers between devices: 6.07 us -> 0.01 us  [gather_z_then_x(): return lax.all_to_all(repeated(column, x_size), 'x', 0, 0, tiled=True)]
    all_to_all x2, starting transfers between devices: 13.5 us -> 19.2 us  [per_device(): lax.all_to_all(dq.reshape(chips, held, span), CHIP, 0, 0, tiled=True)]
    all_to_all x2, waiting for transfers between devices: 18.4 us -> 14.6 us  [per_device(): lax.all_to_all(dq.reshape(chips, held, span), CHIP, 0, 0, tiled=True)]
  transfers between devices with their start and end apart: 12 -> 12, of which waited for: 6 -> 5; matrix products, arithmetic and copies ran while one was open for 8% -> 8% of each run, Pallas kernels for 11% -> 7%
where the time goes in v5:
time: 203 us; the launch traced here: 200 us
  blocking collectives  71.9 us (35%)
  starting transfers between devices  48.2 us (24%)
  Pallas kernels  29.5 us (15%)
  waiting for transfers between devices  17.1 us (8%)
  between operations  15.5 us (8%)
  local copies, waits for them, and re-layouts  14.5 us (7%)
  other arithmetic  3.16 us (2%)
    ppermute x8, starting transfers between devices, swap_cores(): return lax.ppermute(value, 'core', [(0, 1), (1, 0)])  24.5 us
    all_to_all x1, blocking collectives, gather_z_then_x(): column = lax.all_to_all(repeated(value, z_size), 'z', 0, 0, tiled=True)  24.4 us
    all_to_all x1, blocking collectives, per_device(): stats = lax.all_to_all(stats[0], CHIP, 0, 0, tiled=True)  21.3 us
    all_to_all x2, starting transfers between devices, per_device(): lax.all_to_all(dq.reshape(chips, held, span), CHIP, 0, 0, tiled=True)  19.2 us
    pallas_call x2, Pallas kernels, gradients(): pl.pallas_call(functools.partial(grads_kernel, part == 0), grid_spec=pltp...  16.1 us
    all_to_all x2, waiting for transfers between devices, per_device(): lax.all_to_all(dq.reshape(chips, held, span), CHIP, 0, 0, tiled=True)  14.6 us
    all_to_all x1, blocking collectives, per_device(): stats = lax.all_to_all(merge_stats(stats), CHIP, 0, 0, tiled=True)  14.2 us
    pallas_call x2, Pallas kernels, row_stats(): pl.pallas_call(functools.partial(stats_kernel, part == 0), grid_spec=pltp...  11.4 us
  transfers between devices with their start and end apart: 12, of which 5 were waited for; matrix products, arithmetic and copies ran while one was open for 8% of the time, Pallas kernels for 7%

profile of v5, /device:TPU:25, one launch (start us, length us, event | category | flops | bytes accessed | tf_op | source)
XLA Modules:
  0.0 199.8 jit_solution(10811197578938331738)
XLA Ops:
  7.2 0.0 all-gather.4.cloned.1.call-start
  7.2 0.9 pad_maximum_fusion
  8.1 2.3 %all-gather = bf16[4,16,2048]{2,1,0:T(8,128)(2,1)S(1)} all-gather(bf16[2,16,2048]{2,1,0:T(8,128)(2,1)S(1)} %pad_maximum_fusion), channel_id=2, replica_groups=mesh['group'=4,'x'=4,'z'=8,'core'=2] {'core'}, dimensions={0}, use_global_device_ids=true | all-gather | bytes 393216 | tf_op jit(solution)/shard_map/all_gather | solution.py:287
  10.5 9.7 %all_to_all.35 = bf16[4,2,2,16,512]{4,3,2,1,0:T(8,128)(2,1)} all-to-all(bf16[4,2,2,16,512]{4,3,2,1,0:T(8,128)(2,1)S(1)} %broadcast_in_dim.32), channel_id=1, replica_groups=mesh['group'=4,'x'=4,'z'=8,'core'=2] {'x'}, dimensions={0} | all-to-all | bytes 524288 | tf_op jit(solution)/shard_map/all_to_all | solution.py:29
  20.2 0.0 all-gather.4.cloned.1.call-update
  20.2 0.1 broadcast_in_dim.33
  20.3 24.4 %all_to_all.36 = bf16[8,2,2,16,512]{4,3,2,1,0:T(8,128)(2,1)S(1)} all-to-all(bf16[8,2,2,16,512]{4,3,2,1,0:T(8,128)(2,1)S(1)} %broadcast_in_dim.33), channel_id=1, replica_groups=mesh['group'=4,'x'=4,'z'=8,'core'=2] {'z'}, dimensions={0} | all-to-all | bytes 1048576 | tf_op jit(solution)/shard_map/all_to_all | solution.py:34
  44.6 1.6 broadcast_in_dim.34
  46.2 4.5 %all-to-all-start.2 = ((bf16[4,8,2,2,16,512]{5,4,3,2,1,0:T(8,128)(2,1)}), bf16[4,8,2,2,16,512]{5,4,3,2,1,0:T(8,128)(2,1)}, u32[]{:S(2)}, u32[]{:S(2)}) async-start(bf16[4,8,2,2,16,512]{5,4,3,2,1,0:T(8,128)(2,1)} %broadcast_in_dim.34), calls=%async_computation.2 | async-start | bytes 4194304 | tf_op jit(solution)/shard_map/all_to_all | solution.py:35
  50.7 0.0 copy-start
  50.7 2.5 %dynamic-slice_bitcast_fusion = bf16[512,1024]{1,0:T(8,128)(2,1)} fusion(bf16[1,512,2048]{2,1,0:T(8,128)(2,1)} %param.8, s32[]{:T(128)S(6)} %select_n.31), kind=kLoop, calls=%fused_computation | loop fusion | bytes 2097156 | tf_op jit(solution)/shard_map/dynamic_slice | solution.py:285
  53.2 6.6 %collective-permute-start.2 = (bf16[512,1024]{1,0:T(8,128)(2,1)}, bf16[512,1024]{1,0:T(8,128)(2,1)S(1)}, u32[]{:S(2)}, u32[]{:S(2)}) collective-permute-start(bf16[512,1024]{1,0:T(8,128)(2,1)} %dynamic-slice_bitcast_fusion), channel_id=1, source_target_pairs={{0,1},{1,0},{2,3},{3,2},{4,5},{5,4},{6,7},{7,6},{8,9},{9,8},{10,11... | collective-permute-start | bytes 3145736 | tf_op jit(solution)/shard_map/ppermute | solution.py:21
  59.8 1.1 dynamic-slice_bitcast_fusion.1
  60.9 0.0 collective-permute-start.1
  62.2 0.1 pad_add_fusion
  62.3 0.5 collective-permute-start
  62.8 0.8 collective-permute-done
  63.6 0.6 fusion.2
  64.2 1.3 stack.16.info
  65.5 0.0 collective-permute-done.2.sib_v
  65.5 0.0 collective-permute-done.1.sib_k
  65.5 0.5 all-gather.4.cloned.1.call-done
  66.0 5.7 %row_stats.2.rest_0_ = f32[32,8,256]{2,1,0:T(8,128)S(1)} custom-call(s32[5]{0:T(128)S(1)} %stack.16.info, bf16[512,2048]{1,0:T(8,128)(2,1)S(1)} %bitcast.25, bf16[512,1024]{1,0:T(8,128)(2,1)} %collective-permute-done.1.sib_k, bf16[512,2048]{1,0:T(8,128)(2,1)} %bitcast.27, bf16[512,1024]{1,0:T(8,128)(2,1)S(1)} %collective-permute-done.2.sib_v, ...), custom_call_target="tpu_custom_call" | custom-call | flops 1073741824 | bytes 5242880 | tf_op jit(solution)/shard_map/row_stats/pallas_call | solution.py:210
  71.7 5.7 %row_stats.3 = f32[32,8,256]{2,1,0:T(8,128)S(1)} custom-call(s32[5]{0:T(128)S(1)} %stack.16.info, bf16[512,2048]{1,0:T(8,128)(2,1)S(1)} %bitcast.26, bf16[512,1024]{1,0:T(8,128)(2,1)} %collective-permute-done.1.sib_k, bf16[512,2048]{1,0:T(8,128)(2,1)} %bitcast.28, ...), custom_call_target="tpu_custom_call", output_to_operand_aliasing={{}: (7, {})} | custom-call | flops 1073741824 | bytes 5242880 | tf_op jit(solution)/shard_map/row_stats/pallas_call | solution.py:210
  77.4 21.3 %all_to_all.37.in_ref = f32[32,8,256]{2,1,0:T(8,128)} all-to-all(f32[32,8,256]{2,1,0:T(8,128)S(1)} %row_stats.3), channel_id=1, replica_groups=mesh['group'=4,'x'=4,'z'=8,'core'=2] {'x','z'}, dimensions={0} | all-to-all | bytes 524288 | tf_op jit(solution)/shard_map/all_to_all | solution.py:303
  98.7 2.0 merge_stats.1
  100.7 14.2 %all_to_all.38.st_ref = f32[32,8,256]{2,1,0:T(8,128)S(1)} all-to-all(f32[32,8,256]{2,1,0:T(8,128)} %merge_stats.1), channel_id=1, replica_groups=mesh['group'=4,'x'=4,'z'=8,'core'=2] {'x','z'}, dimensions={0} | all-to-all | bytes 524288 | tf_op jit(solution)/shard_map/all_to_all | solution.py:304
  114.9 8.0 %gradients.2 = (bf16[512,2048]{1,0:T(8,128)(2,1)}, bf16[512,512]{1,0:T(8,128)(2,1)S(1)}, bf16[512,2048]{1,0:T(8,128)(2,1)}, bf16[512,512]{1,0:T(8,128)(2,1)S(1)}, bf16[1024,512]{1,0:T(8,128)(2,1)}) custom-call(s32[5]{0:T(128)S(1)} %stack.16.info, bf16[512,2048]{1,0:T(8,128)(2,1)} %bitcast.23, bf16[512,1024]{1,0:T(8,128)(2,1)} %collective-permute-done.1.sib_k, ...), custom_call_target="tpu_custom_call" | custom-call | flops 2684354560 | bytes 8388608 | tf_op jit(solution)/shard_map/gradients/pallas_call | solution.py:250
  122.9 11.0 %all-to-all-start.5 = ((bf16[32,32,512]{2,1,0:T(8,128)(2,1)}), bf16[32,32,512]{2,1,0:T(8,128)(2,1)}, u32[]{:S(2)}, u32[]{:S(2)}) async-start(bf16[32,32,512]{2,1,0:T(8,128)(2,1)} %bitcast.9), calls=%async_computation.5 | async-start | bytes 2097152 | tf_op jit(solution)/shard_map/all_to_all | solution.py:313
  134.0 8.1 %gradients.3 = (bf16[512,2048]{1,0:T(8,128)(2,1)}, bf16[512,512]{1,0:T(8,128)(2,1)S(1)}, bf16[512,2048]{1,0:T(8,128)(2,1)}, bf16[512,512]{1,0:T(8,128)(2,1)S(1)}, bf16[1024,512]{1,0:T(8,128)(2,1)}) custom-call(s32[5]{0:T(128)S(1)} %stack.16.info, bf16[512,2048]{1,0:T(8,128)(2,1)} %bitcast.24, ...), custom_call_target="tpu_custom_call", output_to_operand_aliasing={{0}: (8, {}), {2}: (9, {})} | custom-call | flops 2684354560 | bytes 8388608 | tf_op jit(solution)/shard_map/gradients/pallas_call | solution.py:250
  142.1 11.2 %all-to-all-done.5 = bf16[32,32,512]{2,1,0:T(8,128)(2,1)} async-done(((bf16[32,32,512]{2,1,0:T(8,128)(2,1)}), bf16[32,32,512]{2,1,0:T(8,128)(2,1)}, u32[]{:S(2)}, u32[]{:S(2)}) %all-to-all-start.5) | async-done | bytes 1048608 | tf_op jit(solution)/shard_map/all_to_all | solution.py:313
  153.3 8.2 %all-to-all-start.6 = ((bf16[32,32,512]{2,1,0:T(8,128)(2,1)}), bf16[32,32,512]{2,1,0:T(8,128)(2,1)S(1)}, u32[]{:S(2)}, u32[]{:S(2)}) async-start(bf16[32,32,512]{2,1,0:T(8,128)(2,1)} %bitcast.10), calls=%async_computation.6 | async-start | bytes 2097152 | tf_op jit(solution)/shard_map/all_to_all | solution.py:313
  161.5 7.1 %collective-permute-start.4 = (bf16[512,512]{1,0:T(8,128)(2,1)S(1)}, bf16[512,512]{1,0:T(8,128)(2,1)}, u32[]{:S(2)}, u32[]{:S(2)}) collective-permute-start(bf16[512,512]{1,0:T(8,128)(2,1)S(1)} %copy-done.2), channel_id=1, source_target_pairs={{0,1},{1,0},{2,3},{3,2},{4,5},{5,4},{6,7},{7,6},{8,9},{9,8},{10,11... | collective-permute-start | bytes 1572872 | tf_op jit(solution)/shard_map/ppermute | solution.py:21
  168.5 0.1 collective-permute-start.6
  168.6 0.4 collective-permute-start.5
  169.0 0.1 collective-permute-start.7
  169.1 1.1 collective-permute-done.4
  170.2 1.9 bitcast_dynamic-update-slice_fusion.3
  172.1 1.9 bitcast_dynamic-update-slice_fusion.1
  173.9 0.0 collective-permute-done.5
  173.9 1.9 bitcast_dynamic-update-slice_fusion.2
  175.8 1.4 reduce_sum.24
  177.2 3.4 %all-to-all-done.6 = bf16[32,32,512]{2,1,0:T(8,128)(2,1)S(1)} async-done(((bf16[32,32,512]{2,1,0:T(8,128)(2,1)}), bf16[32,32,512]{2,1,0:T(8,128)(2,1)S(1)}, u32[]{:S(2)}, u32[]{:S(2)}) %all-to-all-start.6) | async-done | bytes 1048608 | tf_op jit(solution)/shard_map/all_to_all | solution.py:313
  180.6 0.2 reduce_sum.25
  180.8 9.6 %collective-permute-start.3 = (bf16[16,1024]{1,0:T(8,128)(2,1)S(1)}, bf16[16,1024]{1,0:T(8,128)(2,1)S(1)}, u32[]{:S(2)}, u32[]{:S(2)}) collective-permute-start(bf16[16,1024]{1,0:T(8,128)(2,1)S(1)} %get-tuple-element.26), channel_id=1, source_target_pairs={{0,1},{1,0},{2,3},{3,2},{4,5},{5,4},{6,7},{7,6},{8,9},{9,8},{10,11... | collective-permute-start | bytes 98312 | tf_op jit(solution)/shard_map/ppermute | solution.py:21
  190.4 0.0 collective-permute-done.7
  190.4 1.9 bitcast_dynamic-update-slice_fusion
  192.3 0.6 maximum_select_fusion
  (11 shorter events, 0.1 us)
Async XLA Ops:
  7.2 58.8 %all-gather.4.cloned.1.call-start = ((), (), s32[]{:S(2)}) async-start(), calls=%async_computation.7 | async-start | bytes 2359296 | tf_op jit(solution)/shard_map/all_gather | solution.py:30
  46.2 25.5 %all-to-all-start.2 = ((bf16[4,8,2,2,16,512]{5,4,3,2,1,0:T(8,128)(2,1)}), bf16[4,8,2,2,16,512]{5,4,3,2,1,0:T(8,128)(2,1)}, u32[]{:S(2)}, u32[]{:S(2)}) async-start(bf16[4,8,2,2,16,512]{5,4,3,2,1,0:T(8,128)(2,1)} %broadcast_in_dim.34), calls=%async_computation.2 | async-start | bytes 4194304 | tf_op jit(solution)/shard_map/all_to_all | solution.py:35
  50.7 9.1 %copy-start = (bf16[1,512,2048]{2,1,0:T(8,128)(2,1)S(1)}, bf16[1,512,2048]{2,1,0:T(8,128)(2,1)}, u32[]{:S(2)}) copy-start(bf16[1,512,2048]{2,1,0:T(8,128)(2,1)} %param.7) | copy-start | bytes 6291460
  53.2 12.3 %collective-permute-start.2 = (bf16[512,1024]{1,0:T(8,128)(2,1)}, bf16[512,1024]{1,0:T(8,128)(2,1)S(1)}, u32[]{:S(2)}, u32[]{:S(2)}) collective-permute-start(bf16[512,1024]{1,0:T(8,128)(2,1)} %dynamic-slice_bitcast_fusion), channel_id=1, source_target_pairs={{0,1},{1,0},{2,3},{3,2},{4,5},{5,4},{6,7},{7,6},{8,9},{9,8},{10,11... | collective-permute-start | bytes 3145736 | tf_op jit(solution)/shard_map/ppermute | solution.py:21
  60.9 4.6 %collective-permute-start.1 = (bf16[512,1024]{1,0:T(8,128)(2,1)}, bf16[512,1024]{1,0:T(8,128)(2,1)}, u32[]{:S(2)}, u32[]{:S(2)}) collective-permute-start(bf16[512,1024]{1,0:T(8,128)(2,1)} %dynamic-slice_bitcast_fusion.1), channel_id=1, source_target_pairs={{0,1},{1,0},{2,3},{3,2},{4,5},{5,4},{6,7},{7,6},{8,9},{9,8},{10,11... | collective-permute-start | bytes 3145736 | tf_op jit(solution)/shard_map/ppermute | solution.py:21
  62.3 1.4 collective-permute-start
  122.9 11.1 %copy-start.1 = (bf16[512,512]{1,0:T(8,128)(2,1)}, bf16[512,512]{1,0:T(8,128)(2,1)S(1)}, u32[]{:S(2)}) copy-start(bf16[512,512]{1,0:T(8,128)(2,1)S(1)} %get-tuple-element.18) | copy-start | bytes 1572868
  122.9 30.3 %all-to-all-start.5 = ((bf16[32,32,512]{2,1,0:T(8,128)(2,1)}), bf16[32,32,512]{2,1,0:T(8,128)(2,1)}, u32[]{:S(2)}, u32[]{:S(2)}) async-start(bf16[32,32,512]{2,1,0:T(8,128)(2,1)} %bitcast.9), calls=%async_computation.5 | async-start | bytes 2097152 | tf_op jit(solution)/shard_map/all_to_all | solution.py:313
  142.1 19.4 %copy-start.2 = (bf16[512,512]{1,0:T(8,128)(2,1)S(1)}, bf16[512,512]{1,0:T(8,128)(2,1)}, u32[]{:S(2)}) copy-start(bf16[512,512]{1,0:T(8,128)(2,1)} %copy-done.1) | copy-start | bytes 1572868
  153.3 27.4 %all-to-all-start.6 = ((bf16[32,32,512]{2,1,0:T(8,128)(2,1)}), bf16[32,32,512]{2,1,0:T(8,128)(2,1)S(1)}, u32[]{:S(2)}, u32[]{:S(2)}) async-start(bf16[32,32,512]{2,1,0:T(8,128)(2,1)} %bitcast.10), calls=%async_computation.6 | async-start | bytes 2097152 | tf_op jit(solution)/shard_map/all_to_all | solution.py:313
  161.5 8.7 %collective-permute-start.4 = (bf16[512,512]{1,0:T(8,128)(2,1)S(1)}, bf16[512,512]{1,0:T(8,128)(2,1)}, u32[]{:S(2)}, u32[]{:S(2)}) collective-permute-start(bf16[512,512]{1,0:T(8,128)(2,1)S(1)} %copy-done.2), channel_id=1, source_target_pairs={{0,1},{1,0},{2,3},{3,2},{4,5},{5,4},{6,7},{7,6},{8,9},{9,8},{10,11... | collective-permute-start | bytes 1572872 | tf_op jit(solution)/shard_map/ppermute | solution.py:21
  168.5 3.5 %collective-permute-start.6 = (bf16[512,512]{1,0:T(8,128)(2,1)S(1)}, bf16[512,512]{1,0:T(8,128)(2,1)}, u32[]{:S(2)}, u32[]{:S(2)}) collective-permute-start(bf16[512,512]{1,0:T(8,128)(2,1)S(1)} %get-tuple-element.21), channel_id=1, source_target_pairs={{0,1},{1,0},{2,3},{3,2},{4,5},{5,4},{6,7},{7,6},{8,9},{9,8},{10,11... | collective-permute-start | bytes 1572872 | tf_op jit(solution)/shard_map/ppermute | solution.py:21
  168.6 5.3 %collective-permute-start.5 = (bf16[512,512]{1,0:T(8,128)(2,1)S(1)}, bf16[512,512]{1,0:T(8,128)(2,1)}, u32[]{:S(2)}, u32[]{:S(2)}) collective-permute-start(bf16[512,512]{1,0:T(8,128)(2,1)S(1)} %get-tuple-element.19), channel_id=1, source_target_pairs={{0,1},{1,0},{2,3},{3,2},{4,5},{5,4},{6,7},{7,6},{8,9},{9,8},{10,11... | collective-permute-start | bytes 1572872 | tf_op jit(solution)/shard_map/ppermute | solution.py:21
  169.0 21.4 %collective-permute-start.7 = (bf16[512,512]{1,0:T(8,128)(2,1)S(1)}, bf16[512,512]{1,0:T(8,128)(2,1)}, u32[]{:S(2)}, u32[]{:S(2)}) collective-permute-start(bf16[512,512]{1,0:T(8,128)(2,1)S(1)} %get-tuple-element.22), channel_id=1, source_target_pairs={{0,1},{1,0},{2,3},{3,2},{4,5},{5,4},{6,7},{7,6},{8,9},{9,8},{10,11... | collective-permute-start | bytes 1572872 | tf_op jit(solution)/shard_map/ppermute | solution.py:21
  180.8 11.5 %collective-permute-start.3 = (bf16[16,1024]{1,0:T(8,128)(2,1)S(1)}, bf16[16,1024]{1,0:T(8,128)(2,1)S(1)}, u32[]{:S(2)}, u32[]{:S(2)}) collective-permute-start(bf16[16,1024]{1,0:T(8,128)(2,1)S(1)} %get-tuple-element.26), channel_id=1, source_target_pairs={{0,1},{1,0},{2,3},{3,2},{4,5},{5,4},{6,7},{7,6},{8,9},{9,8},{10,11... | collective-permute-start | bytes 98312 | tf_op jit(solution)/shard_map/ppermute | solution.py:21
Sparse Core Ops, SparseCore 0:
  20.3 45.5 all-gather.3

commit v6 on v5

--- a/solution.py
+++ b/solution.py
@@ -126,42 +126,16 @@
     out_ref[...] = jnp.broadcast_to(table[None], out_ref.shape)
 
 
-def grads_kernel(z_first, info, own_k, sib_k, own_v, sib_v, q_ref, g_ref, st_ref, *rest):
-    own_dk, sib_dk, own_dv, sib_dv, dq_ref, q_head, g_head, turned = rest[-8:]
-    rows = q_head.shape[1]
-    half = rows // 2
-    sides = ((own_k, own_v, own_dk, own_dv), (sib_k, sib_v, sib_dk, sib_dv))
-
-    for p, refs in enumerate(sides):
-        with_rows(p, z_first, info, q_ref, g_ref, q_head, g_head)
-
-        def step(count, tail_used, p=p, refs=refs, owner=info[1 + p]):
-            k_ref, v_ref, dk_ref, dv_ref = refs
-            k_part, v_part = k_ref[:count, :], v_ref[:count, :]
-            k_turned = k_part.T
-            heads = [(h, slice(s * half, (s + 1) * half)) for h in range(2) for s in range(2)]
-            scores = [masked(dot_nt(k_part, q_head[h, at, :]), tail_used) for h, at in heads]
-            upstream = [dot_nt(v_part, g_head[h, at, :]) for h, at in heads]
-            probs = [jnp.exp(scores[n] - st_ref[n, pl.ds(owner, 1), :]) for n in range(4)]
-            dscore = [
-                (probs[n] * (upstream[n] - st_ref[n, pl.ds(2 + owner, 1), :])).astype(BF16)
-                for n in range(4)
-            ]
-            low = jnp.concatenate([x.astype(BF16) for x in probs], axis=1)
-            dv_part = dot_nn(low, g_head[...].reshape(2 * rows, LANES))
-            dk_part = dot_nn(jnp.concatenate(dscore, axis=1), q_head[...].reshape(2 * rows, LANES))
-            for h in range(2):
-                own = slice(h * HDIM, (h + 1) * HDIM)
-                both = jnp.concatenate(dscore[2 * h:2 * h + 2], axis=1)
-                turned[p, own, :] = dot_nn(k_turned[own, :], both)
-            for ref, part in ((dk_ref, dk_part), (dv_ref, dv_part)):
-                ref[:count, :] = part.astype(BF16)
-                unused = ref.shape[0] - count
-                if unused:
-                    ref[count:, :] = jnp.zeros((unused, LANES), BF16)
-
-        by_length(info[3 + p], step)
-
+def query_terms(p, turned, k_part, dscore):
+    k_turned = k_part.T
+    for h in range(2):
+        own = slice(h * HDIM, (h + 1) * HDIM)
+        both = jnp.concatenate(dscore[2 * h:2 * h + 2], axis=1)
+        turned[p, own, :] = dot_nn(k_turned[own, :], both)
+
+
+def write_query_terms(info, turned, dq_ref):
+    rows = turned.shape[2]
     first = pl.ds(pl.multiple_of(info[1] * rows, rows), rows)
     other = pl.ds(pl.multiple_of((1 - info[1]) * rows, rows), rows)
     same = info[1] == info[2]
@@ -175,6 +149,95 @@
     def _():
         dq_ref[first, :] = turned[0].astype(BF16).T
         dq_ref[other, :] = turned[1].astype(BF16).T
+
+
+def key_terms(probs, dscore, q_head, g_head, dk_ref, dv_ref):
+    rows = q_head.shape[1]
+    count = probs[0].shape[0]
+    low = jnp.concatenate([x.astype(BF16) for x in probs], axis=1)
+    dv_part = dot_nn(low, g_head[...].reshape(2 * rows, LANES))
+    dk_part = dot_nn(jnp.concatenate(dscore, axis=1), q_head[...].reshape(2 * rows, LANES))
+    for ref, part in ((dk_ref, dk_part), (dv_ref, dv_part)):
+        ref[:count, :] = part.astype(BF16)
+        unused = ref.shape[0] - count
+        if unused:
+            ref[count:, :] = jnp.zeros((unused, LANES), BF16)
+
+
+def scored(z_first, p, info, refs, q_ref, g_ref, st_ref, q_head, g_head, use):
+    half = q_head.shape[1] // 2
+    with_rows(p, z_first, info, q_ref, g_ref, q_head, g_head)
+    k_ref, v_ref = refs
+    owner = info[1 + p]
+
+    def stat(n, row):
+        return st_ref[n, pl.ds(row, 1), :]
+
+    def step(count, tail_used):
+        k_part, v_part = k_ref[:count, :], v_ref[:count, :]
+        heads = [(h, slice(s * half, (s + 1) * half)) for h in range(2) for s in range(2)]
+        scores = [masked(dot_nt(k_part, q_head[h, at, :]), tail_used) for h, at in heads]
+        upstream = [dot_nt(v_part, g_head[h, at, :]) for h, at in heads]
+        probs = [jnp.exp(scores[n] - stat(n, owner)) for n in range(4)]
+        dscore = [(probs[n] * (upstream[n] - stat(n, 2 + owner))).astype(BF16) for n in range(4)]
+        use(k_part, probs, dscore)
+
+    by_length(info[3 + p], step)
+
+
+def dq_kernel(z_first, info, own_k, sib_k, own_v, sib_v, q_ref, g_ref, st_ref, dq_ref,
+              q_head, g_head, turned):
+    for p, refs in enumerate(((own_k, own_v), (sib_k, sib_v))):
+
+        def use(k_part, probs, dscore, p=p):
+            query_terms(p, turned, k_part, dscore)
+
+        scored(z_first, p, info, refs, q_ref, g_ref, st_ref, q_head, g_head, use)
+
+    write_query_terms(info, turned, dq_ref)
+
+
+def dkv_kernel(z_first, info, own_k, sib_k, own_v, sib_v, q_ref, g_ref, st_ref, *rest):
+    own_dk, sib_dk, own_dv, sib_dv, q_head, g_head = rest[-6:]
+    sides = ((own_k, own_v, own_dk, own_dv), (sib_k, sib_v, sib_dk, sib_dv))
+    for p, (k_ref, v_ref, dk_ref, dv_ref) in enumerate(sides):
+
+        def use(k_part, probs, dscore, dk_ref=dk_ref, dv_ref=dv_ref):
+            key_terms(probs, dscore, q_head, g_head, dk_ref, dv_ref)
+
+        scored(z_first, p, info, (k_ref, v_ref), q_ref, g_ref, st_ref, q_head, g_head, use)
+
+
+def grads_kernel(z_first, info, own_k, sib_k, own_v, sib_v, q_ref, g_ref, st_ref,
+                 own_dk, sib_dk, own_dv, sib_dv, dq_ref, q_head, g_head, turned):
+    sides = ((own_k, own_v, own_dk, own_dv), (sib_k, sib_v, sib_dk, sib_dv))
+    for p, (k_ref, v_ref, dk_ref, dv_ref) in enumerate(sides):
+
+        def use(k_part, probs, dscore, p=p, dk_ref=dk_ref, dv_ref=dv_ref):
+            key_terms(probs, dscore, q_head, g_head, dk_ref, dv_ref)
+            query_terms(p, turned, k_part, dscore)
+
+        scored(z_first, p, info, (k_ref, v_ref), q_ref, g_ref, st_ref, q_head, g_head, use)
+
+    write_query_terms(info, turned, dq_ref)
+
+
+def complete_kernel(half, info, *refs):
+    sibs, (own_dk, own_dv, held, sems) = refs[:4], refs[-4:]
+    span = half // PARTS
+    loads, stores = [], []
+    for n, sib in enumerate(sibs):
+        part, own = n // 2, (own_dk, own_dv)[n % 2]
+        at = pl.multiple_of((1 - info[0]) * half + part * span, span)
+        loads.append(pltpu.make_async_copy(sib, held.at[n], sems.at[0, n]))
+        stores.append(pltpu.make_async_copy(held.at[n], own.at[:, pl.ds(at, span)], sems.at[1, n]))
+    for load in loads:
+        load.start()
+    for load, store in zip(loads, stores):
+        load.wait()
+        store.start()
+    for store in stores:
+        store.wait()
 
 
 PARTS = 2
@@ -239,34 +302,86 @@
     )(stats)
 
 
-def gradients(operands, stats, part, begun):
+def key_specs(operands, part):
+    slots, half, pairs, all_rows, rows = sizes(operands)
+    own = blocks(slots, pairs, operands[5].shape, part)[0]
+    sib = pl.BlockSpec((slots, LANES), lambda i, info: (0, i))
+    whole = jax.ShapeDtypeStruct((slots, 2 * half), BF16)
+    half_part = jax.ShapeDtypeStruct((slots, half // PARTS), BF16)
+    return [own, sib, own, sib], [whole, half_part, whole, half_part]
+
+
+def query_specs(operands):
+    slots, half, pairs, all_rows, rows = sizes(operands)
+    spec = pl.BlockSpec((all_rows, LANES), lambda i, info: (0, i))
+    scratch = pltpu.VMEM((2, LANES, rows), F32)
+    return [spec], [jax.ShapeDtypeStruct((all_rows, half // PARTS), BF16)], [scratch]
+
+
+def call(kernel, operands, stats, part, out_specs, out_shape, scratch, begun, share, name):
     slots, half, pairs, all_rows, rows = sizes(operands)
     own, in_blocks, first, steps = blocks(slots, pairs, operands[5].shape, part)
-    span = LANES
-    sib = pl.BlockSpec((slots, span), lambda i, info: (0, i))
     stat = pl.BlockSpec((4, 8, rows // 2), lambda i, info: (first + i, 0, 0))
-    whole = jax.ShapeDtypeStruct((slots, 2 * half), BF16)
-    half_part = jax.ShapeDtypeStruct((slots, steps * span), BF16)
     return pl.pallas_call(
-        functools.partial(grads_kernel, part == 0),
+        functools.partial(kernel, part == 0),
         grid_spec=pltpu.PrefetchScalarGridSpec(
             num_scalar_prefetch=1,
             grid=(steps,),
             in_specs=in_blocks + [stat] + [pl.BlockSpec(memory_space=pl.ANY)] * len(begun),
-            out_specs=[own, sib, own, sib, pl.BlockSpec((all_rows, span), lambda i, info: (0, i))],
-            scratch_shapes=[pltpu.VMEM((2, rows, LANES), BF16)] * 2
-            + [pltpu.VMEM((2, LANES, rows), F32)],
+            out_specs=out_specs,
+            scratch_shapes=[pltpu.VMEM((2, rows, LANES), BF16)] * 2 + scratch,
         ),
-        out_shape=[whole, half_part, whole, half_part,
-                   jax.ShapeDtypeStruct((all_rows, steps * span), BF16)],
+        out_shape=out_shape,
         input_output_aliases={8: 0, 9: 2} if begun else {},
         compiler_params=LIMIT,
         cost_estimate=pl.CostEstimate(
-            flops=10 * slots * rows * half, bytes_accessed=8 << 20,
+            flops=share * slots * rows * half, bytes_accessed=share << 20,
             transcendentals=slots * rows * half // HDIM,
         ),
-        name="gradients",
+        name=name,
     )(*operands, stats, *begun)
+
+
+def query_gradients(operands, stats, part):
+    specs, shapes, scratch = query_specs(operands)
+    return call(
+        dq_kernel, operands, stats, part, specs, shapes, scratch, [], 6, "query_gradients"
+    )[0]
+
+
+def key_gradients(operands, stats, part, begun):
+    specs, shapes = key_specs(operands, part)
+    return call(dkv_kernel, operands, stats, part, specs, shapes, [], begun, 8, "key_gradients")
+
+
+def gradients(operands, stats, part):
+    specs, shapes = key_specs(operands, part)
+    more_specs, more_shapes, scratch = query_specs(operands)
+    return call(
+        grads_kernel, operands, stats, part, specs + more_specs, shapes + more_shapes, scratch,
+        [], 10, "gradients",
+    )
+
+
+def completed(info, sibs, own_dk, own_dv):
+    anywhere = pl.BlockSpec(memory_space=pl.ANY)
+    shape = jax.ShapeDtypeStruct(own_dk.shape, BF16)
+    return pl.pallas_call(
+        functools.partial(complete_kernel, own_dk.shape[1] // 2),
+        grid_spec=pltpu.PrefetchScalarGridSpec(
+            num_scalar_prefetch=1,
+            grid=(1,),
+            in_specs=[anywhere] * 6,
+            out_specs=[anywhere] * 2,
+            scratch_shapes=[
+                pltpu.VMEM((4,) + sibs[0].shape, BF16), pltpu.SemaphoreType.DMA((2, 4))
+            ],
+        ),
+        out_shape=[shape, shape],
+        input_output_aliases={5: 0, 6: 1},
+        cost_estimate=pl.CostEstimate(flops=0, bytes_accessed=8 << 20, transcendentals=0),
+        name="complete_keys",
+    )(info, *sibs, own_dk, own_dv)
 
 
 def per_device(x_size, z_size, queries, keys, values, grad_out, lengths, slot_query):
@@ -305,19 +420,22 @@
 
     held = all_rows // chips
     own_rows = held // 2
-    begun, sibs, sums = [], [], []
-    for part in range(PARTS):
-        own_dk, sib_dk, own_dv, sib_dv, dq = gradients(operands[part], stats, part, begun)
-        begun = [own_dk, own_dv]
-        sibs.append((swap_cores(sib_dk), swap_cores(sib_dv)))
-        terms = lax.all_to_all(dq.reshape(chips, held, span), CHIP, 0, 0, tiled=True)
-        sums.append(jnp.sum(terms.astype(F32), axis=0).astype(BF16))
-
-    own_dk, own_dv = begun
-    for part, (sib_dk, sib_dv) in enumerate(sibs):
-        at = (1 - core) * half + part * span
-        own_dk = lax.dynamic_update_slice_in_dim(own_dk, sib_dk, at, 1)
-        own_dv = lax.dynamic_update_slice_in_dim(own_dv, sib_dv, at, 1)
+
+    def to_owners(dq):
+        return lax.all_to_all(dq.reshape(chips, held, span), CHIP, 0, 0, tiled=True)
+
+    first_terms = to_owners(query_gradients(operands[0], stats, 0))
+    own_dk, sib_dk_1, own_dv, sib_dv_1, dq = gradients(operands[1], stats, 1)
+    second_terms = to_owners(dq)
+    sibs = [swap_cores(sib_dk_1), swap_cores(sib_dv_1)]
+    stats, first_terms = lax.optimization_barrier((stats, first_terms))
+    own_dk, sib_dk_0, own_dv, sib_dv_0 = key_gradients(operands[0], stats, 0, [own_dk, own_dv])
+    sibs = [swap_cores(sib_dk_0), swap_cores(sib_dv_0)] + sibs
+    own_dk, own_dv = completed(info, sibs, own_dk, own_dv)
+    own_dk, second_terms = lax.optimization_barrier((own_dk, second_terms))
+    sums = [
+        jnp.sum(terms.astype(F32), axis=0).astype(BF16) for terms in (first_terms, second_terms)
+    ]
 
     summed = jnp.concatenate(sums, axis=1)
     kept = lax.dynamic_slice_in_dim(summed, core * own_rows, own_rows, 0)

time: 203 us -> 199 us (0.980)
  Pallas kernels: 29.5 us -> 52.2 us
  starting transfers between devices: 48.2 us -> 36.4 us
  waiting for transfers between devices: 17.1 us -> 7.92 us
  blocking collectives: 71.9 us -> 67.6 us
  local copies, waits for them, and re-layouts: 14.5 us -> 11.5 us
    pallas_call x2 -> x4, Pallas kernels: 16.1 us -> 35 us  [the longest x3 32 us: call(): pl.pallas_call(functools.partial(kernel, part == 0), grid_spec=pltpu.Pref...]
    all_to_all x2, waiting for transfers between devices: 14.6 us -> 4.79 us  [to_owners(): return lax.all_to_all(dq.reshape(chips, held, span), CHIP, 0, 0, tiled=True)]
    dynamic_update_slice x4 -> x0, local copies, waits for them, and re-layouts: 7.47 us -> none  [the longest x2 3.74 us: per_device(): own_dv = lax.dynamic_update_slice_in_dim(own_dv, sib_dv, at, 1)]
    all_to_all x2, starting transfers between devices: 19.2 us -> 13 us  [to_owners(): return lax.all_to_all(dq.reshape(chips, held, span), CHIP, 0, 0, tiled=True)]
    ppermute x8, starting transfers between devices: 24.5 us -> 18.9 us  [swap_cores(): return lax.ppermute(value, 'core', [(0, 1), (1, 0)])]
    unnamed x6 -> x18, local copies, waits for them, and re-layouts: 0.01 us -> 4.41 us
    all_to_all x1, blocking collectives: 21.3 us -> 17.2 us  [per_device(): stats = lax.all_to_all(stats[0], CHIP, 0, 0, tiled=True)]
    pallas_call x2, Pallas kernels: 11.4 us -> 15.2 us  [row_stats(): pl.pallas_call(functools.partial(stats_kernel, part == 0), grid_spec=pltp...]
  transfers between devices with their start and end apart: 12 -> 12, of which waited for: 5 -> 6; matrix products, arithmetic and copies ran while one was open for 8% -> 4% of each run, Pallas kernels for 7% -> 17%
where the time goes in v6:
time: 199 us; the launch traced here: 196 us
  blocking collectives  67.6 us (34%)
  Pallas kernels  52.2 us (26%)
  starting transfers between devices  36.4 us (18%)
  between operations  15.5 us (8%)
  local copies, waits for them, and re-layouts  11.5 us (6%)
  waiting for transfers between devices  7.92 us (4%)
  other arithmetic  4.38 us (2%)
    pallas_call x3, Pallas kernels, call(): pl.pallas_call(functools.partial(kernel, part == 0), grid_spec=pltpu.Pref...  32 us
    all_to_all x1, blocking collectives, gather_z_then_x(): column = lax.all_to_all(repeated(value, z_size), 'z', 0, 0, tiled=True)  24.4 us
    ppermute x8, starting transfers between devices, swap_cores(): return lax.ppermute(value, 'core', [(0, 1), (1, 0)])  18.9 us
    all_to_all x1, blocking collectives, per_device(): stats = lax.all_to_all(stats[0], CHIP, 0, 0, tiled=True)  17.2 us
    pallas_call x2, Pallas kernels, row_stats(): pl.pallas_call(functools.partial(stats_kernel, part == 0), grid_spec=pltp...  15.2 us
    all_to_all x1, blocking collectives, per_device(): stats = lax.all_to_all(merge_stats(stats), CHIP, 0, 0, tiled=True)  14 us
    all_to_all x2, starting transfers between devices, to_owners(): return lax.all_to_all(dq.reshape(chips, held, span), CHIP, 0, 0, tiled=True)  13 us
    all_to_all x1, blocking collectives, gather_x_then_z(): columns = lax.all_to_all(repeated(value, x_size), 'x', 0, 0, tiled=True)  9.74 us
  transfers between devices with their start and end apart: 12, of which 6 were waited for; matrix products, arithmetic and copies ran while one was open for 4% of the time, Pallas kernels for 17%

profile of v6, /device:TPU:25, one launch (start us, length us, event | category | flops | bytes accessed | tf_op | source)
XLA Modules:
  0.0 195.5 jit_solution(15912085665433267799)
XLA Ops:
  7.2 0.0 all-gather.4.cloned.1.call-start
  7.2 0.9 pad_maximum_fusion
  8.1 2.3 %all-gather = bf16[4,16,2048]{2,1,0:T(8,128)(2,1)S(1)} all-gather(bf16[2,16,2048]{2,1,0:T(8,128)(2,1)S(1)} %pad_maximum_fusion), channel_id=2, replica_groups=mesh['group'=4,'x'=4,'z'=8,'core'=2] {'core'}, dimensions={0}, use_global_device_ids=true | all-gather | bytes 393216 | tf_op jit(solution)/shard_map/all_gather | solution.py:402
  10.5 9.7 %all_to_all.35 = bf16[4,2,2,16,512]{4,3,2,1,0:T(8,128)(2,1)} all-to-all(bf16[4,2,2,16,512]{4,3,2,1,0:T(8,128)(2,1)S(1)} %broadcast_in_dim.12), channel_id=1, replica_groups=mesh['group'=4,'x'=4,'z'=8,'core'=2] {'x'}, dimensions={0} | all-to-all | bytes 524288 | tf_op jit(solution)/shard_map/all_to_all | solution.py:29
  20.2 0.0 all-gather.4.cloned.1.call-update
  20.2 0.1 broadcast_in_dim.10
  20.3 24.4 %all_to_all.36 = bf16[8,2,2,16,512]{4,3,2,1,0:T(8,128)(2,1)S(1)} all-to-all(bf16[8,2,2,16,512]{4,3,2,1,0:T(8,128)(2,1)S(1)} %broadcast_in_dim.10), channel_id=1, replica_groups=mesh['group'=4,'x'=4,'z'=8,'core'=2] {'z'}, dimensions={0} | all-to-all | bytes 1048576 | tf_op jit(solution)/shard_map/all_to_all | solution.py:34
  44.6 1.6 broadcast_in_dim.11
  46.2 4.5 %all-to-all-start.1 = ((bf16[4,8,2,2,16,512]{5,4,3,2,1,0:T(8,128)(2,1)}), bf16[4,8,2,2,16,512]{5,4,3,2,1,0:T(8,128)(2,1)}, u32[]{:S(2)}, u32[]{:S(2)}) async-start(bf16[4,8,2,2,16,512]{5,4,3,2,1,0:T(8,128)(2,1)} %broadcast_in_dim.11), calls=%async_computation.1 | async-start | bytes 4194304 | tf_op jit(solution)/shard_map/all_to_all | solution.py:35
  50.7 0.0 copy-start
  50.7 2.4 %dynamic-slice_bitcast_fusion = bf16[512,1024]{1,0:T(8,128)(2,1)} fusion(bf16[1,512,2048]{2,1,0:T(8,128)(2,1)} %param.8, s32[]{:T(128)S(6)} %select_n.25), kind=kLoop, calls=%fused_computation | loop fusion | bytes 2097156 | tf_op jit(solution)/shard_map/dynamic_slice | solution.py:400
  53.2 6.6 %collective-permute-start.2 = (bf16[512,1024]{1,0:T(8,128)(2,1)}, bf16[512,1024]{1,0:T(8,128)(2,1)S(1)}, u32[]{:S(2)}, u32[]{:S(2)}) collective-permute-start(bf16[512,1024]{1,0:T(8,128)(2,1)} %dynamic-slice_bitcast_fusion), channel_id=1, source_target_pairs={{0,1},{1,0},{2,3},{3,2},{4,5},{5,4},{6,7},{7,6},{8,9},{9,8},{10,11... | collective-permute-start | bytes 3145736 | tf_op jit(solution)/shard_map/ppermute | solution.py:21
  59.8 1.1 dynamic-slice_bitcast_fusion.1
  62.2 0.1 pad_add_fusion
  62.2 0.5 collective-permute-start
  62.8 0.8 collective-permute-done
  63.6 0.6 fusion.2
  64.2 1.2 stack.16.info
  65.5 0.5 all-gather.4.cloned.1.call-done
  66.0 7.6 %row_stats.2.rest_0_ = f32[32,8,256]{2,1,0:T(8,128)S(1)} custom-call(s32[5]{0:T(128)S(1)} %stack.16.info, bf16[512,2048]{1,0:T(8,128)(2,1)S(1)} %bitcast.16, bf16[512,1024]{1,0:T(8,128)(2,1)} %collective-permute-done.1.sib_k, bf16[512,2048]{1,0:T(8,128)(2,1)} %bitcast.28, bf16[512,1024]{1,0:T(8,128)(2,1)S(1)} %collective-permute-done.2.sib_v, ...), custom_call_target="tpu_custom_call" | custom-call | flops 1073741824 | bytes 5242880 | tf_op jit(solution)/shard_map/row_stats/pallas_call | solution.py:273
  73.6 7.6 %row_stats.3 = f32[32,8,256]{2,1,0:T(8,128)S(1)} custom-call(s32[5]{0:T(128)S(1)} %stack.16.info, bf16[512,2048]{1,0:T(8,128)(2,1)S(1)} %bitcast.17, bf16[512,1024]{1,0:T(8,128)(2,1)} %collective-permute-done.1.sib_k, bf16[512,2048]{1,0:T(8,128)(2,1)} %bitcast.29, ...), custom_call_target="tpu_custom_call", output_to_operand_aliasing={{}: (7, {})} | custom-call | flops 1073741824 | bytes 5242880 | tf_op jit(solution)/shard_map/row_stats/pallas_call | solution.py:273
  81.2 17.2 %all_to_all.37.in_ref = f32[32,8,256]{2,1,0:T(8,128)} all-to-all(f32[32,8,256]{2,1,0:T(8,128)S(1)} %row_stats.3), channel_id=1, replica_groups=mesh['group'=4,'x'=4,'z'=8,'core'=2] {'x','z'}, dimensions={0} | all-to-all | bytes 524288 | tf_op jit(solution)/shard_map/all_to_all | solution.py:418
  98.4 2.0 %merge_stats.1 = f32[32,8,256]{2,1,0:T(8,128)} custom-call(f32[32,8,256]{2,1,0:T(8,128)} %all_to_all.37.in_ref), custom_call_target="tpu_custom_call" | custom-call | tf_op jit(solution)/shard_map/merge_stats/pallas_call | solution.py:296
  100.4 14.0 %all_to_all.38.st_ref = f32[32,8,256]{2,1,0:T(8,128)S(1)} all-to-all(f32[32,8,256]{2,1,0:T(8,128)} %merge_stats.1), channel_id=1, replica_groups=mesh['group'=4,'x'=4,'z'=8,'core'=2] {'x','z'}, dimensions={0} | all-to-all | bytes 524288 | tf_op jit(solution)/shard_map/all_to_all | solution.py:419
  114.4 9.0 %query_gradients.1 = bf16[1024,512]{1,0:T(8,128)(2,1)S(1)} custom-call(s32[5]{0:T(128)S(1)} %stack.16.info, bf16[512,2048]{1,0:T(8,128)(2,1)S(1)} %bitcast.18, bf16[512,1024]{1,0:T(8,128)(2,1)} %collective-permute-done.1.sib_k, bf16[512,2048]{1,0:T(8,128)(2,1)} %bitcast.30, bf16[512,1024]{1,0:T(8,128)(2,1)S(1)} %collective-permute-done.2.sib_v, ...), custom_call_target="tpu_custom_call" | custom-call | flops 1610612736 | bytes 6291456 | tf_op jit(solution)/shard_map/query_gradients/pallas_call | solution.py:325
  123.4 0.9 copy-done.2
  124.4 5.0 %all-to-all-start.5 = ((bf16[32,32,512]{2,1,0:T(8,128)(2,1)}), bf16[32,32,512]{2,1,0:T(8,128)(2,1)}, u32[]{:S(2)}, u32[]{:S(2)}) async-start(bf16[32,32,512]{2,1,0:T(8,128)(2,1)} %bitcast.20), calls=%async_computation.5 | async-start | bytes 2097152 | tf_op jit(solution)/shard_map/all_to_all | solution.py:425
  129.4 12.2 %gradients.1 = (bf16[512,2048]{1,0:T(8,128)(2,1)}, bf16[512,512]{1,0:T(8,128)(2,1)S(1)}, bf16[512,2048]{1,0:T(8,128)(2,1)}, bf16[512,512]{1,0:T(8,128)(2,1)S(1)}, bf16[1024,512]{1,0:T(8,128)(2,1)S(1)}) custom-call(s32[5]{0:T(128)S(1)} %stack.16.info, bf16[512,2048]{1,0:T(8,128)(2,1)} %bitcast.15, bf16[512,1024]{1,0:T(8,128)(2,1)} %collective-permute-done.1.sib_k, ...), custom_call_target="tpu_custom_call" | custom-call | flops 2684354560 | bytes 10485760 | tf_op jit(solution)/shard_map/gradients/pallas_call | solution.py:325
  141.6 1.0 copy-done.3
  142.5 0.8 copy-done.5
  143.3 0.9 copy-done.6
  144.2 4.8 %all-to-all-done.5 = bf16[32,32,512]{2,1,0:T(8,128)(2,1)} async-done(((bf16[32,32,512]{2,1,0:T(8,128)(2,1)}), bf16[32,32,512]{2,1,0:T(8,128)(2,1)}, u32[]{:S(2)}, u32[]{:S(2)}) %all-to-all-start.5) | async-done | bytes 1048608 | tf_op jit(solution)/shard_map/all_to_all | solution.py:425
  149.0 8.0 %all-to-all-start.6 = ((bf16[32,32,512]{2,1,0:T(8,128)(2,1)}), bf16[32,32,512]{2,1,0:T(8,128)(2,1)}, u32[]{:S(2)}, u32[]{:S(2)}) async-start(bf16[32,32,512]{2,1,0:T(8,128)(2,1)} %bitcast.21), calls=%async_computation.6 | async-start | bytes 2097152 | tf_op jit(solution)/shard_map/all_to_all | solution.py:425
  157.0 7.3 %collective-permute-start.5 = (bf16[512,512]{1,0:T(8,128)(2,1)}, bf16[512,512]{1,0:T(8,128)(2,1)}, u32[]{:S(2)}, u32[]{:S(2)}) collective-permute-start(bf16[512,512]{1,0:T(8,128)(2,1)} %copy-done.6), channel_id=1, source_target_pairs={{0,1},{1,0},{2,3},{3,2},{4,5},{5,4},{6,7},{7,6},{8,9},{9,8},{10,11... | collective-permute-start | bytes 1572872 | tf_op jit(solution)/shard_map/ppermute | solution.py:21
  164.2 0.3 collective-permute-start.6
  164.6 10.8 %key_gradients.1 = (bf16[512,2048]{1,0:T(8,128)(2,1)}, bf16[512,512]{1,0:T(8,128)(2,1)}, bf16[512,2048]{1,0:T(8,128)(2,1)}, bf16[512,512]{1,0:T(8,128)(2,1)}) custom-call(s32[5]{0:T(128)S(1)} %stack.16.info, bf16[512,2048]{1,0:T(8,128)(2,1)S(1)} %bitcast.19, ...), custom_call_target="tpu_custom_call", output_to_operand_aliasing={{0}: (8, {}), {2}: (9, {})} | custom-call | flops 2147483648 | bytes 8388608 | tf_op jit(solution)/shard_map/key_gradients/pallas_call | solution.py:325
  175.4 0.2 collective-permute-start.3
  175.6 0.3 collective-permute-start.4
  175.9 1.4 reduce_sum.24
  177.3 0.2 collective-permute-done.3.refs_0_
  177.5 0.7 collective-permute-done.4.refs_1_
  178.2 0.0 copy-done.7
  178.3 0.7 copy-done.8
  179.0 3.1 %complete_keys.1 = (bf16[512,2048]{1,0:T(8,128)(2,1)}, bf16[512,2048]{1,0:T(8,128)(2,1)}) custom-call(s32[5]{0:T(128)} %copy-done.4, bf16[512,512]{1,0:T(8,128)(2,1)} %copy-done.7, bf16[512,512]{1,0:T(8,128)(2,1)} %copy-done.8, bf16[512,512]{1,0:T(8,128)(2,1)} %collective-permute-done.5.refs_2_, ...), custom_call_target="tpu_custom_call", output_to_operand_aliasing={{0}: (5, {}), {1}: (6, {})} | custom-call | bytes 8388608 | tf_op jit(solution)/shard_map/complete_keys/pallas_call | solution.py:369
  182.1 1.4 reduce_sum.25
  183.6 3.6 %collective-permute-start.7 = (bf16[16,1024]{1,0:T(8,128)(2,1)S(1)}, bf16[16,1024]{1,0:T(8,128)(2,1)S(1)}, u32[]{:S(2)}, u32[]{:S(2)}) collective-permute-start(bf16[16,1024]{1,0:T(8,128)(2,1)S(1)} %get-tuple-element.36), channel_id=1, source_target_pairs={{0,1},{1,0},{2,3},{3,2},{4,5},{5,4},{6,7},{7,6},{8,9},{9,8},{10,11... | collective-permute-start | bytes 98312 | tf_op jit(solution)/shard_map/ppermute | solution.py:21
  187.2 0.9 collective-permute-done.7
  188.0 0.6 maximum_select_fusion
  (21 shorter events, 0.1 us)
Async XLA Ops:
  7.2 58.8 %all-gather.4.cloned.1.call-start = ((), (), s32[]{:S(2)}) async-start(), calls=%async_computation.7 | async-start | bytes 2359296 | tf_op jit(solution)/shard_map/all_gather | solution.py:30
  46.2 27.3 %all-to-all-start.1 = ((bf16[4,8,2,2,16,512]{5,4,3,2,1,0:T(8,128)(2,1)}), bf16[4,8,2,2,16,512]{5,4,3,2,1,0:T(8,128)(2,1)}, u32[]{:S(2)}, u32[]{:S(2)}) async-start(bf16[4,8,2,2,16,512]{5,4,3,2,1,0:T(8,128)(2,1)} %broadcast_in_dim.11), calls=%async_computation.1 | async-start | bytes 4194304 | tf_op jit(solution)/shard_map/all_to_all | solution.py:35
  50.7 9.1 %copy-start = (bf16[1,512,2048]{2,1,0:T(8,128)(2,1)S(1)}, bf16[1,512,2048]{2,1,0:T(8,128)(2,1)}, u32[]{:S(2)}) copy-start(bf16[1,512,2048]{2,1,0:T(8,128)(2,1)} %param.7) | copy-start | bytes 6291460
  53.2 12.3 %collective-permute-start.2 = (bf16[512,1024]{1,0:T(8,128)(2,1)}, bf16[512,1024]{1,0:T(8,128)(2,1)S(1)}, u32[]{:S(2)}, u32[]{:S(2)}) collective-permute-start(bf16[512,1024]{1,0:T(8,128)(2,1)} %dynamic-slice_bitcast_fusion), channel_id=1, source_target_pairs={{0,1},{1,0},{2,3},{3,2},{4,5},{5,4},{6,7},{7,6},{8,9},{9,8},{10,11... | collective-permute-start | bytes 3145736 | tf_op jit(solution)/shard_map/ppermute | solution.py:21
  60.9 4.6 %collective-permute-start.1 = (bf16[512,1024]{1,0:T(8,128)(2,1)}, bf16[512,1024]{1,0:T(8,128)(2,1)}, u32[]{:S(2)}, u32[]{:S(2)}) collective-permute-start(bf16[512,1024]{1,0:T(8,128)(2,1)} %dynamic-slice_bitcast_fusion.1), channel_id=1, source_target_pairs={{0,1},{1,0},{2,3},{3,2},{4,5},{5,4},{6,7},{7,6},{8,9},{9,8},{10,11... | collective-permute-start | bytes 3145736 | tf_op jit(solution)/shard_map/ppermute | solution.py:21
  62.2 1.4 collective-permute-start
  65.5 99.1 %copy-start.4 = (s32[5]{0:T(128)}, s32[5]{0:T(128)S(1)}, u32[]{:S(2)}) copy-start(s32[5]{0:T(128)S(1)} %stack.16.info) | copy-start | bytes 64
  123.4 1.0 copy-start.2
  124.4 24.6 %all-to-all-start.5 = ((bf16[32,32,512]{2,1,0:T(8,128)(2,1)}), bf16[32,32,512]{2,1,0:T(8,128)(2,1)}, u32[]{:S(2)}, u32[]{:S(2)}) async-start(bf16[32,32,512]{2,1,0:T(8,128)(2,1)} %bitcast.20), calls=%async_computation.5 | async-start | bytes 2097152 | tf_op jit(solution)/shard_map/all_to_all | solution.py:425
  141.6 1.0 copy-start.3
  142.5 0.8 copy-start.5
  143.3 0.9 copy-start.6
  144.2 20.4 %copy-start.1 = (bf16[1,512,2048]{2,1,0:T(8,128)(2,1)S(1)}, bf16[1,512,2048]{2,1,0:T(8,128)(2,1)}, u32[]{:S(2)}) copy-start(bf16[1,512,2048]{2,1,0:T(8,128)(2,1)} %param.7) | copy-start | bytes 6291460
  149.0 33.1 %all-to-all-start.6 = ((bf16[32,32,512]{2,1,0:T(8,128)(2,1)}), bf16[32,32,512]{2,1,0:T(8,128)(2,1)}, u32[]{:S(2)}, u32[]{:S(2)}) async-start(bf16[32,32,512]{2,1,0:T(8,128)(2,1)} %bitcast.21), calls=%async_computation.6 | async-start | bytes 2097152 | tf_op jit(solution)/shard_map/all_to_all | solution.py:425
  157.0 20.3 %collective-permute-start.5 = (bf16[512,512]{1,0:T(8,128)(2,1)}, bf16[512,512]{1,0:T(8,128)(2,1)}, u32[]{:S(2)}, u32[]{:S(2)}) collective-permute-start(bf16[512,512]{1,0:T(8,128)(2,1)} %copy-done.6), channel_id=1, source_target_pairs={{0,1},{1,0},{2,3},{3,2},{4,5},{5,4},{6,7},{7,6},{8,9},{9,8},{10,11... | collective-permute-start | bytes 1572872 | tf_op jit(solution)/shard_map/ppermute | solution.py:21
  164.2 13.0 %collective-permute-start.6 = (bf16[512,512]{1,0:T(8,128)(2,1)}, bf16[512,512]{1,0:T(8,128)(2,1)}, u32[]{:S(2)}, u32[]{:S(2)}) collective-permute-start(bf16[512,512]{1,0:T(8,128)(2,1)} %copy-done.5), channel_id=1, source_target_pairs={{0,1},{1,0},{2,3},{3,2},{4,5},{5,4},{6,7},{7,6},{8,9},{9,8},{10,11... | collective-permute-start | bytes 1572872 | tf_op jit(solution)/shard_map/ppermute | solution.py:21
  175.4 2.1 %collective-permute-start.3 = (bf16[512,512]{1,0:T(8,128)(2,1)}, bf16[512,512]{1,0:T(8,128)(2,1)S(1)}, u32[]{:S(2)}, u32[]{:S(2)}) collective-permute-start(bf16[512,512]{1,0:T(8,128)(2,1)} %get-tuple-element.22), channel_id=1, source_target_pairs={{0,1},{1,0},{2,3},{3,2},{4,5},{5,4},{6,7},{7,6},{8,9},{9,8},{10,11... | collective-permute-start | bytes 1572872 | tf_op jit(solution)/shard_map/ppermute | solution.py:21
  175.6 2.7 %collective-permute-start.4 = (bf16[512,512]{1,0:T(8,128)(2,1)}, bf16[512,512]{1,0:T(8,128)(2,1)S(1)}, u32[]{:S(2)}, u32[]{:S(2)}) collective-permute-start(bf16[512,512]{1,0:T(8,128)(2,1)} %get-tuple-element.23), channel_id=1, source_target_pairs={{0,1},{1,0},{2,3},{3,2},{4,5},{5,4},{6,7},{7,6},{8,9},{9,8},{10,11... | collective-permute-start | bytes 1572872 | tf_op jit(solution)/shard_map/ppermute | solution.py:21
  177.5 0.8 copy-start.7
  178.2 0.8 copy-start.8
  183.6 4.5 %collective-permute-start.7 = (bf16[16,1024]{1,0:T(8,128)(2,1)S(1)}, bf16[16,1024]{1,0:T(8,128)(2,1)S(1)}, u32[]{:S(2)}, u32[]{:S(2)}) collective-permute-start(bf16[16,1024]{1,0:T(8,128)(2,1)S(1)} %get-tuple-element.36), channel_id=1, source_target_pairs={{0,1},{1,0},{2,3},{3,2},{4,5},{5,4},{6,7},{7,6},{8,9},{9,8},{10,11... | collective-permute-start | bytes 98312 | tf_op jit(solution)/shard_map/ppermute | solution.py:21
Sparse Core Ops, SparseCore 0:
  20.3 45.5 all-gather.3

commit v7 on v6

--- a/solution.py
+++ b/solution.py
@@ -78,7 +78,7 @@
 
 
 def stats_kernel(z_first, info, own_k, sib_k, own_v, sib_v, q_ref, g_ref, *rest):
-    out_ref, q_head, g_head = rest[-3:]
+    out_ref, q_head, g_head, held = rest[-4:]
     rows = q_head.shape[1]
     half = rows // 2
 
@@ -93,37 +93,44 @@
             for n in range(4):
                 peak = jnp.max(scores[n], axis=0, keepdims=True)
                 weights = jnp.exp(scores[n] - peak)
-                stats = (
-                    peak,
-                    jnp.sum(weights, axis=0, keepdims=True),
-                    jnp.sum(weights * upstream[n], axis=0, keepdims=True),
-                    jnp.full((1, half), info[1 + p].astype(F32)),
-                )
-                for t, stat in enumerate(stats):
-                    out_ref[n, 2 * t + p:2 * t + p + 1, :] = stat
+                total = jnp.sum(weights, axis=0, keepdims=True)
+                dotted = jnp.sum(weights * upstream[n], axis=0, keepdims=True)
+                held[p, 0, n:n + 1, :] = peak + jnp.log(total)
+                held[p, 1, n:n + 1, :] = dotted / total
 
         by_length(info[3 + p], step)
 
+    same = info[1] == info[2]
+    first = (held[0, 0], held[0, 1])
+    second = (held[1, 0], held[1, 1])
+
+    def write(query, top, delta):
+        for n in range(4):
+            out_ref[n, pl.ds(query, 1), :] = top[n:n + 1]
+            out_ref[n, pl.ds(QRY + query, 1), :] = delta[n:n + 1]
+
+    @pl.when(same)
+    def _():
+        write(info[1], *joined(jnp.stack([first[0], second[0]]), jnp.stack([first[1], second[1]])))
+        write(1 - info[1], jnp.full_like(first[0], -jnp.inf), jnp.zeros_like(first[1]))
+
+    @pl.when(jnp.logical_not(same))
+    def _():
+        write(info[1], *first)
+        write(info[2], *second)
+
+
+def joined(tops, deltas):
+    peak = jnp.max(tops, axis=0)
+    factors = jnp.exp(tops - peak[None])
+    total = jnp.sum(factors, axis=0)
+    return peak + jnp.log(total), jnp.sum(deltas * factors, axis=0) / total
+
 
 def merge_kernel(in_ref, out_ref):
-    chips = in_ref.shape[0]
-    merged = []
-    tops = [in_ref[:, t, :] for t in range(2)]
-    sums = [in_ref[:, 2 + t, :] for t in range(2)]
-    dots = [in_ref[:, 4 + t, :] for t in range(2)]
-    owners = [in_ref[:, 6 + t, :] for t in range(2)]
-    for query in range(QRY):
-        held = [jnp.where(owners[t] == query, tops[t], -jnp.inf) for t in range(2)]
-        peak = jnp.max(jnp.maximum(held[0], held[1]), axis=0, keepdims=True)
-        factors = [jnp.exp(held[t] - peak) for t in range(2)]
-        total = jnp.sum(sums[0] * factors[0] + sums[1] * factors[1], axis=0, keepdims=True)
-        dotted = jnp.sum(dots[0] * factors[0] + dots[1] * factors[1], axis=0, keepdims=True)
-        merged.append((peak + jnp.log(total), dotted / total))
-    table = jnp.concatenate(
-        [merged[0][0], merged[1][0], merged[0][1], merged[1][1]]
-        + [jnp.zeros_like(merged[0][0])] * 4, axis=0
-    )
-    out_ref[...] = jnp.broadcast_to(table[None], out_ref.shape)
+    table = in_ref[...]
+    tops, deltas = joined(table[:, :QRY], table[:, QRY:])
+    out_ref[...] = jnp.broadcast_to(jnp.concatenate([tops, deltas])[None], out_ref.shape)
 
 
 def query_terms(p, turned, k_part, dscore):
@@ -277,11 +284,12 @@
             grid=(steps,),
             in_specs=in_blocks + [pl.BlockSpec(memory_space=pl.ANY)] * len(begun),
             out_specs=pl.BlockSpec(
-                (4, 8, rows // 2), lambda i, info: (first + i, 0, 0)
+                (4, 2 * QRY, rows // 2), lambda i, info: (first + i, 0, 0)
             ),
-            scratch_shapes=[pltpu.VMEM((2, rows, LANES), BF16)] * 2,
+            scratch_shapes=[pltpu.VMEM((2, rows, LANES), BF16)] * 2
+            + [pltpu.VMEM((2, 2, 4, rows // 2), F32)],
         ),
-        out_shape=jax.ShapeDtypeStruct((4 * pairs, 8, rows // 2), F32),
+        out_shape=jax.ShapeDtypeStruct((4 * pairs, 2 * QRY, rows // 2), F32),
         input_output_aliases={7: 0} if begun else {},
         compiler_params=LIMIT,
         cost_estimate=pl.CostEstimate(
@@ -321,7 +329,7 @@
 def call(kernel, operands, stats, part, out_specs, out_shape, scratch, begun, share, name):
     slots, half, pairs, all_rows, rows = sizes(operands)
     own, in_blocks, first, steps = blocks(slots, pairs, operands[5].shape, part)
-    stat = pl.BlockSpec((4, 8, rows // 2), lambda i, info: (first + i, 0, 0))
+    stat = pl.BlockSpec((4, 2 * QRY, rows // 2), lambda i, info: (first + i, 0, 0))
     return pl.pallas_call(
         functools.partial(kernel, part == 0),
         grid_spec=pltpu.PrefetchScalarGridSpec(

time: 199 us -> 197 us (0.990)
  blocking collectives: 67.6 us -> 64.7 us
  Pallas kernels: 52.2 us -> 54.6 us
  transfers between devices with their start and end apart: 12 -> 12, of which waited for: 6 -> 6; matrix products, arithmetic and copies ran while one was open for 4% -> 4% of each run, Pallas kernels for 17% -> 18%
where the time goes in v7:
time: 197 us; the launch traced here: 193 us
  blocking collectives  64.7 us (33%)
  Pallas kernels  54.6 us (28%)
  starting transfers between devices  35.7 us (18%)
  between operations  15.5 us (8%)
  local copies, waits for them, and re-layouts  11.5 us (6%)
  waiting for transfers between devices  7.02 us (4%)
  other arithmetic  4.38 us (2%)
    pallas_call x3, Pallas kernels, call(): pl.pallas_call(functools.partial(kernel, part == 0), grid_spec=pltpu.Pref...  33.8 us
    all_to_all x1, blocking collectives, gather_z_then_x(): column = lax.all_to_all(repeated(value, z_size), 'z', 0, 0, tiled=True)  24.4 us
    ppermute x8, starting transfers between devices, swap_cores(): return lax.ppermute(value, 'core', [(0, 1), (1, 0)])  18.3 us
    pallas_call x2, Pallas kernels, row_stats(): pl.pallas_call(functools.partial(stats_kernel, part == 0), grid_spec=pltp...  16.1 us
    all_to_all x1, blocking collectives, per_device(): stats = lax.all_to_all(stats[0], CHIP, 0, 0, tiled=True)  15.3 us
    all_to_all x1, blocking collectives, per_device(): stats = lax.all_to_all(merge_stats(stats), CHIP, 0, 0, tiled=True)  13 us
    all_to_all x2, starting transfers between devices, to_owners(): return lax.all_to_all(dq.reshape(chips, held, span), CHIP, 0, 0, tiled=True)  12.8 us
    all_to_all x1, blocking collectives, gather_x_then_z(): columns = lax.all_to_all(repeated(value, x_size), 'x', 0, 0, tiled=True)  9.74 us
  transfers between devices with their start and end apart: 12, of which 6 were waited for; matrix products, arithmetic and copies ran while one was open for 4% of the time, Pallas kernels for 18%

profile of v7, /device:TPU:25, one launch (start us, length us, event | category | flops | bytes accessed | tf_op | source)
XLA Modules:
  0.0 193.3 jit_solution(3203189977399366009)
XLA Ops:
  7.2 0.0 all-gather.4.cloned.1.call-start
  7.2 0.9 pad_maximum_fusion
  8.1 2.3 %all-gather = bf16[4,16,2048]{2,1,0:T(8,128)(2,1)S(1)} all-gather(bf16[2,16,2048]{2,1,0:T(8,128)(2,1)S(1)} %pad_maximum_fusion), channel_id=2, replica_groups=mesh['group'=4,'x'=4,'z'=8,'core'=2] {'core'}, dimensions={0}, use_global_device_ids=true | all-gather | bytes 393216 | tf_op jit(solution)/shard_map/all_gather | solution.py:410
  10.5 9.7 %all_to_all.35 = bf16[4,2,2,16,512]{4,3,2,1,0:T(8,128)(2,1)} all-to-all(bf16[4,2,2,16,512]{4,3,2,1,0:T(8,128)(2,1)S(1)} %broadcast_in_dim.12), channel_id=1, replica_groups=mesh['group'=4,'x'=4,'z'=8,'core'=2] {'x'}, dimensions={0} | all-to-all | bytes 524288 | tf_op jit(solution)/shard_map/all_to_all | solution.py:29
  20.2 0.0 all-gather.4.cloned.1.call-update
  20.2 0.1 broadcast_in_dim.10
  20.3 24.4 %all_to_all.36 = bf16[8,2,2,16,512]{4,3,2,1,0:T(8,128)(2,1)S(1)} all-to-all(bf16[8,2,2,16,512]{4,3,2,1,0:T(8,128)(2,1)S(1)} %broadcast_in_dim.10), channel_id=1, replica_groups=mesh['group'=4,'x'=4,'z'=8,'core'=2] {'z'}, dimensions={0} | all-to-all | bytes 1048576 | tf_op jit(solution)/shard_map/all_to_all | solution.py:34
  44.6 1.6 broadcast_in_dim.11
  46.2 4.5 %all-to-all-start.1 = ((bf16[4,8,2,2,16,512]{5,4,3,2,1,0:T(8,128)(2,1)}), bf16[4,8,2,2,16,512]{5,4,3,2,1,0:T(8,128)(2,1)}, u32[]{:S(2)}, u32[]{:S(2)}) async-start(bf16[4,8,2,2,16,512]{5,4,3,2,1,0:T(8,128)(2,1)} %broadcast_in_dim.11), calls=%async_computation.1 | async-start | bytes 4194304 | tf_op jit(solution)/shard_map/all_to_all | solution.py:35
  50.7 0.0 copy-start
  50.7 2.4 %dynamic-slice_bitcast_fusion = bf16[512,1024]{1,0:T(8,128)(2,1)} fusion(bf16[1,512,2048]{2,1,0:T(8,128)(2,1)} %param.8, s32[]{:T(128)S(6)} %select_n.25), kind=kLoop, calls=%fused_computation | loop fusion | bytes 2097156 | tf_op jit(solution)/shard_map/dynamic_slice | solution.py:408
  53.2 6.6 %collective-permute-start.2 = (bf16[512,1024]{1,0:T(8,128)(2,1)}, bf16[512,1024]{1,0:T(8,128)(2,1)S(1)}, u32[]{:S(2)}, u32[]{:S(2)}) collective-permute-start(bf16[512,1024]{1,0:T(8,128)(2,1)} %dynamic-slice_bitcast_fusion), channel_id=1, source_target_pairs={{0,1},{1,0},{2,3},{3,2},{4,5},{5,4},{6,7},{7,6},{8,9},{9,8},{10,11... | collective-permute-start | bytes 3145736 | tf_op jit(solution)/shard_map/ppermute | solution.py:21
  59.8 1.1 dynamic-slice_bitcast_fusion.1
  62.2 0.1 pad_add_fusion
  62.2 0.7 collective-permute-start
  63.0 0.8 collective-permute-done
  63.8 0.6 fusion.2
  64.4 1.2 stack.16.info
  65.7 0.3 all-gather.4.cloned.1.call-done
  66.0 8.0 %row_stats.2.rest_0_ = f32[32,4,256]{2,1,0:T(4,128)S(1)} custom-call(s32[5]{0:T(128)S(1)} %stack.16.info, bf16[512,2048]{1,0:T(8,128)(2,1)S(1)} %bitcast.16, bf16[512,1024]{1,0:T(8,128)(2,1)} %collective-permute-done.1.sib_k, bf16[512,2048]{1,0:T(8,128)(2,1)} %bitcast.28, bf16[512,1024]{1,0:T(8,128)(2,1)S(1)} %collective-permute-done.2.sib_v, ...), custom_call_target="tpu_custom_call" | custom-call | flops 1073741824 | bytes 5242880 | tf_op jit(solution)/shard_map/row_stats/pallas_call | solution.py:280
  74.1 8.1 %row_stats.3 = f32[32,4,256]{2,1,0:T(4,128)S(1)} custom-call(s32[5]{0:T(128)S(1)} %stack.16.info, bf16[512,2048]{1,0:T(8,128)(2,1)S(1)} %bitcast.17, bf16[512,1024]{1,0:T(8,128)(2,1)} %collective-permute-done.1.sib_k, bf16[512,2048]{1,0:T(8,128)(2,1)} %bitcast.29, ...), custom_call_target="tpu_custom_call", output_to_operand_aliasing={{}: (7, {})} | custom-call | flops 1073741824 | bytes 5242880 | tf_op jit(solution)/shard_map/row_stats/pallas_call | solution.py:280
  82.1 15.3 %all_to_all.37.in_ref = f32[32,4,256]{2,1,0:T(4,128)} all-to-all(f32[32,4,256]{2,1,0:T(4,128)S(1)} %row_stats.3), channel_id=1, replica_groups=mesh['group'=4,'x'=4,'z'=8,'core'=2] {'x','z'}, dimensions={0} | all-to-all | bytes 262144 | tf_op jit(solution)/shard_map/all_to_all | solution.py:426
  97.4 1.7 merge_stats.1
  99.0 13.0 %all_to_all.38.st_ref = f32[32,4,256]{2,1,0:T(4,128)S(1)} all-to-all(f32[32,4,256]{2,1,0:T(4,128)} %merge_stats.1), channel_id=1, replica_groups=mesh['group'=4,'x'=4,'z'=8,'core'=2] {'x','z'}, dimensions={0} | all-to-all | bytes 262144 | tf_op jit(solution)/shard_map/all_to_all | solution.py:427
  112.0 9.3 %query_gradients.1 = bf16[1024,512]{1,0:T(8,128)(2,1)S(1)} custom-call(s32[5]{0:T(128)S(1)} %stack.16.info, bf16[512,2048]{1,0:T(8,128)(2,1)S(1)} %bitcast.18, bf16[512,1024]{1,0:T(8,128)(2,1)} %collective-permute-done.1.sib_k, bf16[512,2048]{1,0:T(8,128)(2,1)} %bitcast.30, bf16[512,1024]{1,0:T(8,128)(2,1)S(1)} %collective-permute-done.2.sib_v, ...), custom_call_target="tpu_custom_call" | custom-call | flops 1610612736 | bytes 6291456 | tf_op jit(solution)/shard_map/query_gradients/pallas_call | solution.py:333
  121.3 0.9 copy-done.2
  122.3 4.7 %all-to-all-start.5 = ((bf16[32,32,512]{2,1,0:T(8,128)(2,1)}), bf16[32,32,512]{2,1,0:T(8,128)(2,1)}, u32[]{:S(2)}, u32[]{:S(2)}) async-start(bf16[32,32,512]{2,1,0:T(8,128)(2,1)} %bitcast.20), calls=%async_computation.5 | async-start | bytes 2097152 | tf_op jit(solution)/shard_map/all_to_all | solution.py:433
  126.9 13.0 %gradients.1 = (bf16[512,2048]{1,0:T(8,128)(2,1)}, bf16[512,512]{1,0:T(8,128)(2,1)S(1)}, bf16[512,2048]{1,0:T(8,128)(2,1)}, bf16[512,512]{1,0:T(8,128)(2,1)S(1)}, bf16[1024,512]{1,0:T(8,128)(2,1)S(1)}) custom-call(s32[5]{0:T(128)S(1)} %stack.16.info, bf16[512,2048]{1,0:T(8,128)(2,1)} %bitcast.15, bf16[512,1024]{1,0:T(8,128)(2,1)} %collective-permute-done.1.sib_k, ...), custom_call_target="tpu_custom_call" | custom-call | flops 2684354560 | bytes 10485760 | tf_op jit(solution)/shard_map/gradients/pallas_call | solution.py:333
  139.9 1.0 copy-done.3
  140.9 0.8 copy-done.5
  141.7 0.9 copy-done.6
  142.6 4.0 %all-to-all-done.5 = bf16[32,32,512]{2,1,0:T(8,128)(2,1)} async-done(((bf16[32,32,512]{2,1,0:T(8,128)(2,1)}), bf16[32,32,512]{2,1,0:T(8,128)(2,1)}, u32[]{:S(2)}, u32[]{:S(2)}) %all-to-all-start.5) | async-done | bytes 1048608 | tf_op jit(solution)/shard_map/all_to_all | solution.py:433
  146.6 8.2 %all-to-all-start.6 = ((bf16[32,32,512]{2,1,0:T(8,128)(2,1)}), bf16[32,32,512]{2,1,0:T(8,128)(2,1)}, u32[]{:S(2)}, u32[]{:S(2)}) async-start(bf16[32,32,512]{2,1,0:T(8,128)(2,1)} %bitcast.21), calls=%async_computation.6 | async-start | bytes 2097152 | tf_op jit(solution)/shard_map/all_to_all | solution.py:433
  154.7 7.3 %collective-permute-start.5 = (bf16[512,512]{1,0:T(8,128)(2,1)}, bf16[512,512]{1,0:T(8,128)(2,1)}, u32[]{:S(2)}, u32[]{:S(2)}) collective-permute-start(bf16[512,512]{1,0:T(8,128)(2,1)} %copy-done.6), channel_id=1, source_target_pairs={{0,1},{1,0},{2,3},{3,2},{4,5},{5,4},{6,7},{7,6},{8,9},{9,8},{10,11... | collective-permute-start | bytes 1572872 | tf_op jit(solution)/shard_map/ppermute | solution.py:21
  162.1 0.1 collective-permute-start.6
  162.2 11.5 %key_gradients.1 = (bf16[512,2048]{1,0:T(8,128)(2,1)}, bf16[512,512]{1,0:T(8,128)(2,1)}, bf16[512,2048]{1,0:T(8,128)(2,1)}, bf16[512,512]{1,0:T(8,128)(2,1)}) custom-call(s32[5]{0:T(128)S(1)} %stack.16.info, bf16[512,2048]{1,0:T(8,128)(2,1)S(1)} %bitcast.19, ...), custom_call_target="tpu_custom_call", output_to_operand_aliasing={{0}: (8, {}), {2}: (9, {})} | custom-call | flops 2147483648 | bytes 8388608 | tf_op jit(solution)/shard_map/key_gradients/pallas_call | solution.py:333
  173.7 0.4 collective-permute-start.3
  174.1 0.1 collective-permute-start.4
  174.2 1.4 reduce_sum.24
  175.6 0.2 collective-permute-done.3.refs_0_
  175.9 0.7 collective-permute-done.4.refs_1_
  176.6 0.0 copy-done.7
  176.7 0.7 copy-done.8
  177.4 3.1 %complete_keys.1 = (bf16[512,2048]{1,0:T(8,128)(2,1)}, bf16[512,2048]{1,0:T(8,128)(2,1)}) custom-call(s32[5]{0:T(128)} %copy-done.4, bf16[512,512]{1,0:T(8,128)(2,1)} %copy-done.7, bf16[512,512]{1,0:T(8,128)(2,1)} %copy-done.8, bf16[512,512]{1,0:T(8,128)(2,1)} %collective-permute-done.5.refs_2_, ...), custom_call_target="tpu_custom_call", output_to_operand_aliasing={{0}: (5, {}), {1}: (6, {})} | custom-call | bytes 8388608 | tf_op jit(solution)/shard_map/complete_keys/pallas_call | solution.py:377
  180.5 1.4 reduce_sum.25
  181.9 3.0 %collective-permute-start.7 = (bf16[16,1024]{1,0:T(8,128)(2,1)S(1)}, bf16[16,1024]{1,0:T(8,128)(2,1)S(1)}, u32[]{:S(2)}, u32[]{:S(2)}) collective-permute-start(bf16[16,1024]{1,0:T(8,128)(2,1)S(1)} %get-tuple-element.36), channel_id=1, source_target_pairs={{0,1},{1,0},{2,3},{3,2},{4,5},{5,4},{6,7},{7,6},{8,9},{9,8},{10,11... | collective-permute-start | bytes 98312 | tf_op jit(solution)/shard_map/ppermute | solution.py:21
  184.9 0.9 collective-permute-done.7
  185.8 0.6 maximum_select_fusion
  (21 shorter events, 0.1 us)
Async XLA Ops:
  7.2 58.8 %all-gather.4.cloned.1.call-start = ((), (), s32[]{:S(2)}) async-start(), calls=%async_computation.7 | async-start | bytes 2359296 | tf_op jit(solution)/shard_map/all_gather | solution.py:30
  46.2 27.8 %all-to-all-start.1 = ((bf16[4,8,2,2,16,512]{5,4,3,2,1,0:T(8,128)(2,1)}), bf16[4,8,2,2,16,512]{5,4,3,2,1,0:T(8,128)(2,1)}, u32[]{:S(2)}, u32[]{:S(2)}) async-start(bf16[4,8,2,2,16,512]{5,4,3,2,1,0:T(8,128)(2,1)} %broadcast_in_dim.11), calls=%async_computation.1 | async-start | bytes 4194304 | tf_op jit(solution)/shard_map/all_to_all | solution.py:35
  50.7 9.1 %copy-start = (bf16[1,512,2048]{2,1,0:T(8,128)(2,1)S(1)}, bf16[1,512,2048]{2,1,0:T(8,128)(2,1)}, u32[]{:S(2)}) copy-start(bf16[1,512,2048]{2,1,0:T(8,128)(2,1)} %param.7) | copy-start | bytes 6291460
  53.2 12.5 %collective-permute-start.2 = (bf16[512,1024]{1,0:T(8,128)(2,1)}, bf16[512,1024]{1,0:T(8,128)(2,1)S(1)}, u32[]{:S(2)}, u32[]{:S(2)}) collective-permute-start(bf16[512,1024]{1,0:T(8,128)(2,1)} %dynamic-slice_bitcast_fusion), channel_id=1, source_target_pairs={{0,1},{1,0},{2,3},{3,2},{4,5},{5,4},{6,7},{7,6},{8,9},{9,8},{10,11... | collective-permute-start | bytes 3145736 | tf_op jit(solution)/shard_map/ppermute | solution.py:21
  60.9 4.8 %collective-permute-start.1 = (bf16[512,1024]{1,0:T(8,128)(2,1)}, bf16[512,1024]{1,0:T(8,128)(2,1)}, u32[]{:S(2)}, u32[]{:S(2)}) collective-permute-start(bf16[512,1024]{1,0:T(8,128)(2,1)} %dynamic-slice_bitcast_fusion.1), channel_id=1, source_target_pairs={{0,1},{1,0},{2,3},{3,2},{4,5},{5,4},{6,7},{7,6},{8,9},{9,8},{10,11... | collective-permute-start | bytes 3145736 | tf_op jit(solution)/shard_map/ppermute | solution.py:21
  62.2 1.5 collective-permute-start
  65.7 96.5 %copy-start.4 = (s32[5]{0:T(128)}, s32[5]{0:T(128)S(1)}, u32[]{:S(2)}) copy-start(s32[5]{0:T(128)S(1)} %stack.16.info) | copy-start | bytes 64
  121.3 1.0 copy-start.2
  122.3 24.3 %all-to-all-start.5 = ((bf16[32,32,512]{2,1,0:T(8,128)(2,1)}), bf16[32,32,512]{2,1,0:T(8,128)(2,1)}, u32[]{:S(2)}, u32[]{:S(2)}) async-start(bf16[32,32,512]{2,1,0:T(8,128)(2,1)} %bitcast.20), calls=%async_computation.5 | async-start | bytes 2097152 | tf_op jit(solution)/shard_map/all_to_all | solution.py:433
  139.9 1.0 copy-start.3
  140.9 0.8 copy-start.5
  141.7 0.9 copy-start.6
  142.6 19.6 %copy-start.1 = (bf16[1,512,2048]{2,1,0:T(8,128)(2,1)S(1)}, bf16[1,512,2048]{2,1,0:T(8,128)(2,1)}, u32[]{:S(2)}) copy-start(bf16[1,512,2048]{2,1,0:T(8,128)(2,1)} %param.7) | copy-start | bytes 6291460
  146.6 33.9 %all-to-all-start.6 = ((bf16[32,32,512]{2,1,0:T(8,128)(2,1)}), bf16[32,32,512]{2,1,0:T(8,128)(2,1)}, u32[]{:S(2)}, u32[]{:S(2)}) async-start(bf16[32,32,512]{2,1,0:T(8,128)(2,1)} %bitcast.21), calls=%async_computation.6 | async-start | bytes 2097152 | tf_op jit(solution)/shard_map/all_to_all | solution.py:433
  154.7 20.8 %collective-permute-start.5 = (bf16[512,512]{1,0:T(8,128)(2,1)}, bf16[512,512]{1,0:T(8,128)(2,1)}, u32[]{:S(2)}, u32[]{:S(2)}) collective-permute-start(bf16[512,512]{1,0:T(8,128)(2,1)} %copy-done.6), channel_id=1, source_target_pairs={{0,1},{1,0},{2,3},{3,2},{4,5},{5,4},{6,7},{7,6},{8,9},{9,8},{10,11... | collective-permute-start | bytes 1572872 | tf_op jit(solution)/shard_map/ppermute | solution.py:21
  162.1 13.5 %collective-permute-start.6 = (bf16[512,512]{1,0:T(8,128)(2,1)}, bf16[512,512]{1,0:T(8,128)(2,1)}, u32[]{:S(2)}, u32[]{:S(2)}) collective-permute-start(bf16[512,512]{1,0:T(8,128)(2,1)} %copy-done.5), channel_id=1, source_target_pairs={{0,1},{1,0},{2,3},{3,2},{4,5},{5,4},{6,7},{7,6},{8,9},{9,8},{10,11... | collective-permute-start | bytes 1572872 | tf_op jit(solution)/shard_map/ppermute | solution.py:21
  173.7 2.2 %collective-permute-start.3 = (bf16[512,512]{1,0:T(8,128)(2,1)}, bf16[512,512]{1,0:T(8,128)(2,1)S(1)}, u32[]{:S(2)}, u32[]{:S(2)}) collective-permute-start(bf16[512,512]{1,0:T(8,128)(2,1)} %get-tuple-element.22), channel_id=1, source_target_pairs={{0,1},{1,0},{2,3},{3,2},{4,5},{5,4},{6,7},{7,6},{8,9},{9,8},{10,11... | collective-permute-start | bytes 1572872 | tf_op jit(solution)/shard_map/ppermute | solution.py:21
  174.1 2.5 %collective-permute-start.4 = (bf16[512,512]{1,0:T(8,128)(2,1)}, bf16[512,512]{1,0:T(8,128)(2,1)S(1)}, u32[]{:S(2)}, u32[]{:S(2)}) collective-permute-start(bf16[512,512]{1,0:T(8,128)(2,1)} %get-tuple-element.23), channel_id=1, source_target_pairs={{0,1},{1,0},{2,3},{3,2},{4,5},{5,4},{6,7},{7,6},{8,9},{9,8},{10,11... | collective-permute-start | bytes 1572872 | tf_op jit(solution)/shard_map/ppermute | solution.py:21
  175.9 0.8 copy-start.7
  176.6 0.8 copy-start.8
  181.9 3.9 %collective-permute-start.7 = (bf16[16,1024]{1,0:T(8,128)(2,1)S(1)}, bf16[16,1024]{1,0:T(8,128)(2,1)S(1)}, u32[]{:S(2)}, u32[]{:S(2)}) collective-permute-start(bf16[16,1024]{1,0:T(8,128)(2,1)S(1)} %get-tuple-element.36), channel_id=1, source_target_pairs={{0,1},{1,0},{2,3},{3,2},{4,5},{5,4},{6,7},{7,6},{8,9},{9,8},{10,11... | collective-permute-start | bytes 98312 | tf_op jit(solution)/shard_map/ppermute | solution.py:21
Sparse Core Ops, SparseCore 0:
  20.3 45.6 all-gather.3

commit v8 on v7

--- a/solution.py
+++ b/solution.py
@@ -270,7 +270,7 @@
 
 
 LIMIT = pltpu.CompilerParams(
-    dimension_semantics=("arbitrary",), vmem_limit_bytes=48 * 1024 * 1024
+    dimension_semantics=("arbitrary",), vmem_limit_bytes=58 * 1024 * 1024
 )
 
 

time: 197 us -> 201 us (1.020); the launches traced: 193 us -> 200 us
  Pallas kernels: 54.6 us -> 41.7 us
  waiting for transfers between devices: 7.02 us -> 19.9 us
  blocking collectives: 64.7 us -> 70.6 us
  starting transfers between devices: 35.7 us -> 41.4 us
  local copies, waits for them, and re-layouts: 11.5 us -> 8.97 us
  other arithmetic: 4.38 us -> 1.94 us
    all_to_all x2, waiting for transfers between devices: 4 us -> 15.9 us  [to_owners(): return lax.all_to_all(dq.reshape(chips, held, span), CHIP, 0, 0, tiled=True)]
    pallas_call x3, Pallas kernels: 33.8 us -> 23.5 us  [call(): pl.pallas_call(functools.partial(kernel, part == 0), grid_spec=pltpu.Pref...]
    all_to_all x1, blocking collectives: 15.3 us -> 20.5 us  [per_device(): stats = lax.all_to_all(stats[0], CHIP, 0, 0, tiled=True)]
    unnamed x18 -> x10, local copies, waits for them, and re-layouts: 4.41 us -> 1.34 us
    ppermute x8, starting transfers between devices: 18.3 us -> 21.2 us  [swap_cores(): return lax.ppermute(value, 'core', [(0, 1), (1, 0)])]
    all_to_all x2, starting transfers between devices: 12.8 us -> 15.7 us  [to_owners(): return lax.all_to_all(dq.reshape(chips, held, span), CHIP, 0, 0, tiled=True)]
    pallas_call x2, Pallas kernels: 16.1 us -> 13.5 us  [row_stats(): pl.pallas_call(functools.partial(stats_kernel, part == 0), grid_spec=pltp...]
    reduce_sum x2, other arithmetic: 2.77 us -> 0.32 us  [per_device(): jnp.sum(terms.astype(F32), axis=0).astype(BF16)]
  transfers between devices with their start and end apart: 12 -> 12, of which waited for: 6 -> 6; matrix products, arithmetic and copies ran while one was open for 4% -> 4% of each run, Pallas kernels for 18% -> 13%
where the time goes in v8:
time: 201 us; the launch traced here: 200 us
  blocking collectives  70.6 us (35%)
  Pallas kernels  41.7 us (21%)
  starting transfers between devices  41.4 us (21%)
  waiting for transfers between devices  19.9 us (10%)
  between operations  15.5 us (8%)
  local copies, waits for them, and re-layouts  8.97 us (4%)
    all_to_all x1, blocking collectives, gather_z_then_x(): column = lax.all_to_all(repeated(value, z_size), 'z', 0, 0, tiled=True)  24.4 us
    pallas_call x3, Pallas kernels, call(): pl.pallas_call(functools.partial(kernel, part == 0), grid_spec=pltpu.Pref...  23.5 us
    ppermute x8, starting transfers between devices, swap_cores(): return lax.ppermute(value, 'core', [(0, 1), (1, 0)])  21.2 us
    all_to_all x1, blocking collectives, per_device(): stats = lax.all_to_all(stats[0], CHIP, 0, 0, tiled=True)  20.5 us
    all_to_all x2, waiting for transfers between devices, to_owners(): return lax.all_to_all(dq.reshape(chips, held, span), CHIP, 0, 0, tiled=True)  15.9 us
    all_to_all x2, starting transfers between devices, to_owners(): return lax.all_to_all(dq.reshape(chips, held, span), CHIP, 0, 0, tiled=True)  15.7 us
    all_to_all x1, blocking collectives, per_device(): stats = lax.all_to_all(merge_stats(stats), CHIP, 0, 0, tiled=True)  13.7 us
    pallas_call x2, Pallas kernels, row_stats(): pl.pallas_call(functools.partial(stats_kernel, part == 0), grid_spec=pltp...  13.5 us
  transfers between devices with their start and end apart: 12, of which 6 were waited for; matrix products, arithmetic and copies ran while one was open for 4% of the time, Pallas kernels for 13%

profile of v8, /device:TPU:25, one launch (start us, length us, event | category | flops | bytes accessed | tf_op | source)
XLA Modules:
  0.0 199.9 jit_solution(1831868309308774560)
XLA Ops:
  7.2 0.0 all-gather.4.cloned.1.call-start
  7.2 0.9 pad_maximum_fusion
  8.1 2.3 %all-gather = bf16[4,16,2048]{2,1,0:T(8,128)(2,1)S(1)} all-gather(bf16[2,16,2048]{2,1,0:T(8,128)(2,1)S(1)} %pad_maximum_fusion), channel_id=2, replica_groups=mesh['group'=4,'x'=4,'z'=8,'core'=2] {'core'}, dimensions={0}, use_global_device_ids=true | all-gather | bytes 393216 | tf_op jit(solution)/shard_map/all_gather | solution.py:410
  10.5 9.7 %all_to_all.35 = bf16[4,2,2,16,512]{4,3,2,1,0:T(8,128)(2,1)} all-to-all(bf16[4,2,2,16,512]{4,3,2,1,0:T(8,128)(2,1)S(1)} %broadcast_in_dim.12), channel_id=1, replica_groups=mesh['group'=4,'x'=4,'z'=8,'core'=2] {'x'}, dimensions={0} | all-to-all | bytes 524288 | tf_op jit(solution)/shard_map/all_to_all | solution.py:29
  20.2 0.0 all-gather.4.cloned.1.call-update
  20.2 0.1 broadcast_in_dim.10
  20.3 24.4 %all_to_all.36 = bf16[8,2,2,16,512]{4,3,2,1,0:T(8,128)(2,1)S(1)} all-to-all(bf16[8,2,2,16,512]{4,3,2,1,0:T(8,128)(2,1)S(1)} %broadcast_in_dim.10), channel_id=1, replica_groups=mesh['group'=4,'x'=4,'z'=8,'core'=2] {'z'}, dimensions={0} | all-to-all | bytes 1048576 | tf_op jit(solution)/shard_map/all_to_all | solution.py:34
  44.6 1.6 broadcast_in_dim.11
  46.2 4.4 %all-to-all-start.1 = ((bf16[4,8,2,2,16,512]{5,4,3,2,1,0:T(8,128)(2,1)}), bf16[4,8,2,2,16,512]{5,4,3,2,1,0:T(8,128)(2,1)}, u32[]{:S(2)}, u32[]{:S(2)}) async-start(bf16[4,8,2,2,16,512]{5,4,3,2,1,0:T(8,128)(2,1)} %broadcast_in_dim.11), calls=%async_computation.1 | async-start | bytes 4194304 | tf_op jit(solution)/shard_map/all_to_all | solution.py:35
  50.7 0.0 copy-start
  50.7 2.5 %dynamic-slice_bitcast_fusion = bf16[512,1024]{1,0:T(8,128)(2,1)} fusion(bf16[1,512,2048]{2,1,0:T(8,128)(2,1)} %param.8, s32[]{:T(128)S(6)} %select_n.25), kind=kLoop, calls=%fused_computation | loop fusion | bytes 2097156 | tf_op jit(solution)/shard_map/dynamic_slice | solution.py:408
  53.1 6.6 %collective-permute-start.2 = (bf16[512,1024]{1,0:T(8,128)(2,1)}, bf16[512,1024]{1,0:T(8,128)(2,1)S(1)}, u32[]{:S(2)}, u32[]{:S(2)}) collective-permute-start(bf16[512,1024]{1,0:T(8,128)(2,1)} %dynamic-slice_bitcast_fusion), channel_id=1, source_target_pairs={{0,1},{1,0},{2,3},{3,2},{4,5},{5,4},{6,7},{7,6},{8,9},{9,8},{10,11... | collective-permute-start | bytes 3145736 | tf_op jit(solution)/shard_map/ppermute | solution.py:21
  59.8 1.1 dynamic-slice_bitcast_fusion.1
  60.9 0.0 collective-permute-start.1
  62.2 0.1 pad_add_fusion
  62.2 0.7 collective-permute-start
  63.0 0.8 collective-permute-done
  63.8 0.6 fusion.2
  64.4 1.8 stack.16.info
  66.2 0.0 collective-permute-done.2.sib_v
  66.2 0.0 collective-permute-done.1.sib_k
  66.2 0.0 all-gather.4.cloned.1.call-done
  66.3 0.9 copy-done.1
  67.2 0.4 copy-done.2
  67.6 6.7 %row_stats.2.rest_0_ = f32[32,4,256]{2,1,0:T(4,128)} custom-call(s32[5]{0:T(128)} %stack.16.info, bf16[512,2048]{1,0:T(8,128)(2,1)} %bitcast.21, bf16[512,1024]{1,0:T(8,128)(2,1)} %copy-done.2, bf16[512,2048]{1,0:T(8,128)(2,1)} %bitcast.26, bf16[512,1024]{1,0:T(8,128)(2,1)} %copy-done.1, bf16[8,4,2,2,16,512]{5,4,3,2,1,0:T(8,128)(2,1)} %bitcast.15, ...), custom_call_target="tpu_custom_call" | custom-call | flops 1073741824 | bytes 5242880 | tf_op jit(solution)/shard_map/row_stats/pallas_call | solution.py:280
  74.3 6.8 %row_stats.3 = f32[32,4,256]{2,1,0:T(4,128)} custom-call(s32[5]{0:T(128)} %stack.16.info, bf16[512,2048]{1,0:T(8,128)(2,1)} %bitcast.22, bf16[512,1024]{1,0:T(8,128)(2,1)} %copy-done.2, bf16[512,2048]{1,0:T(8,128)(2,1)} %bitcast.27, bf16[512,1024]{1,0:T(8,128)(2,1)} %copy-done.1, ...), custom_call_target="tpu_custom_call", output_to_operand_aliasing={{}: (7, {})} | custom-call | flops 1073741824 | bytes 5242880 | tf_op jit(solution)/shard_map/row_stats/pallas_call | solution.py:280
  81.1 20.5 %all_to_all.37.in_ref = f32[32,4,256]{2,1,0:T(4,128)} all-to-all(f32[32,4,256]{2,1,0:T(4,128)} %row_stats.3), channel_id=1, replica_groups=mesh['group'=4,'x'=4,'z'=8,'core'=2] {'x','z'}, dimensions={0} | all-to-all | bytes 262144 | tf_op jit(solution)/shard_map/all_to_all | solution.py:426
  101.5 1.7 merge_stats.1
  103.2 13.7 %all_to_all.38.st_ref = f32[32,4,256]{2,1,0:T(4,128)} all-to-all(f32[32,4,256]{2,1,0:T(4,128)} %merge_stats.1), channel_id=1, replica_groups=mesh['group'=4,'x'=4,'z'=8,'core'=2] {'x','z'}, dimensions={0} | all-to-all | bytes 262144 | tf_op jit(solution)/shard_map/all_to_all | solution.py:427
  116.9 7.7 %query_gradients.1 = bf16[1024,512]{1,0:T(8,128)(2,1)} custom-call(s32[5]{0:T(128)} %stack.16.info, bf16[512,2048]{1,0:T(8,128)(2,1)} %bitcast.23, bf16[512,1024]{1,0:T(8,128)(2,1)} %copy-done.2, bf16[512,2048]{1,0:T(8,128)(2,1)} %bitcast.28, bf16[512,1024]{1,0:T(8,128)(2,1)} %copy-done.1, bf16[8,4,2,2,16,512]{5,4,3,2,1,0:T(8,128)(2,1)} %bitcast.17, ...), custom_call_target="tpu_custom_call" | custom-call | flops 1610612736 | bytes 6291456 | tf_op jit(solution)/shard_map/query_gradients/pallas_call | solution.py:333
  124.5 6.6 %all-to-all-start.5 = ((bf16[32,32,512]{2,1,0:T(8,128)(2,1)}), bf16[32,32,512]{2,1,0:T(8,128)(2,1)S(1)}, u32[]{:S(2)}, u32[]{:S(2)}) async-start(bf16[32,32,512]{2,1,0:T(8,128)(2,1)} %bitcast.33), calls=%async_computation.5 | async-start | bytes 2097152 | tf_op jit(solution)/shard_map/all_to_all | solution.py:433
  131.1 8.3 %gradients.1 = (bf16[512,2048]{1,0:T(8,128)(2,1)}, bf16[512,512]{1,0:T(8,128)(2,1)}, bf16[512,2048]{1,0:T(8,128)(2,1)}, bf16[512,512]{1,0:T(8,128)(2,1)}, bf16[1024,512]{1,0:T(8,128)(2,1)}) custom-call(s32[5]{0:T(128)} %stack.16.info, bf16[512,2048]{1,0:T(8,128)(2,1)} %bitcast.24, bf16[512,1024]{1,0:T(8,128)(2,1)} %copy-done.2, bf16[512,2048]{1,0:T(8,128)(2,1)} %bitcast.29, ...), custom_call_target="tpu_custom_call" | custom-call | flops 2684354560 | bytes 10485760 | tf_op jit(solution)/shard_map/gradients/pallas_call | solution.py:333
  139.4 13.2 %all-to-all-done.5 = bf16[32,32,512]{2,1,0:T(8,128)(2,1)S(1)} async-done(((bf16[32,32,512]{2,1,0:T(8,128)(2,1)}), bf16[32,32,512]{2,1,0:T(8,128)(2,1)S(1)}, u32[]{:S(2)}, u32[]{:S(2)}) %all-to-all-start.5) | async-done | bytes 1048608 | tf_op jit(solution)/shard_map/all_to_all | solution.py:433
  152.6 9.1 %all-to-all-start.6 = ((bf16[32,32,512]{2,1,0:T(8,128)(2,1)}), bf16[32,32,512]{2,1,0:T(8,128)(2,1)S(1)}, u32[]{:S(2)}, u32[]{:S(2)}) async-start(bf16[32,32,512]{2,1,0:T(8,128)(2,1)} %bitcast.34), calls=%async_computation.6 | async-start | bytes 2097152 | tf_op jit(solution)/shard_map/all_to_all | solution.py:433
  161.7 4.2 %collective-permute-start.5 = (bf16[512,512]{1,0:T(8,128)(2,1)}, bf16[512,512]{1,0:T(8,128)(2,1)S(1)}, u32[]{:S(2)}, u32[]{:S(2)}) collective-permute-start(bf16[512,512]{1,0:T(8,128)(2,1)} %get-tuple-element.24), channel_id=1, source_target_pairs={{0,1},{1,0},{2,3},{3,2},{4,5},{5,4},{6,7},{7,6},{8,9},{9,8},{10,11... | collective-permute-start | bytes 1572872 | tf_op jit(solution)/shard_map/ppermute | solution.py:21
  165.9 0.1 collective-permute-start.6
  166.0 7.5 %key_gradients.1 = (bf16[512,2048]{1,0:T(8,128)(2,1)}, bf16[512,512]{1,0:T(8,128)(2,1)}, bf16[512,2048]{1,0:T(8,128)(2,1)}, bf16[512,512]{1,0:T(8,128)(2,1)}) custom-call(s32[5]{0:T(128)} %stack.16.info, bf16[512,2048]{1,0:T(8,128)(2,1)} %bitcast.25, bf16[512,1024]{1,0:T(8,128)(2,1)} %copy-done.2, ...), custom_call_target="tpu_custom_call", output_to_operand_aliasing={{0}: (8, {}), {2}: (9, {})} | custom-call | flops 2147483648 | bytes 8388608 | tf_op jit(solution)/shard_map/key_gradients/pallas_call | solution.py:333
  173.5 0.4 collective-permute-start.3
  173.9 0.1 collective-permute-start.4
  174.1 0.2 reduce_sum.24
  174.3 1.6 collective-permute-done.3.refs_0_
  175.8 0.7 collective-permute-done.4.refs_1_
  176.6 3.1 %complete_keys.1 = (bf16[512,2048]{1,0:T(8,128)(2,1)}, bf16[512,2048]{1,0:T(8,128)(2,1)}) custom-call(s32[5]{0:T(128)} %stack.16.info, bf16[512,512]{1,0:T(8,128)(2,1)} %collective-permute-done.3.refs_0_, bf16[512,512]{1,0:T(8,128)(2,1)} %collective-permute-done.4.refs_1_, bf16[512,512]{1,0:T(8,128)(2,1)} %copy-done.3, ...), custom_call_target="tpu_custom_call", output_to_operand_aliasing={{0}: (5, {}), {1}: (6, {})} | custom-call | bytes 8388608 | tf_op jit(solution)/shard_map/complete_keys/pallas_call | solution.py:377
  179.7 2.7 %all-to-all-done.6 = bf16[32,32,512]{2,1,0:T(8,128)(2,1)S(1)} async-done(((bf16[32,32,512]{2,1,0:T(8,128)(2,1)}), bf16[32,32,512]{2,1,0:T(8,128)(2,1)S(1)}, u32[]{:S(2)}, u32[]{:S(2)}) %all-to-all-start.6) | async-done | bytes 1048608 | tf_op jit(solution)/shard_map/all_to_all | solution.py:433
  182.4 0.2 reduce_sum.25
  182.6 9.0 %collective-permute-start.7 = (bf16[16,1024]{1,0:T(8,128)(2,1)S(1)}, bf16[16,1024]{1,0:T(8,128)(2,1)S(1)}, u32[]{:S(2)}, u32[]{:S(2)}) collective-permute-start(bf16[16,1024]{1,0:T(8,128)(2,1)S(1)} %get-tuple-element.36), channel_id=1, source_target_pairs={{0,1},{1,0},{2,3},{3,2},{4,5},{5,4},{6,7},{7,6},{8,9},{9,8},{10,11... | collective-permute-start | bytes 98312 | tf_op jit(solution)/shard_map/ppermute | solution.py:21
  191.6 0.9 collective-permute-done.7
  192.4 0.6 maximum_select_fusion
  (13 shorter events, 0.1 us)
Async XLA Ops:
  7.2 59.1 %all-gather.4.cloned.1.call-start = ((), (), s32[]{:S(2)}) async-start(), calls=%async_computation.7 | async-start | bytes 2359296 | tf_op jit(solution)/shard_map/all_gather | solution.py:30
  46.2 28.1 %all-to-all-start.1 = ((bf16[4,8,2,2,16,512]{5,4,3,2,1,0:T(8,128)(2,1)}), bf16[4,8,2,2,16,512]{5,4,3,2,1,0:T(8,128)(2,1)}, u32[]{:S(2)}, u32[]{:S(2)}) async-start(bf16[4,8,2,2,16,512]{5,4,3,2,1,0:T(8,128)(2,1)} %broadcast_in_dim.11), calls=%async_computation.1 | async-start | bytes 4194304 | tf_op jit(solution)/shard_map/all_to_all | solution.py:35
  50.7 9.1 %copy-start = (bf16[1,512,2048]{2,1,0:T(8,128)(2,1)S(1)}, bf16[1,512,2048]{2,1,0:T(8,128)(2,1)}, u32[]{:S(2)}) copy-start(bf16[1,512,2048]{2,1,0:T(8,128)(2,1)} %param.7) | copy-start | bytes 6291460
  53.1 13.1 %collective-permute-start.2 = (bf16[512,1024]{1,0:T(8,128)(2,1)}, bf16[512,1024]{1,0:T(8,128)(2,1)S(1)}, u32[]{:S(2)}, u32[]{:S(2)}) collective-permute-start(bf16[512,1024]{1,0:T(8,128)(2,1)} %dynamic-slice_bitcast_fusion), channel_id=1, source_target_pairs={{0,1},{1,0},{2,3},{3,2},{4,5},{5,4},{6,7},{7,6},{8,9},{9,8},{10,11... | collective-permute-start | bytes 3145736 | tf_op jit(solution)/shard_map/ppermute | solution.py:21
  60.9 5.4 %collective-permute-start.1 = (bf16[512,1024]{1,0:T(8,128)(2,1)}, bf16[512,1024]{1,0:T(8,128)(2,1)S(1)}, u32[]{:S(2)}, u32[]{:S(2)}) collective-permute-start(bf16[512,1024]{1,0:T(8,128)(2,1)} %dynamic-slice_bitcast_fusion.1), channel_id=1, source_target_pairs={{0,1},{1,0},{2,3},{3,2},{4,5},{5,4},{6,7},{7,6},{8,9},{9,8},{10,11... | collective-permute-start | bytes 3145736 | tf_op jit(solution)/shard_map/ppermute | solution.py:21
  62.2 1.5 collective-permute-start
  66.2 1.0 copy-start.1
  66.2 1.4 copy-start.2
  124.5 28.1 %all-to-all-start.5 = ((bf16[32,32,512]{2,1,0:T(8,128)(2,1)}), bf16[32,32,512]{2,1,0:T(8,128)(2,1)S(1)}, u32[]{:S(2)}, u32[]{:S(2)}) async-start(bf16[32,32,512]{2,1,0:T(8,128)(2,1)} %bitcast.33), calls=%async_computation.5 | async-start | bytes 2097152 | tf_op jit(solution)/shard_map/all_to_all | solution.py:433
  152.6 29.8 %all-to-all-start.6 = ((bf16[32,32,512]{2,1,0:T(8,128)(2,1)}), bf16[32,32,512]{2,1,0:T(8,128)(2,1)S(1)}, u32[]{:S(2)}, u32[]{:S(2)}) async-start(bf16[32,32,512]{2,1,0:T(8,128)(2,1)} %bitcast.34), calls=%async_computation.6 | async-start | bytes 2097152 | tf_op jit(solution)/shard_map/all_to_all | solution.py:433
  161.7 12.6 %collective-permute-start.5 = (bf16[512,512]{1,0:T(8,128)(2,1)}, bf16[512,512]{1,0:T(8,128)(2,1)S(1)}, u32[]{:S(2)}, u32[]{:S(2)}) collective-permute-start(bf16[512,512]{1,0:T(8,128)(2,1)} %get-tuple-element.24), channel_id=1, source_target_pairs={{0,1},{1,0},{2,3},{3,2},{4,5},{5,4},{6,7},{7,6},{8,9},{9,8},{10,11... | collective-permute-start | bytes 1572872 | tf_op jit(solution)/shard_map/ppermute | solution.py:21
  165.9 8.3 %collective-permute-start.6 = (bf16[512,512]{1,0:T(8,128)(2,1)}, bf16[512,512]{1,0:T(8,128)(2,1)S(1)}, u32[]{:S(2)}, u32[]{:S(2)}) collective-permute-start(bf16[512,512]{1,0:T(8,128)(2,1)} %get-tuple-element.25), channel_id=1, source_target_pairs={{0,1},{1,0},{2,3},{3,2},{4,5},{5,4},{6,7},{7,6},{8,9},{9,8},{10,11... | collective-permute-start | bytes 1572872 | tf_op jit(solution)/shard_map/ppermute | solution.py:21
  173.5 2.3 %collective-permute-start.3 = (bf16[512,512]{1,0:T(8,128)(2,1)}, bf16[512,512]{1,0:T(8,128)(2,1)}, u32[]{:S(2)}, u32[]{:S(2)}) collective-permute-start(bf16[512,512]{1,0:T(8,128)(2,1)} %get-tuple-element.22), channel_id=1, source_target_pairs={{0,1},{1,0},{2,3},{3,2},{4,5},{5,4},{6,7},{7,6},{8,9},{9,8},{10,11... | collective-permute-start | bytes 1572872 | tf_op jit(solution)/shard_map/ppermute | solution.py:21
  173.9 2.6 %collective-permute-start.4 = (bf16[512,512]{1,0:T(8,128)(2,1)}, bf16[512,512]{1,0:T(8,128)(2,1)}, u32[]{:S(2)}, u32[]{:S(2)}) collective-permute-start(bf16[512,512]{1,0:T(8,128)(2,1)} %get-tuple-element.23), channel_id=1, source_target_pairs={{0,1},{1,0},{2,3},{3,2},{4,5},{5,4},{6,7},{7,6},{8,9},{9,8},{10,11... | collective-permute-start | bytes 1572872 | tf_op jit(solution)/shard_map/ppermute | solution.py:21
  174.2 2.3 %copy-start.3 = (bf16[512,512]{1,0:T(8,128)(2,1)}, bf16[512,512]{1,0:T(8,128)(2,1)S(1)}, u32[]{:S(2)}) copy-start(bf16[512,512]{1,0:T(8,128)(2,1)S(1)} %collective-permute-done.5.refs_2_) | copy-start | bytes 1572868
  174.3 2.3 %copy-start.4 = (bf16[512,512]{1,0:T(8,128)(2,1)}, bf16[512,512]{1,0:T(8,128)(2,1)S(1)}, u32[]{:S(2)}) copy-start(bf16[512,512]{1,0:T(8,128)(2,1)S(1)} %collective-permute-done.6.refs_3_) | copy-start | bytes 1572868
  182.6 9.8 %collective-permute-start.7 = (bf16[16,1024]{1,0:T(8,128)(2,1)S(1)}, bf16[16,1024]{1,0:T(8,128)(2,1)S(1)}, u32[]{:S(2)}, u32[]{:S(2)}) collective-permute-start(bf16[16,1024]{1,0:T(8,128)(2,1)S(1)} %get-tuple-element.36), channel_id=1, source_target_pairs={{0,1},{1,0},{2,3},{3,2},{4,5},{5,4},{6,7},{7,6},{8,9},{9,8},{10,11... | collective-permute-start | bytes 98312 | tf_op jit(solution)/shard_map/ppermute | solution.py:21
Sparse Core Ops, SparseCore 0:
  20.3 45.6 all-gather.3
